TPU v7x, 512 devices: a whole 4x8x8 slice. The times are simulated.
512 devices in a mesh: dp: 8 (over y), ctx: 64 (over z, x, core).
Axes of the slice: x: 4, y: 8, z: 8, core: 2. Of those that a mesh axis runs over, the one named last changes fastest.
Arguments:
- q_stream: bfloat16 [8192, 4096], P('ctx', 'dp'), may hold values from -6 to 6
- k_stream: bfloat16 [8192, 4096], P('ctx', 'dp'), may hold values from -6 to 6
- v_stream: bfloat16 [8192, 4096], P('ctx', 'dp'), may hold values from -6 to 6
- filter_taps: float32 [128, 4096], P('dp'), may hold values from -0.6 to 0.6
- short_taps: float32 [9, 4096], P(None, 'dp'), may hold values from -3 to 3
- cotangent: bfloat16 [8192, 4096], P('ctx', 'dp'), may hold values from -6 to 6
Outputs:
- mixed: bfloat16 [8192, 4096], P('ctx', 'dp')
- grad_q: bfloat16 [8192, 4096], P('ctx', 'dp')
- grad_k: bfloat16 [8192, 4096], P('ctx', 'dp')
- grad_v: bfloat16 [8192, 4096], P('ctx', 'dp')
- grad_filter: float32 [128, 4096], P('dp')
- grad_short: float32 [9, 4096], P(None, 'dp')
All inputs are finite; a program needn't handle non-finite values.
Results may differ from a plain program's by a relative error of at most 0.00175.
Values may be sent and summed in bfloat16 or wider, within the bound.
No kernel may reach another device: no remote copies, remote signals or barrier semaphores. Data moves between devices by JAX's collectives and lax.ppermute only.
A program may use at most 64 MiB of HBM per device.

v0:
```python
import math

import jax
import jax.numpy as jnp
from jax import lax
from jax.sharding import PartitionSpec as P


def as_sent(value):
    return jax.tree.map(lambda a: a.astype(jnp.bfloat16) if a.dtype == jnp.float32 else a, value)


def shifted(value, axis, by):
    peers = lax.axis_size(axis)
    pairs = [(i, i + by) for i in range(peers) if 0 <= i + by < peers]
    return lax.ppermute(value, axis, pairs)


def apply_taps(extended, taps, row_count, reverse):
    tap_count = taps.shape[0]
    group_width = 32 if tap_count % 32 == 0 else tap_count

    def apply_group(group_index, running):
        for offset in range(group_width):
            tap_index = group_index * group_width + offset
            start = tap_index if reverse else tap_count - 1 - tap_index
            window = lax.dynamic_slice_in_dim(extended, start, row_count, 0)
            tap_weight = lax.dynamic_index_in_dim(taps, tap_index, 0, keepdims=False)
            running = running + tap_weight * window
        return running

    running = jnp.zeros((row_count, extended.shape[1]), jnp.float32)
    return lax.fori_loop(0, tap_count // group_width, apply_group, running)


def lag_sums(grads, extended, tap_count):
    row_count = grads.shape[0]
    group_width = 32 if tap_count % 32 == 0 else tap_count

    def lag_group(group_index):
        column_sums = []
        for offset in range(group_width):
            tap_index = group_index * group_width + offset
            window = lax.dynamic_slice_in_dim(extended, tap_count - 1 - tap_index, row_count, 0)
            column_sums.append(jnp.sum(grads * window, axis=0))
        return jnp.stack(column_sums)

    blocks = lax.map(lag_group, jnp.arange(tap_count // group_width, dtype=jnp.int32))
    return blocks.reshape(tap_count, grads.shape[1])


def collect_rows(bulk_rows, edge_rows, needed, before, shifter):
    row_count = bulk_rows[0].shape[0]
    hop_total = -(-needed // row_count)
    direction = 1 if before else -1
    pieces = []
    arrived = ()
    current = bulk_rows
    for hop_index in range(1, hop_total + 1):
        outgoing = current + edge_rows if hop_index == 1 else current
        incoming = shifter(outgoing, direction)
        if hop_index == 1:
            arrived = incoming[len(bulk_rows) :]
        current = incoming[: len(bulk_rows)]
        pieces.append(current)
    joined = []
    for member_index in range(len(bulk_rows)):
        ordered = [segment[member_index] for segment in (pieces[::-1] if before else pieces)]
        stacked = jnp.concatenate(ordered, 0)
        joined.append(stacked[stacked.shape[0] - needed :] if before else stacked[:needed])
    return (tuple(joined), tuple(arrived))


def on_device(q_stream, k_stream, v_stream, filter_taps, short_taps, cotangent):
    row_count = q_stream.shape[0]
    filters = lax.all_to_all(filter_taps, "dp", split_axis=1, concat_axis=0, tiled=True)
    tap_count = filters.shape[0]
    needed = tap_count + 1
    short_query = short_taps[0:3]
    short_key = short_taps[3:6]
    short_value = short_taps[6:9]

    def causal_shift(payload, distance):
        return jax.tree.map(
            lambda part, own: part.astype(own.dtype),
            shifted(as_sent(payload), "ctx", distance),
            payload,
        )

    before_rows, before_edge = collect_rows(
        (k_stream, v_stream), (q_stream[row_count - 2 :],), needed, True, causal_shift
    )
    key_ext = jnp.concatenate([before_rows[0], k_stream], 0).astype(jnp.float32)
    value_ext = jnp.concatenate([before_rows[1], v_stream], 0).astype(jnp.float32)
    query_ext = jnp.concatenate([before_edge[0], q_stream], 0).astype(jnp.float32)
    query_act = apply_taps(query_ext, short_query, row_count, False)
    key_act_ext = apply_taps(key_ext, short_key, tap_count - 1 + row_count, False)
    value_act_ext = apply_taps(value_ext, short_value, tap_count - 1 + row_count, False)
    product_ext = key_act_ext * value_act_ext
    long_part = apply_taps(product_ext, filters, row_count, False)
    mixed = (query_act * long_part).astype(jnp.bfloat16)
    upstream_float = cotangent.astype(jnp.float32)
    long_grad = upstream_float * query_act
    query_err = upstream_float * long_part
    key_act = key_act_ext[tap_count - 1 :]
    value_act = value_act_ext[tap_count - 1 :]

    def product_shift(payload, distance):
        return shifted(payload, "ctx", distance)

    after_rows, after_edge = collect_rows(
        (long_grad,), (key_act[:2], value_act[:2], query_err[:2]), needed, False, product_shift
    )
    long_grad_after = after_rows[0]
    key_next, value_next, query_err_next = after_edge
    long_grad_full = jnp.concatenate([long_grad, long_grad_after], 0)
    product_grad = apply_taps(long_grad_full, filters, row_count + 2, True)
    key_err = product_grad * jnp.concatenate([value_act, value_next], 0)
    value_err = product_grad * jnp.concatenate([key_act, key_next], 0)
    query_err_full = jnp.concatenate([query_err, query_err_next], 0)
    grad_q = apply_taps(query_err_full, short_query, row_count, True).astype(jnp.bfloat16)
    grad_k = apply_taps(key_err, short_key, row_count, True).astype(jnp.bfloat16)
    grad_v = apply_taps(value_err, short_value, row_count, True).astype(jnp.bfloat16)
    filter_part = lag_sums(long_grad, product_ext, tap_count)
    short_part = jnp.concatenate(
        [
            lag_sums(query_err, query_ext, 3),
            lag_sums(key_err[:row_count], key_ext[tap_count - 1 :], 3),
            lag_sums(value_err[:row_count], value_ext[tap_count - 1 :], 3),
        ],
        0,
    )
    filter_total, short_total = lax.psum((filter_part, short_part), "ctx")
    filter_owned = lax.all_to_all(filter_total, "dp", split_axis=0, concat_axis=1, tiled=True)
    norm_factor = 1.0 / math.sqrt(row_count * lax.axis_size("ctx"))
    grad_filter = filter_owned * norm_factor
    grad_short = short_total * norm_factor
    return (mixed, grad_q, grad_k, grad_v, grad_filter, grad_short)


def solution(mesh):
    in_specs = (
        P("ctx", "dp"),
        P("ctx", "dp"),
        P("ctx", "dp"),
        P("dp", None),
        P(None, "dp"),
        P("ctx", "dp"),
    )
    out_specs = (
        P("ctx", "dp"),
        P("ctx", "dp"),
        P("ctx", "dp"),
        P("ctx", "dp"),
        P("dp", None),
        P(None, "dp"),
    )
    return jax.shard_map(
        on_device, mesh=mesh, in_specs=in_specs, out_specs=out_specs, check_vma=False
    )
```

profile of v0, /device:TPU:1, one launch (start us, length us, event | category | flops | bytes accessed | tf_op | source)
XLA Modules:
  0.0 549.7 jit_solution(15849531009379644230)
XLA Ops:
  7.2 4.5 collective-permute-start.3
  11.7 0.7 slice.86
  12.4 1.9 collective-permute-start
  14.3 3.5 collective-permute-start.1
  17.8 1.7 copy.20
  19.5 7.0 %all-to-all-start = ((f32[16,8,512]{2,0,1:T(8,128)}), f32[16,8,512]{2,0,1:T(8,128)S(1)}, u32[]{:S(2)}, u32[]{:S(2)}) async-start(f32[16,8,512]{2,0,1:T(8,128)} %bitcast.191), calls=%async_computation | async-start | bytes 524288 | tf_op jit(solution)/shard_map/all_to_all | solution.py:76
  26.5 2.2 collective-permute-start.4
  28.8 3.1 collective-permute-start.2
  32.0 1.8 collective-permute-done.2
  34.3 0.7 slice.98
  35.0 1.9 collective-permute-start.9
  36.9 1.9 collective-permute-start.8
  38.8 11.3 %while.33 = (s32[]{:T(128)}, f32[128,512]{1,0:T(8,128)S(1)}, f32[128,512]{1,0:T(8,128)S(1)}, f32[255,512]{1,0:T(8,128)S(1)}, s32[]{:T(128)}, /*index=5*/s32[]{:T...) while((s32[]{:T(128)}, f32[128,512]{1,0:T(8,128)S(1)}, ...), condition=%wide.region_1.2_spmd.clone, body=%wide.region_0.1_spmd.clone.sunk | while | flops 4260099 | bytes 9113311 | solution.py:33
  39.4 2.3 multiply_add_fusion.6
  42.2 2.3 multiply_add_fusion.6
  45.0 2.3 multiply_add_fusion.6
  47.9 2.3 multiply_add_fusion.6
  50.2 1.8 multiply_reduce_fusion.32
  51.9 1.9 collective-permute-start.6
  53.9 23.3 %while.32 = (s32[]{:T(128)}, f32[4,32,512]{2,1,0:T(8,128)}, s32[4]{0:T(128)S(1)}, f32[255,512]{1,0:T(8,128)S(1)}, f32[128,512]{1,0:T(8,128)}, /*index=5*/s32[]{:...) while((s32[]{:T(128)}, f32[4,32,512]{2,1,0:T(8,128)}, ...), condition=%wide.region_37.38_spmd, body=%wide.region_4.37_spmd.sunk | while | flops 4178082 | bytes 9242933 | solution.py:48
  55.3 1.7 multiply_reduce_fusion.37
  57.0 1.9 multiply_reduce_fusion.38
  61.1 1.7 multiply_reduce_fusion.37
  62.8 1.9 multiply_reduce_fusion.38
  64.9 0.6 bitcast_dynamic-update-slice_fusion.2
  67.0 1.7 multiply_reduce_fusion.37
  68.7 1.9 multiply_reduce_fusion.38
  70.7 0.6 bitcast_dynamic-update-slice_fusion.2
  72.8 1.7 multiply_reduce_fusion.37
  74.5 1.9 multiply_reduce_fusion.38
  76.6 0.6 bitcast_dynamic-update-slice_fusion.2
  77.2 1.9 collective-permute-start.5
  79.1 1.9 collective-permute-start.7
  81.1 0.7 multiply_convert_fusion
  81.8 1.1 collective-permute-done.5
  82.8 0.7 fusion.61
  83.6 195.4 %all-reduce.2.cloned.1.call-done = f32[8,16,512]{2,1,0:T(8,128)} async-done(((f32[8,16,512]{2,1,0:T(8,128)}), f32[8,16,512]{2,1,0:T(8,128)}) %all-reduce.2.cloned.1.call-update) | async-done | bytes 262160 | tf_op jit(solution)/shard_map/psum | solution.py:133
  279.0 6.5 %all-to-all-start.1 = ((f32[8,16,512]{2,1,0:T(8,128)}), f32[8,16,512]{2,1,0:T(8,128)S(1)}, u32[]{:S(2)}, u32[]{:S(2)}) async-start(f32[8,16,512]{2,1,0:T(8,128)} %all-reduce.2.cloned.1.call-done), calls=%async_computation.1 | async-start | bytes 524288 | tf_op jit(solution)/shard_map/all_to_all | solution.py:134
  285.5 1.1 fusion.48
  286.6 11.5 %while.34 = (s32[]{:T(128)}, f32[130,512]{1,0:T(8,128)S(1)}, f32[128,512]{1,0:T(8,128)S(1)}, f32[257,512]{1,0:T(8,128)S(1)}, s32[]{:T(128)}, /*index=5*/s32[]{:T...) while((s32[]{:T(128)}, f32[130,512]{1,0:T(8,128)S(1)}, ...), condition=%wide.region_3.4_spmd.clone, body=%wide.region_2.3_spmd.clone.sunk | while | flops 4326595 | bytes 9252143 | solution.py:33
  287.0 2.4 multiply_add_fusion.7
  289.9 2.4 multiply_add_fusion.7
  292.8 2.4 multiply_add_fusion.7
  295.7 2.4 multiply_add_fusion.7
  298.2 0.8 fusion.65
  299.0 0.8 fusion.62
  299.9 241.6 %psum.15 = f32[9,512]{1,0:T(8,128)S(1)} all-reduce(f32[9,512]{1,0:T(8,128)S(1)} %concatenate.44), channel_id=1, replica_groups=mesh['dp'=8,'ctx'=64] {'ctx'}, use_global_device_ids=true, to_apply=%region_48.49 | all-reduce | flops 4608 | bytes 36864 | tf_op jit(solution)/shard_map/psum | solution.py:133
  542.2 0.7 copy.18
  (64 shorter events, 6.4 us)
Async XLA Ops:
  7.2 19.3 %collective-permute-start.3 = (bf16[128,512]{1,0:T(8,128)(2,1)}, bf16[128,512]{1,0:T(8,128)(2,1)S(1)}, u32[]{:S(2)}, u32[]{:S(2)}) collective-permute-start(bf16[128,512]{1,0:T(8,128)(2,1)} %param.14), channel_id=1, source_target_pairs={{0,1},{1,2},{2,3},{3,4},{4,5},{5,6},{6,7},{7,8},{8,9},{9,10},{10,1... | collective-permute-start | bytes 393224 | tf_op jit(solution)/shard_map/ppermute | solution.py:16
  12.4 19.5 %collective-permute-start = (bf16[2,512]{1,0:T(2,128)(2,1)S(1)}, bf16[2,512]{1,0:T(2,128)(2,1)S(1)}, u32[]{:S(2)}, u32[]{:S(2)}) collective-permute-start(bf16[2,512]{1,0:T(2,128)(2,1)S(1)} %slice.86), channel_id=1, source_target_pairs={{0,1},{1,2},{2,3},{3,4},{4,5},{5,6},{6,7},{7,8},{8,9},{9,10},{10,1... | collective-permute-start | bytes 6152 | tf_op jit(solution)/shard_map/ppermute | solution.py:16
  14.3 14.5 %collective-permute-start.1 = (bf16[128,512]{1,0:T(8,128)(2,1)}, bf16[128,512]{1,0:T(8,128)(2,1)S(1)}, u32[]{:S(2)}, u32[]{:S(2)}) collective-permute-start(bf16[128,512]{1,0:T(8,128)(2,1)} %param.13), channel_id=1, source_target_pairs={{0,1},{1,2},{2,3},{3,4},{4,5},{5,6},{6,7},{7,8},{8,9},{9,10},{10,1... | collective-permute-start | bytes 393224 | tf_op jit(solution)/shard_map/ppermute | solution.py:16
  19.5 9.2 %copy-start.4 = (f32[9,512]{1,0:T(8,128)S(1)}, f32[9,512]{1,0:T(8,128)}, u32[]{:S(2)}) copy-start(f32[9,512]{1,0:T(8,128)} %param.16) | copy-start | bytes 55300
  19.5 12.4 %copy-start.1 = (bf16[128,512]{1,0:T(8,128)(2,1)S(1)}, bf16[128,512]{1,0:T(8,128)(2,1)}, u32[]{:S(2)}) copy-start(bf16[128,512]{1,0:T(8,128)(2,1)} %param.12) | copy-start | bytes 393220
  19.5 19.3 %all-to-all-start = ((f32[16,8,512]{2,0,1:T(8,128)}), f32[16,8,512]{2,0,1:T(8,128)S(1)}, u32[]{:S(2)}, u32[]{:S(2)}) async-start(f32[16,8,512]{2,0,1:T(8,128)} %bitcast.191), calls=%async_computation | async-start | bytes 524288 | tf_op jit(solution)/shard_map/all_to_all | solution.py:76
  26.4 252.6 %all-reduce.2.cloned.1.call-start = ((), (), s32[]{:S(2)}) async-start(), calls=%async_computation.2 | async-start | bytes 524288 | tf_op jit(solution)/shard_map/psum | solution.py:133
  26.5 5.4 collective-permute-start.4
  28.8 3.2 copy-start.2
  28.8 5.0 collective-permute-start.2
  31.9 1.9 copy-start.3
  35.0 263.1 %collective-permute-start.9 = (f32[2,512]{1,0:T(2,128)S(1)}, f32[2,512]{1,0:T(2,128)S(1)}, u32[]{:S(2)}, u32[]{:S(2)}) collective-permute-start(f32[2,512]{1,0:T(2,128)S(1)} %slice.99), channel_id=1, source_target_pairs={{1,0},{2,1},{3,2},{4,3},{5,4},{6,5},{7,6},{8,7},{9,8},{10,9},{11,1... | collective-permute-start | bytes 12296 | tf_op jit(solution)/shard_map/ppermute | solution.py:16
  36.9 261.2 %collective-permute-start.8 = (f32[2,512]{1,0:T(2,128)S(1)}, f32[2,512]{1,0:T(2,128)S(1)}, u32[]{:S(2)}, u32[]{:S(2)}) collective-permute-start(f32[2,512]{1,0:T(2,128)S(1)} %slice.97), channel_id=1, source_target_pairs={{1,0},{2,1},{3,2},{4,3},{5,4},{6,5},{7,6},{8,7},{9,8},{10,9},{11,1... | collective-permute-start | bytes 12296 | tf_op jit(solution)/shard_map/ppermute | solution.py:16
  51.9 27.2 %collective-permute-start.6 = (f32[128,512]{1,0:T(8,128)}, f32[128,512]{1,0:T(8,128)}, u32[]{:S(2)}, u32[]{:S(2)}) collective-permute-start(f32[128,512]{1,0:T(8,128)} %get-tuple-element.1639), channel_id=1, source_target_pairs={{1,0},{2,1},{3,2},{4,3},{5,4},{6,5},{7,6},{8,7},{9,8},{10,9},{11,1... | collective-permute-start | bytes 786440 | tf_op jit(solution)/shard_map/ppermute | solution.py:16
  77.2 5.6 %collective-permute-start.5 = (f32[2,512]{1,0:T(2,128)S(1)}, f32[2,512]{1,0:T(2,128)S(1)}, u32[]{:S(2)}, u32[]{:S(2)}) collective-permute-start(f32[2,512]{1,0:T(2,128)S(1)} %slice.95), channel_id=1, source_target_pairs={{1,0},{2,1},{3,2},{4,3},{5,4},{6,5},{7,6},{8,7},{9,8},{10,9},{11,1... | collective-permute-start | bytes 12296 | tf_op jit(solution)/shard_map/ppermute | solution.py:16
  79.1 206.3 %collective-permute-start.7 = (f32[128,512]{1,0:T(8,128)}, f32[128,512]{1,0:T(8,128)S(1)}, u32[]{:S(2)}, u32[]{:S(2)}) collective-permute-start(f32[128,512]{1,0:T(8,128)} %collective-permute-done.6), channel_id=1, source_target_pairs={{1,0},{2,1},{3,2},{4,3},{5,4},{6,5},{7,6},{8,7},{9,8},{10,9},{11,1... | collective-permute-start | bytes 786440 | tf_op jit(solution)/shard_map/ppermute | solution.py:16
  279.0 263.1 %all-to-all-start.1 = ((f32[8,16,512]{2,1,0:T(8,128)}), f32[8,16,512]{2,1,0:T(8,128)S(1)}, u32[]{:S(2)}, u32[]{:S(2)}) async-start(f32[8,16,512]{2,1,0:T(8,128)} %all-reduce.2.cloned.1.call-done), calls=%async_computation.1 | async-start | bytes 524288 | tf_op jit(solution)/shard_map/all_to_all | solution.py:134
  286.5 11.6 %copy-start = (f32[128,512]{1,0:T(8,128)S(1)}, f32[128,512]{1,0:T(8,128)}, u32[]{:S(2)}) copy-start(f32[128,512]{1,0:T(8,128)} %slice.98) | copy-start | bytes 786436
Sparse Core Ops, SparseCore 0:
  81.9 197.0 all-reduce.1
where the time goes:
time: 555 us; the launch traced here: 550 us
  blocking collectives  242 us (44%)
  waiting for transfers between devices  198 us (36%)
  other arithmetic  40.4 us (7%)
  starting transfers between devices  38.2 us (7%)
  between operations  14.4 us (3%)
  local copies, waits for them, and re-layouts  10.8 us (2%)
  loops' own time  6.12 us (1%)
    psum x1, blocking collectives, on_device(): filter_total, short_total = lax.psum((filter_part, short_part), 'ctx')  242 us
    psum x1, waiting for transfers between devices, on_device(): filter_total, short_total = lax.psum((filter_part, short_part), 'ctx')  195 us
    ppermute x10, starting transfers between devices, shifted(): return lax.ppermute(value, axis, pairs)  24.8 us
    add x8, other arithmetic, apply_group(): running = running + tap_weight * window  18.8 us
    reduce_sum x11, other arithmetic, lag_group(): column_sums.append(jnp.sum(grads * window, axis=0))  17.8 us
  transfers between devices with their start and end apart: 13, of which 3 were waited for; matrix products, arithmetic and copies ran while one was open for 9% of the time, Pallas kernels for 0%

commit v1 on v0

v1 whole, which is shorter than its diff:
```python
import functools
import math

import jax
import jax.numpy as jnp
import ml_dtypes
import numpy as np
from jax import lax
from jax.experimental import pallas as pl
from jax.experimental.pallas import tpu as pltpu
from jax.sharding import PartitionSpec as P

BF16 = jnp.bfloat16
F32 = jnp.float32

ROWS = 128
PERIOD = 256
HALF = PERIOD // 2
OUT = 136
WIDE = 256
EDGE = 16
TILE = 128
CHUNK = 24
VMEM_LIMIT = 48 * 1024 * 1024


def two_parts(matrix):
    high = matrix.astype(ml_dtypes.bfloat16)
    low = (matrix - high.astype(np.float64)).astype(ml_dtypes.bfloat16)
    return np.stack([high, low])


def transform_matrices():
    freqs = np.arange(HALF) + 0.5

    def angles(places):
        return 2.0 * np.pi * np.outer(freqs, places) / PERIOD

    forward = angles(np.arange(PERIOD))
    forward = np.concatenate([np.cos(forward), -np.sin(forward)], 0)

    def inverse(places):
        turned = angles(places).T
        return np.concatenate([np.cos(turned), -np.sin(turned)], 1) * (2.0 / PERIOD)

    long_back = inverse(np.arange(HALF, HALF + OUT))
    grad_back = inverse(np.arange(OUT))
    filter_back = inverse(HALF - np.arange(ROWS))
    return tuple(two_parts(m) for m in (forward, long_back, grad_back, filter_back))


def split(value):
    high = value.astype(BF16)
    low = (value - high.astype(F32)).astype(BF16)
    return high, low


def dot3(matrix_high, matrix_low, value):
    high, low = split(value)
    dot = functools.partial(jnp.dot, preferred_element_type=F32)
    return dot(matrix_high, high) + (dot(matrix_high, low) + dot(matrix_low, high))


def as_chunk(tile, row_value):
    first = tile.astype(BF16).astype(F32)
    row_first = row_value.astype(BF16).astype(F32)
    row = lax.broadcasted_iota(jnp.int32, (8, TILE), 0)
    last = jnp.where(row == 0, row_first, jnp.where(row == 1, row_value - row_first, 0.0))
    return jnp.concatenate([first, tile - first, last], 0).astype(BF16)


def layer_kernel(
    q_ref, k_ref, v_ref, c_ref,
    k_prev, v_prev, q_next, c_next,
    q_tail, kv_tail, kv_head, qc_head,
    h_ref, s_ref,
    fwd_ref, long_ref, grad_ref, filt_ref,
    mixed_ref, gq_ref, gk_ref, gv_ref, part_ref,
    q_ext, k_ext, v_ext, e_ext,
):
    def f32(x):
        return x.astype(F32)

    q_ext[0:8] = f32(q_tail[...])[8:16]
    q_ext[8:136] = f32(q_ref[...])
    q_ext[136:264] = f32(q_next[...])
    q_ext[264:272] = f32(qc_head[0:EDGE])[0:8]
    for ext, own, prev, n in ((k_ext, k_ref, k_prev, 0), (v_ext, v_ref, v_prev, 1)):
        ext[0:8] = f32(kv_tail[EDGE * n : EDGE * (n + 1)])[8:16]
        ext[8:136] = f32(prev[...])
        ext[136:264] = f32(own[...])
        ext[264:272] = f32(kv_head[EDGE * n : EDGE * (n + 1)])[0:8]

    def tap(s, j):
        return s_ref[3 * s + j : 3 * s + j + 1, :]

    def causal(ext, s):
        return (
            tap(s, 0) * ext[8:272] + tap(s, 1) * ext[7:271] + tap(s, 2) * ext[6:270]
        )

    a0 = causal(q_ext, 0)
    a1 = causal(k_ext, 1)
    a2 = causal(v_ext, 2)
    product = a1 * a2
    cot = f32(c_ref[...])
    cot_next = f32(c_next[...])
    cot_far = f32(qc_head[EDGE : 2 * EDGE])[0:8]
    lg_own = cot * a0[0:128]
    lg_next = cot_next * a0[128:256]
    lg_far = cot_far * a0[256:264]

    taps = h_ref[...]
    fh, fl = fwd_ref[0], fwd_ref[1]
    x_f = dot3(fh, fl, product[0:256])
    own_f = dot3(fh[:, 0:128], fl[:, 0:128], lg_own)
    lg_f = own_f + dot3(fh[:, 128:256], fl[:, 128:256], lg_next)
    h_f = dot3(fh[:, 0:128], fl[:, 0:128], taps)

    def times(a, b):
        ar, ai, br, bi = a[0:128], a[128:256], b[0:128], b[128:256]
        return jnp.concatenate([ar * br - ai * bi, ar * bi + ai * br], 0)

    def times_conj(a, b):
        ar, ai, br, bi = a[0:128], a[128:256], b[0:128], b[128:256]
        return jnp.concatenate([ar * br + ai * bi, ai * br - ar * bi], 0)

    long = dot3(long_ref[0], long_ref[1], times(x_f, h_f))
    pg = dot3(grad_ref[0], grad_ref[1], times_conj(lg_f, h_f))
    filt = dot3(filt_ref[0], filt_ref[1], times_conj(x_f, own_f))

    h0, h1, h127 = taps[0:1], taps[1:2], taps[127:128]
    p_first = product[0:8]
    p_last = product[256:264]
    row = lax.broadcasted_iota(jnp.int32, (8, long.shape[1]), 0)
    sum0 = p_last[0:1] + p_first[0:1]
    sum1 = p_last[1:2] + p_first[1:2]
    fix_long = jnp.where(row == 0, h0 * sum0, jnp.where(row == 1, h0 * sum1 + h1 * sum0, 0.0))
    fix_grad = jnp.where(row == 1, h127 * (lg_far[0:1] + lg_own[0:1]), 0.0)
    long_own, long_far = long[0:128], long[128:136] + fix_long
    pg_own, pg_far = pg[0:128], pg[128:136] + fix_grad

    mixed_ref[...] = (a0[0:128] * long_own).astype(BF16)

    short = []

    def finish(s, err_own, err_far, ext, base, out_ref):
        e_ext[0:128] = err_own
        e_ext[128:136] = err_far
        total = tap(s, 0) * err_own + tap(s, 1) * e_ext[1:129] + tap(s, 2) * e_ext[2:130]
        out_ref[...] = total.astype(BF16)
        for j in range(3):
            short.append(
                jnp.sum(err_own * ext[base - j : base - j + 128], axis=0, keepdims=True)
            )

    finish(0, cot * long_own, cot_next[0:8] * long_far, q_ext, 8, gq_ref)
    finish(1, pg_own * a2[128:256], pg_far * a2[256:264], k_ext, 136, gk_ref)
    finish(2, pg_own * a1[128:256], pg_far * a1[256:264], v_ext, 136, gv_ref)

    for h in range(WIDE // TILE):
        cols = slice(h * TILE, (h + 1) * TILE)
        for g in range(16):
            row_value = short[g][:, cols] if g < 9 else jnp.zeros((1, TILE), F32)
            part_ref[h, g] = as_chunk(filt[8 * g : 8 * g + 8, cols], row_value)


def run_layer(args, taps, shorts, matrices):
    channels = args[0].shape[1]
    steps = channels // WIDE

    def rows(count):
        return pl.BlockSpec((count, WIDE), lambda i: (0, i))

    def whole(matrix):
        return pl.BlockSpec(matrix.shape, lambda i: (0, 0, 0))

    sizes = [ROWS] * 8 + [EDGE, 2 * EDGE, 2 * EDGE, 2 * EDGE] + [ROWS, 9]
    out_rows = jax.ShapeDtypeStruct((ROWS, channels), BF16)
    ext = pltpu.VMEM((272, WIDE), F32)
    return pl.pallas_call(
        layer_kernel,
        grid=(steps,),
        in_specs=[rows(n) for n in sizes] + [whole(m) for m in matrices],
        out_specs=[rows(ROWS)] * 4
        + [pl.BlockSpec((WIDE // TILE, 16, CHUNK, TILE), lambda i: (i, 0, 0, 0))],
        out_shape=[out_rows] * 4
        + [jax.ShapeDtypeStruct((channels // TILE, 16, CHUNK, TILE), BF16)],
        scratch_shapes=[ext, ext, ext, pltpu.VMEM((OUT, WIDE), F32)],
        compiler_params=pltpu.CompilerParams(vmem_limit_bytes=VMEM_LIMIT),
        name="layer",
    )(*args, taps, shorts, *matrices)


def sum_kernel(part_ref, tile_ref, short_ref):
    total = jnp.sum(part_ref[...].astype(F32), axis=0)
    tile_ref[...] = total[0:8] + total[8:16]
    short_ref[...] = jnp.broadcast_to(total[16:17] + total[17:18], (8, TILE))


def spread_kernel(tile_ref, short_ref, out_ref):
    chunk = as_chunk(tile_ref[...], short_ref[0:1])
    out_ref[...] = jnp.broadcast_to(chunk[None], out_ref.shape)


def final_kernel(scale, groups, gathered_ref, filter_ref, short_ref):
    for h in range(4):
        for d in range(groups):
            for half in range(2):
                chunk = gathered_ref[h * 16 + d * 2 + half].astype(F32)
                start = (d * 4 + h) * TILE
                filter_ref[8 * half : 8 * half + 8, start : start + TILE] = (
                    chunk[0:8] + chunk[8:16]
                ) * scale
        for g in range(9):
            chunk = gathered_ref[h * 16 + g].astype(F32)
            short_ref[g : g + 1, h * TILE : (h + 1) * TILE] = (
                chunk[16:17] + chunk[17:18]
            ) * scale


def on_device(q_stream, k_stream, v_stream, filter_taps, short_taps, cotangent, *, matrices):
    groups, peers = lax.axis_size("dp"), lax.axis_size("ctx")

    def shifted(value, by):
        pairs = [(i, i + by) for i in range(peers) if 0 <= i + by < peers]
        return lax.ppermute(value, "ctx", pairs)

    k_prev = shifted(k_stream, 1)
    v_prev = shifted(v_stream, 1)
    q_next = shifted(q_stream, -1)
    c_next = shifted(cotangent, -1)
    q_tail = shifted(q_stream[ROWS - EDGE :], 1)
    kv_tail = shifted(jnp.concatenate([k_stream[ROWS - EDGE :], v_stream[ROWS - EDGE :]], 0), 2)
    kv_head = shifted(jnp.concatenate([k_stream[:EDGE], v_stream[:EDGE]], 0), -1)
    qc_head = shifted(jnp.concatenate([q_stream[:EDGE], cotangent[:EDGE]], 0), -2)
    taps = lax.all_to_all(filter_taps, "dp", split_axis=1, concat_axis=0, tiled=True)

    mixed, grad_q, grad_k, grad_v, part = run_layer(
        (
            q_stream, k_stream, v_stream, cotangent,
            k_prev, v_prev, q_next, c_next,
            q_tail, kv_tail, kv_head, qc_head,
        ),
        taps,
        short_taps,
        matrices,
    )

    part = part.reshape(peers, CHUNK, TILE)
    part = lax.all_to_all(part, "ctx", split_axis=0, concat_axis=0, tiled=True)
    tile, short = pl.pallas_call(
        sum_kernel,
        out_shape=[
            jax.ShapeDtypeStruct((8, TILE), F32),
            jax.ShapeDtypeStruct((8, TILE), F32),
        ],
        name="sum",
    )(part)

    pairs = [
        (d * peers + h * 16 + e * 2 + half, e * peers + h * 16 + d * 2 + half)
        for d in range(groups)
        for h in range(4)
        for e in range(groups)
        for half in range(2)
    ]
    tile = lax.ppermute(tile, ("dp", "ctx"), pairs)
    sent = pl.pallas_call(
        spread_kernel,
        out_shape=jax.ShapeDtypeStruct((peers, CHUNK, TILE), BF16),
        name="spread",
    )(tile, short)
    gathered = lax.all_to_all(sent, "ctx", split_axis=0, concat_axis=0, tiled=True)
    scale = 1.0 / math.sqrt(ROWS * peers)
    grad_filter, grad_short = pl.pallas_call(
        functools.partial(final_kernel, scale, groups),
        out_shape=[
            jax.ShapeDtypeStruct(filter_taps.shape, F32),
            jax.ShapeDtypeStruct(short_taps.shape, F32),
        ],
        name="final",
    )(gathered)
    return (mixed, grad_q, grad_k, grad_v, grad_filter, grad_short)


def solution(mesh):
    streams = P("ctx", "dp")
    in_specs = (streams, streams, streams, P("dp", None), P(None, "dp"), streams)
    out_specs = (streams,) * 4 + (P("dp", None), P(None, "dp"))
    matrices = transform_matrices()
    return jax.shard_map(
        functools.partial(on_device, matrices=matrices),
        mesh=mesh,
        in_specs=in_specs,
        out_specs=out_specs,
        check_vma=False,
    )
```

time: 555 us -> 113 us (0.20)
  waiting for transfers between devices: 198 us -> 8.32 us
  blocking collectives: 242 us -> 62.2 us
  other arithmetic: 40.4 us -> 0.01 us
  between operations: 14.4 us -> 0.9 us
  starting transfers between devices: 38.2 us -> 28.5 us
  Pallas kernels: 0 us -> 8.86 us
  local copies, waits for them, and re-layouts: 10.8 us -> 3.12 us
  loops' own time: 6.12 us -> 0 us
    psum x1 -> x0, blocking collectives: 242 us -> none  [on_device(): filter_total, short_total = lax.psum((filter_part, short_part), 'ctx')]
    psum x1 -> x0, waiting for transfers between devices: 195 us -> none  [on_device(): filter_total, short_total = lax.psum((filter_part, short_part), 'ctx')]
    all_to_all x0 -> x2, blocking collectives: none -> 62.2 us  [the longest x1 32.1 us: on_device(): part = lax.all_to_all(part, 'ctx', split_axis=0, concat_axis=0, tiled=True)]
    add x8 -> x0, other arithmetic: 18.8 us -> none  [apply_group(): running = running + tap_weight * window]
    reduce_sum x11 -> x0, other arithmetic: 17.8 us -> none  [lag_group(): column_sums.append(jnp.sum(grads * window, axis=0))]
    pallas_call x0 -> x4, Pallas kernels: none -> 8.86 us  [the longest x1 3.96 us: run_layer(): pl.pallas_call(layer_kernel, grid=(steps,), in_specs=[rows(n) for n in si...]
    all_to_all x1 -> x0, starting transfers between devices: 6.46 us -> none  [on_device(): lax.all_to_all(filter_total, 'dp', split_axis=0, concat_axis=1, tiled=True)]
    another operation x3 -> x0, loops' own time: 6.12 us -> none  [the longest x1 3.45 us: lag_sums(): lax.map(lag_group, jnp.arange(tap_count // group_width, dtype=jnp.int32))]
  transfers between devices with their start and end apart: 13 -> 10, of which waited for: 3 -> 2; matrix products, arithmetic and copies ran while one was open for 9% -> 2% of each run, Pallas kernels for 0% -> 0%
where the time goes in v1:
time: 113 us; the launch traced here: 112 us
  blocking collectives  62.2 us (55%)
  starting transfers between devices  28.5 us (25%)
  Pallas kernels  8.86 us (8%)
  waiting for transfers between devices  8.32 us (7%)
  local copies, waits for them, and re-layouts  3.12 us (3%)
    all_to_all x1, blocking collectives, on_device(): part = lax.all_to_all(part, 'ctx', split_axis=0, concat_axis=0, tiled=True)  32.1 us
    all_to_all x1, blocking collectives, on_device(): lax.all_to_all(sent, 'ctx', split_axis=0, concat_axis=0, tiled=True)  30.1 us
    ppermute x8, starting transfers between devices, shifted(): return lax.ppermute(value, 'ctx', pairs)  22.9 us
    ppermute x8, waiting for transfers between devices, shifted(): return lax.ppermute(value, 'ctx', pairs)  8.31 us
    all_to_all x1, starting transfers between devices, on_device(): lax.all_to_all(filter_taps, 'dp', split_axis=1, concat_axis=0, tiled=True)  4.3 us
    pallas_call x1, Pallas kernels, run_layer(): pl.pallas_call(layer_kernel, grid=(steps,), in_specs=[rows(n) for n in si...  3.96 us
  transfers between devices with their start and end apart: 10, of which 2 were waited for; matrix products, arithmetic and copies ran while one was open for 2% of the time, Pallas kernels for 0%

profile of v1, /device:TPU:1, one launch (start us, length us, event | category | flops | bytes accessed | tf_op | source)
XLA Modules:
  0.0 111.9 jit_solution(13011095248451926410)
XLA Ops:
  0.6 8.8 %collective-permute-start.2 = (bf16[128,512]{1,0:T(8,128)(2,1)}, bf16[128,512]{1,0:T(8,128)(2,1)S(1)}, u32[]{:S(2)}, u32[]{:S(2)}) collective-permute-start(bf16[128,512]{1,0:T(8,128)(2,1)} %q_ref.1), channel_id=1, source_target_pairs={{1,0},{2,1},{3,2},{4,3},{5,4},{6,5},{7,6},{8,7},{9,8},{10,9},{11,1... | collective-permute-start | bytes 393224 | tf_op jit(solution)/shard_map/ppermute | solution.py:227
  9.4 0.7 fusion
  10.2 1.9 %collective-permute-start.4 = (bf16[16,512]{1,0:T(8,128)(2,1)S(1)}, bf16[16,512]{1,0:T(8,128)(2,1)S(1)}, u32[]{:S(2)}, u32[]{:S(2)}) collective-permute-start(bf16[16,512]{1,0:T(8,128)(2,1)S(1)} %get-tuple-element.25), channel_id=1, source_target_pairs={{0,1},{1,2},{2,3},{3,4},{4,5},{5,6},{6,7},{7,8},{8,9},{9,10},{10,1... | collective-permute-start | bytes 49160 | tf_op jit(solution)/shard_map/ppermute | solution.py:227
  12.1 1.9 %collective-permute-start = (bf16[128,512]{1,0:T(8,128)(2,1)}, bf16[128,512]{1,0:T(8,128)(2,1)S(1)}, u32[]{:S(2)}, u32[]{:S(2)}) collective-permute-start(bf16[128,512]{1,0:T(8,128)(2,1)} %k_ref.1), channel_id=1, source_target_pairs={{0,1},{1,2},{2,3},{3,4},{4,5},{5,6},{6,7},{7,8},{8,9},{9,10},{10,1... | collective-permute-start | bytes 393224 | tf_op jit(solution)/shard_map/ppermute | solution.py:227
  14.0 1.9 %collective-permute-start.1 = (bf16[128,512]{1,0:T(8,128)(2,1)}, bf16[128,512]{1,0:T(8,128)(2,1)S(1)}, u32[]{:S(2)}, u32[]{:S(2)}) collective-permute-start(bf16[128,512]{1,0:T(8,128)(2,1)} %v_ref.1), channel_id=1, source_target_pairs={{0,1},{1,2},{2,3},{3,4},{4,5},{5,6},{6,7},{7,8},{8,9},{9,10},{10,1... | collective-permute-start | bytes 393224 | tf_op jit(solution)/shard_map/ppermute | solution.py:227
  15.9 0.0 copy-start.5
  16.0 0.0 copy-start.6
  16.0 0.0 copy-start.7
  16.0 1.7 %copy.19 = f32[2,8,8,512]{3,2,0,1:T(8,128)} copy(f32[2,8,8,512]{3,2,1,0:T(8,128)} %bitcast.10) | data formatting | bytes 524288 | tf_op jit(solution)/shard_map/all_to_all | solution.py:237
  17.7 0.0 copy-start.2
  17.7 0.0 copy-start.3
  17.7 0.0 copy-start.4
  17.7 0.0 copy-start.1
  17.7 4.3 %all-to-all-start = ((f32[16,8,512]{2,0,1:T(8,128)}), f32[16,8,512]{2,0,1:T(8,128)S(1)}, u32[]{:S(2)}, u32[]{:S(2)}) async-start(f32[16,8,512]{2,0,1:T(8,128)} %bitcast.7), calls=%async_computation | async-start | bytes 524288 | tf_op jit(solution)/shard_map/all_to_all | solution.py:237
  22.0 0.0 copy-done.2
  22.0 0.0 copy-start
  22.1 0.0 copy-done.3
  22.1 3.2 %collective-permute-start.5 = (bf16[32,512]{1,0:T(8,128)(2,1)S(1)}, bf16[32,512]{1,0:T(8,128)(2,1)S(1)}, u32[]{:S(2)}, u32[]{:S(2)}) collective-permute-start(bf16[32,512]{1,0:T(8,128)(2,1)S(1)} %pad_maximum_fusion), channel_id=1, source_target_pairs={{0,2},{1,3},{2,4},{3,5},{4,6},{5,7},{6,8},{7,9},{8,10},{9,11},{10,... | collective-permute-start | bytes 98312 | tf_op jit(solution)/shard_map/ppermute | solution.py:227
  25.3 0.0 copy-done.4
  25.3 0.0 collective-permute-done.4.q_tail
  25.3 1.9 %collective-permute-start.3 = (bf16[128,512]{1,0:T(8,128)(2,1)S(1)}, bf16[128,512]{1,0:T(8,128)(2,1)S(1)}, u32[]{:S(2)}, u32[]{:S(2)}) collective-permute-start(bf16[128,512]{1,0:T(8,128)(2,1)S(1)} %copy-done.4), channel_id=1, source_target_pairs={{1,0},{2,1},{3,2},{4,3},{5,4},{6,5},{7,6},{8,7},{9,8},{10,9},{11,1... | collective-permute-start | bytes 393224 | tf_op jit(solution)/shard_map/ppermute | solution.py:227
  27.3 0.0 collective-permute-done.5.kv_tail
  27.3 1.9 %collective-permute-start.6 = (bf16[32,512]{1,0:T(8,128)(2,1)S(1)}, bf16[32,512]{1,0:T(8,128)(2,1)S(1)}, u32[]{:S(2)}, u32[]{:S(2)}) collective-permute-start(bf16[32,512]{1,0:T(8,128)(2,1)S(1)} %pad_maximum_fusion.1), channel_id=1, source_target_pairs={{1,0},{2,1},{3,2},{4,3},{5,4},{6,5},{7,6},{8,7},{9,8},{10,9},{11,1... | collective-permute-start | bytes 98312 | tf_op jit(solution)/shard_map/ppermute | solution.py:227
  29.2 0.0 copy-start.8
  29.2 3.6 %collective-permute-done.6.kv_head = bf16[32,512]{1,0:T(8,128)(2,1)S(1)} collective-permute-done((bf16[32,512]{1,0:T(8,128)(2,1)S(1)}, bf16[32,512]{1,0:T(8,128)(2,1)S(1)}, u32[]{:S(2)}, u32[]{:S(2)}) %collective-permute-start.6) | collective-permute-done | bytes 32800 | tf_op jit(solution)/shard_map/ppermute | solution.py:227
  32.8 1.3 %collective-permute-start.7 = (bf16[32,512]{1,0:T(8,128)(2,1)S(1)}, bf16[32,512]{1,0:T(8,128)(2,1)S(1)}, u32[]{:S(2)}, u32[]{:S(2)}) collective-permute-start(bf16[32,512]{1,0:T(8,128)(2,1)S(1)} %pad_maximum_fusion.2), channel_id=1, source_target_pairs={{2,0},{3,1},{4,2},{5,3},{6,4},{7,5},{8,6},{9,7},{10,8},{11,9},{12,... | collective-permute-start | bytes 98312 | tf_op jit(solution)/shard_map/ppermute | solution.py:227
  34.1 4.7 %collective-permute-done.7.qc_head = bf16[32,512]{1,0:T(8,128)(2,1)S(1)} collective-permute-done((bf16[32,512]{1,0:T(8,128)(2,1)S(1)}, bf16[32,512]{1,0:T(8,128)(2,1)S(1)}, u32[]{:S(2)}, u32[]{:S(2)}) %collective-permute-start.7) | collective-permute-done | bytes 32800 | tf_op jit(solution)/shard_map/ppermute | solution.py:227
  38.8 0.0 collective-permute-done.2.q_next
  38.8 0.0 collective-permute-done.k_prev
  38.8 0.0 collective-permute-done.1.v_prev
  38.8 0.0 collective-permute-done.3.c_next
  38.8 0.0 all-to-all-done
  38.9 0.0 copy-done.5
  38.9 0.0 copy-done.6
  38.9 0.0 copy-done.7
  38.9 0.0 copy-done.1
  38.9 0.0 copy-done
  38.9 0.0 copy-done.8
  38.9 4.0 %layer.1 = (bf16[128,512]{1,0:T(8,128)(2,1)}, bf16[128,512]{1,0:T(8,128)(2,1)}, bf16[128,512]{1,0:T(8,128)(2,1)}, bf16[128,512]{1,0:T(8,128)(2,1)}, bf16[4,16,24,128]{3,2,1,0:T(8,128)(2,1)S(1)}) custom-call(bf16[128,512]{1,0:T(8,128)(2,1)S(1)} %copy-done.1, bf16[128,512]{1,0:T(8,128)(2,1)S(1)} %copy-done.2, bf16[128,512]{1,0:T(8,128)(2,1)S(1)} %copy-done.3, ...), custom_call_target="tpu_custom_call" | custom-call | tf_op jit(solution)/shard_map/layer/pallas_call | solution.py:181
  42.9 32.1 %all_to_all.29.part_ref = bf16[64,24,128]{2,1,0:T(8,128)(2,1)} all-to-all(bf16[64,24,128]{2,1,0:T(8,128)(2,1)S(1)} %bitcast.9), channel_id=1, replica_groups=mesh['dp'=8,'ctx'=64] {'ctx'}, dimensions={0} | all-to-all | bytes 786432 | tf_op jit(solution)/shard_map/all_to_all | solution.py:251
  75.0 1.7 %sum.1 = (f32[8,128]{1,0:T(8,128)}, f32[8,128]{1,0:T(8,128)}) custom-call(bf16[64,24,128]{2,1,0:T(8,128)(2,1)} %all_to_all.29.part_ref), custom_call_target="tpu_custom_call" | custom-call | tf_op jit(solution)/shard_map/sum/pallas_call | solution.py:252
  76.7 1.3 %collective-permute-start.8 = (f32[8,128]{1,0:T(8,128)}, f32[8,128]{1,0:T(8,128)S(1)}, u32[]{:S(2)}, u32[]{:S(2)}) collective-permute-start(f32[8,128]{1,0:T(8,128)} %get-tuple-element.20), channel_id=1, source_target_pairs={{0,0},{1,1},{2,64},{3,65},{4,128},{5,129},{6,192},{7,193},{8,256},... | collective-permute-start | bytes 12296 | tf_op jit(solution)/shard_map/ppermute | solution.py:268
  78.0 0.0 collective-permute-done.8.tile_ref
  78.0 0.0 copy-start.9
  78.0 0.6 copy-done.9
  78.6 1.5 %spread.1 = bf16[64,24,128]{2,1,0:T(8,128)(2,1)} custom-call(f32[8,128]{1,0:T(8,128)} %copy-done.9, f32[8,128]{1,0:T(8,128)} %get-tuple-element.21.short_ref), custom_call_target="tpu_custom_call" | custom-call | tf_op jit(solution)/shard_map/spread/pallas_call | solution.py:269
  80.1 30.1 %all_to_all.30.gathered_ref = bf16[64,24,128]{2,1,0:T(8,128)(2,1)} all-to-all(bf16[64,24,128]{2,1,0:T(8,128)(2,1)} %spread.1), channel_id=1, replica_groups=mesh['dp'=8,'ctx'=64] {'ctx'}, dimensions={0} | all-to-all | bytes 786432 | tf_op jit(solution)/shard_map/all_to_all | solution.py:274
  110.2 1.8 %final.1 = (f32[16,4096]{1,0:T(8,128)}, f32[9,512]{1,0:T(8,128)}) custom-call(bf16[64,24,128]{2,1,0:T(8,128)(2,1)} %all_to_all.30.gathered_ref), custom_call_target="tpu_custom_call" | custom-call | tf_op jit(solution)/shard_map/final/pallas_call | solution.py:276
  (6 shorter events, 0.0 us)
Async XLA Ops:
  0.6 38.2 %collective-permute-start.2 = (bf16[128,512]{1,0:T(8,128)(2,1)}, bf16[128,512]{1,0:T(8,128)(2,1)S(1)}, u32[]{:S(2)}, u32[]{:S(2)}) collective-permute-start(bf16[128,512]{1,0:T(8,128)(2,1)} %q_ref.1), channel_id=1, source_target_pairs={{1,0},{2,1},{3,2},{4,3},{5,4},{6,5},{7,6},{8,7},{9,8},{10,9},{11,1... | collective-permute-start | bytes 393224 | tf_op jit(solution)/shard_map/ppermute | solution.py:227
  10.2 15.2 %collective-permute-start.4 = (bf16[16,512]{1,0:T(8,128)(2,1)S(1)}, bf16[16,512]{1,0:T(8,128)(2,1)S(1)}, u32[]{:S(2)}, u32[]{:S(2)}) collective-permute-start(bf16[16,512]{1,0:T(8,128)(2,1)S(1)} %get-tuple-element.25), channel_id=1, source_target_pairs={{0,1},{1,2},{2,3},{3,4},{4,5},{5,6},{6,7},{7,8},{8,9},{9,10},{10,1... | collective-permute-start | bytes 49160 | tf_op jit(solution)/shard_map/ppermute | solution.py:227
  12.1 26.7 %collective-permute-start = (bf16[128,512]{1,0:T(8,128)(2,1)}, bf16[128,512]{1,0:T(8,128)(2,1)S(1)}, u32[]{:S(2)}, u32[]{:S(2)}) collective-permute-start(bf16[128,512]{1,0:T(8,128)(2,1)} %k_ref.1), channel_id=1, source_target_pairs={{0,1},{1,2},{2,3},{3,4},{4,5},{5,6},{6,7},{7,8},{8,9},{9,10},{10,1... | collective-permute-start | bytes 393224 | tf_op jit(solution)/shard_map/ppermute | solution.py:227
  14.0 24.8 %collective-permute-start.1 = (bf16[128,512]{1,0:T(8,128)(2,1)}, bf16[128,512]{1,0:T(8,128)(2,1)S(1)}, u32[]{:S(2)}, u32[]{:S(2)}) collective-permute-start(bf16[128,512]{1,0:T(8,128)(2,1)} %v_ref.1), channel_id=1, source_target_pairs={{0,1},{1,2},{2,3},{3,4},{4,5},{5,6},{6,7},{7,8},{8,9},{9,10},{10,1... | collective-permute-start | bytes 393224 | tf_op jit(solution)/shard_map/ppermute | solution.py:227
  15.9 22.9 %copy-start.5 = (bf16[2,136,256]{2,1,0:T(8,128)(2,1)S(1)}, bf16[2,136,256]{2,1,0:T(8,128)(2,1)}, u32[]{:S(2)}) copy-start(bf16[2,136,256]{2,1,0:T(8,128)(2,1)} %constant.10.clone.grad_ref) | copy-start | bytes 417796
  16.0 22.9 %copy-start.6 = (bf16[2,136,256]{2,1,0:T(8,128)(2,1)S(1)}, bf16[2,136,256]{2,1,0:T(8,128)(2,1)}, u32[]{:S(2)}) copy-start(bf16[2,136,256]{2,1,0:T(8,128)(2,1)} %constant.9.clone.long_ref) | copy-start | bytes 417796
  16.0 22.9 %copy-start.7 = (bf16[2,128,256]{2,1,0:T(8,128)(2,1)S(1)}, bf16[2,128,256]{2,1,0:T(8,128)(2,1)}, u32[]{:S(2)}) copy-start(bf16[2,128,256]{2,1,0:T(8,128)(2,1)} %constant.11.clone.filt_ref) | copy-start | bytes 393220
  17.7 4.3 %copy-start.2 = (bf16[128,512]{1,0:T(8,128)(2,1)S(1)}, bf16[128,512]{1,0:T(8,128)(2,1)}, u32[]{:S(2)}) copy-start(bf16[128,512]{1,0:T(8,128)(2,1)} %k_ref.1) | copy-start | bytes 393220
  17.7 4.3 %copy-start.3 = (bf16[128,512]{1,0:T(8,128)(2,1)S(1)}, bf16[128,512]{1,0:T(8,128)(2,1)}, u32[]{:S(2)}) copy-start(bf16[128,512]{1,0:T(8,128)(2,1)} %v_ref.1) | copy-start | bytes 393220
  17.7 7.6 %copy-start.4 = (bf16[128,512]{1,0:T(8,128)(2,1)S(1)}, bf16[128,512]{1,0:T(8,128)(2,1)}, u32[]{:S(2)}) copy-start(bf16[128,512]{1,0:T(8,128)(2,1)} %c_ref.1) | copy-start | bytes 393220
  17.7 21.2 %copy-start.1 = (bf16[128,512]{1,0:T(8,128)(2,1)S(1)}, bf16[128,512]{1,0:T(8,128)(2,1)}, u32[]{:S(2)}) copy-start(bf16[128,512]{1,0:T(8,128)(2,1)} %q_ref.1) | copy-start | bytes 393220
  17.7 21.1 %all-to-all-start = ((f32[16,8,512]{2,0,1:T(8,128)}), f32[16,8,512]{2,0,1:T(8,128)S(1)}, u32[]{:S(2)}, u32[]{:S(2)}) async-start(f32[16,8,512]{2,0,1:T(8,128)} %bitcast.7), calls=%async_computation | async-start | bytes 524288 | tf_op jit(solution)/shard_map/all_to_all | solution.py:237
  22.0 16.9 %copy-start = (bf16[2,256,256]{2,1,0:T(8,128)(2,1)S(1)}, bf16[2,256,256]{2,1,0:T(8,128)(2,1)}, u32[]{:S(2)}) copy-start(bf16[2,256,256]{2,1,0:T(8,128)(2,1)} %constant.8.clone.fwd_ref) | copy-start | bytes 786436
  22.1 5.2 %collective-permute-start.5 = (bf16[32,512]{1,0:T(8,128)(2,1)S(1)}, bf16[32,512]{1,0:T(8,128)(2,1)S(1)}, u32[]{:S(2)}, u32[]{:S(2)}) collective-permute-start(bf16[32,512]{1,0:T(8,128)(2,1)S(1)} %pad_maximum_fusion), channel_id=1, source_target_pairs={{0,2},{1,3},{2,4},{3,5},{4,6},{5,7},{6,8},{7,9},{8,10},{9,11},{10,... | collective-permute-start | bytes 98312 | tf_op jit(solution)/shard_map/ppermute | solution.py:227
  25.3 13.5 %collective-permute-start.3 = (bf16[128,512]{1,0:T(8,128)(2,1)S(1)}, bf16[128,512]{1,0:T(8,128)(2,1)S(1)}, u32[]{:S(2)}, u32[]{:S(2)}) collective-permute-start(bf16[128,512]{1,0:T(8,128)(2,1)S(1)} %copy-done.4), channel_id=1, source_target_pairs={{1,0},{2,1},{3,2},{4,3},{5,4},{6,5},{7,6},{8,7},{9,8},{10,9},{11,1... | collective-permute-start | bytes 393224 | tf_op jit(solution)/shard_map/ppermute | solution.py:227
  27.3 5.5 %collective-permute-start.6 = (bf16[32,512]{1,0:T(8,128)(2,1)S(1)}, bf16[32,512]{1,0:T(8,128)(2,1)S(1)}, u32[]{:S(2)}, u32[]{:S(2)}) collective-permute-start(bf16[32,512]{1,0:T(8,128)(2,1)S(1)} %pad_maximum_fusion.1), channel_id=1, source_target_pairs={{1,0},{2,1},{3,2},{4,3},{5,4},{6,5},{7,6},{8,7},{9,8},{10,9},{11,1... | collective-permute-start | bytes 98312 | tf_op jit(solution)/shard_map/ppermute | solution.py:227
  29.2 9.7 %copy-start.8 = (f32[9,512]{1,0:T(8,128)S(1)}, f32[9,512]{1,0:T(8,128)}, u32[]{:S(2)}) copy-start(f32[9,512]{1,0:T(8,128)} %s_ref.1) | copy-start | bytes 55300
  32.8 6.0 %collective-permute-start.7 = (bf16[32,512]{1,0:T(8,128)(2,1)S(1)}, bf16[32,512]{1,0:T(8,128)(2,1)S(1)}, u32[]{:S(2)}, u32[]{:S(2)}) collective-permute-start(bf16[32,512]{1,0:T(8,128)(2,1)S(1)} %pad_maximum_fusion.2), channel_id=1, source_target_pairs={{2,0},{3,1},{4,2},{5,3},{6,4},{7,5},{8,6},{9,7},{10,8},{11,9},{12,... | collective-permute-start | bytes 98312 | tf_op jit(solution)/shard_map/ppermute | solution.py:227
  76.7 1.3 %collective-permute-start.8 = (f32[8,128]{1,0:T(8,128)}, f32[8,128]{1,0:T(8,128)S(1)}, u32[]{:S(2)}, u32[]{:S(2)}) collective-permute-start(f32[8,128]{1,0:T(8,128)} %get-tuple-element.20), channel_id=1, source_target_pairs={{0,0},{1,1},{2,64},{3,65},{4,128},{5,129},{6,192},{7,193},{8,256},... | collective-permute-start | bytes 12296 | tf_op jit(solution)/shard_map/ppermute | solution.py:268
  78.0 0.6 copy-start.9

commit v2 on v1

v2 whole, which is shorter than its diff:
```python
import functools
import math

import jax
import jax.numpy as jnp
import ml_dtypes
import numpy as np
from jax import lax
from jax.experimental import pallas as pl
from jax.experimental.pallas import tpu as pltpu
from jax.sharding import PartitionSpec as P

BF16 = jnp.bfloat16
F32 = jnp.float32

ROWS = 128
PERIOD = 256
HALF = PERIOD // 2
OUT = 136
WIDE = 256
EDGE = 16
TILE = 128
CHUNK = 24
VMEM_LIMIT = 48 * 1024 * 1024


def two_parts(matrix):
    high = matrix.astype(ml_dtypes.bfloat16)
    low = (matrix - high.astype(np.float64)).astype(ml_dtypes.bfloat16)
    return np.stack([high, low])


def transform_matrices():
    freqs = np.arange(HALF) + 0.5

    def angles(places):
        return 2.0 * np.pi * np.outer(freqs, places) / PERIOD

    forward = angles(np.arange(PERIOD))
    forward = np.concatenate([np.cos(forward), -np.sin(forward)], 0)

    def inverse(places):
        turned = angles(places).T
        return np.concatenate([np.cos(turned), -np.sin(turned)], 1) * (2.0 / PERIOD)

    long_back = inverse(np.arange(HALF, HALF + OUT))
    grad_back = inverse(np.arange(OUT))
    return tuple(two_parts(m) for m in (forward, long_back, grad_back))


def split(value):
    high = value.astype(BF16)
    low = (value - high.astype(F32)).astype(BF16)
    return high, low


def dot3(matrix_high, matrix_low, value):
    high, low = split(value)
    dot = functools.partial(jnp.dot, preferred_element_type=F32)
    return dot(matrix_high, high) + (dot(matrix_high, low) + dot(matrix_low, high))


def last_rows(row_value, others):
    first = row_value.astype(BF16).astype(F32)
    row = lax.broadcasted_iota(jnp.int32, (8, TILE), 0)
    return jnp.where(row == 0, first, jnp.where(row == 1, row_value - first, others))


def as_chunk(tile, last):
    first = tile.astype(BF16).astype(F32)
    return jnp.concatenate([first, tile - first, last], 0).astype(BF16)


def pack_kernel(q_ref, k_ref, v_ref, c_ref, right_ref, left_ref, sems):
    tail, head = pl.ds(ROWS - EDGE, EDGE), pl.ds(0, EDGE)
    moves = [
        (k_ref, right_ref.at[pl.ds(0, ROWS)]),
        (v_ref, right_ref.at[pl.ds(ROWS, ROWS)]),
        (q_ref.at[tail], right_ref.at[pl.ds(2 * ROWS, EDGE)]),
        (q_ref, left_ref.at[pl.ds(0, ROWS)]),
        (c_ref, left_ref.at[pl.ds(ROWS, ROWS)]),
        (k_ref.at[head], left_ref.at[pl.ds(2 * ROWS, EDGE)]),
        (v_ref.at[head], left_ref.at[pl.ds(2 * ROWS + EDGE, EDGE)]),
    ]
    copies = [pltpu.make_async_copy(a, b, sems.at[i]) for i, (a, b) in enumerate(moves)]
    for copy in copies:
        copy.start()
    for copy in copies:
        copy.wait()


def pack(q_stream, k_stream, v_stream, cotangent):
    channels = q_stream.shape[1]
    anywhere = pl.BlockSpec(memory_space=pl.ANY)
    return pl.pallas_call(
        pack_kernel,
        in_specs=[anywhere] * 4,
        out_specs=[anywhere] * 2,
        out_shape=[
            jax.ShapeDtypeStruct((2 * ROWS + EDGE, channels), BF16),
            jax.ShapeDtypeStruct((2 * ROWS + 2 * EDGE, channels), BF16),
        ],
        scratch_shapes=[pltpu.SemaphoreType.DMA((7,))],
        name="pack",
    )(q_stream, k_stream, v_stream, cotangent)


def layer_kernel(
    place_ref,
    q_ref, k_ref, v_ref, c_ref, before_ref, after_ref,
    h_ref, s_ref, fwd_ref, long_ref, grad_ref,
    mixed_ref, gq_ref, gk_ref, gv_ref, part_ref, fix_ref,
    q_ext, k_ext, v_ext, e_ext, filt_all, late_all, short_all,
):
    def f32(x):
        return x.astype(F32)

    fh, fl = fwd_ref[0], fwd_ref[1]
    fh_half, fl_half = fh[:, 0:HALF], fl[:, 0:HALF]
    freq = lax.broadcasted_iota(jnp.int32, (HALF, WIDE), 0)
    sign = jnp.where(freq % 2 == 0, 1.0, -1.0).astype(F32)
    row = lax.broadcasted_iota(jnp.int32, (8, WIDE), 0)

    def times(a, b):
        ar, ai, br, bi = a[0:HALF], a[HALF:], b[0:HALF], b[HALF:]
        return jnp.concatenate([ar * br - ai * bi, ar * bi + ai * br], 0)

    def times_conj(a, b):
        ar, ai, br, bi = a[0:HALF], a[HALF:], b[0:HALF], b[HALF:]
        return jnp.concatenate([ar * br + ai * bi, ai * br - ar * bi], 0)

    for step in range(q_ref.shape[1] // WIDE):
        cols = pl.ds(step * WIDE, WIDE)

        q_ext[0:8] = f32(before_ref[2 * ROWS : 2 * ROWS + EDGE, cols])[8:16]
        q_ext[8:136] = f32(q_ref[:, cols])
        q_ext[136:264] = f32(after_ref[0:ROWS, cols])
        for n, ext, own in ((0, k_ext, k_ref), (1, v_ext, v_ref)):
            ext[0:8] = jnp.zeros((8, WIDE), F32)
            ext[8:136] = f32(before_ref[ROWS * n : ROWS * (n + 1), cols])
            ext[136:264] = f32(own[:, cols])
            start = 2 * ROWS + EDGE * n
            ext[264:272] = f32(after_ref[start : start + EDGE, cols])[0:8]

        def tap(s, j):
            return s_ref[3 * s + j : 3 * s + j + 1, cols]

        def causal(ext, s, count):
            return (
                tap(s, 0) * ext[8 : 8 + count]
                + tap(s, 1) * ext[7 : 7 + count]
                + tap(s, 2) * ext[6 : 6 + count]
            )

        a0 = causal(q_ext, 0, 256)
        a1 = causal(k_ext, 1, 264)
        a2 = causal(v_ext, 2, 264)
        product = a1 * a2
        p_before = jnp.concatenate([jnp.where(row < 2, 0.0, product[0:8]), product[8:128]], 0)
        p_own, p_far = product[128:256], product[256:264]
        cot = f32(c_ref[:, cols])
        cot_next = f32(after_ref[ROWS : 2 * ROWS, cols])
        lg = jnp.concatenate([cot, cot_next], 0) * a0

        taps = h_ref[:, cols]
        own_f = dot3(fh_half, fl_half, p_own)
        before_f = dot3(fh_half, fl_half, p_before)
        moved_f = jnp.concatenate([own_f[HALF:] * sign, own_f[0:HALF] * -sign], 0)
        x_f = before_f + moved_f
        lg_f = dot3(fh, fl, lg)
        h_f = dot3(fh_half, fl_half, taps)

        long = dot3(long_ref[0], long_ref[1], times(x_f, h_f))
        pg = dot3(grad_ref[0], grad_ref[1], times_conj(lg_f, h_f))
        filt_all[:, cols] = dot3(grad_ref[0, 0:ROWS], grad_ref[1, 0:ROWS], times_conj(lg_f, own_f))

        h0, h1, h127 = taps[0:1], taps[1:2], taps[127:128]
        p0, p1 = p_far[0:1], p_far[1:2]
        fix_long = jnp.where(row == 0, h0 * p0, jnp.where(row == 1, h0 * p1 + h1 * p0, 0.0))
        fix_grad = jnp.where(row == 1, h127 * lg[0:1], 0.0)
        long_own, long_far = long[0:128], long[128:136] + fix_long
        pg_own, pg_far = pg[0:128], pg[128:136] + fix_grad

        mixed = a0[0:128] * long_own
        mixed_ref[:, cols] = mixed.astype(BF16)

        def finish(s, err_own, err_far, ext, base, out_ref):
            e_ext[0:128] = err_own
            e_ext[128:136] = err_far
            total = tap(s, 0) * err_own + tap(s, 1) * e_ext[1:129] + tap(s, 2) * e_ext[2:130]
            out_ref[:, cols] = total.astype(BF16)
            for j in range(3):
                short_all[3 * s + j : 3 * s + j + 1, cols] = jnp.sum(
                    err_own * ext[base - j : base - j + 128], axis=0, keepdims=True
                )
            return total

        gq = finish(0, cot * long_own, cot_next[0:8] * long_far, q_ext, 8, gq_ref)
        gk = finish(1, pg_own * a2[128:256], pg_far * a2[256:264], k_ext, 136, gk_ref)
        gv = finish(2, pg_own * a1[128:256], pg_far * a1[256:264], v_ext, 136, gv_ref)
        lacking = cot_next[0:1] * h127 * p_own[1:2]
        for j in range(3):
            short_all[j : j + 1, cols] += lacking * q_ext[136 - j : 137 - j]

        late_all[0:1, cols] = p_own[1:2]
        late_all[1:2, cols] = lg[128:129]
        fix_ref[0:1, cols] = mixed[0:1]
        fix_ref[1:2, cols] = gq[0:1]
        fix_ref[2:3, cols] = gk[127:128]
        fix_ref[3:4, cols] = gv[127:128]
        fix_ref[4:5, cols] = a0[0:1] * h127
        fix_ref[5:6, cols] = tap(0, 0) * cot[0:1] * h127
        fix_ref[6:7, cols] = tap(1, 2) * h127 * a2[257:258]
        fix_ref[7:8, cols] = tap(2, 2) * h127 * a1[257:258]

    place = place_ref[0]
    row = lax.broadcasted_iota(jnp.int32, (8, TILE), 0)
    late = []
    for n in range(2):
        rows = jnp.zeros((8, TILE), F32)
        for h in range(4):
            value = late_all[n : n + 1, h * TILE : (h + 1) * TILE]
            rows = jnp.where(row == 2 + h, value, rows)
        late.append(rows)
    for m in range(4):
        to_right = lax.rem(m + 64 - place, 4) == 1
        others = jnp.where(to_right, late[0], late[1])
        for g in range(m, 16, 4):
            for h in range(4):
                lanes = slice(h * TILE, (h + 1) * TILE)
                value = short_all[g : g + 1, lanes] if g < 9 else jnp.zeros((1, TILE), F32)
                part_ref[16 * h + g] = as_chunk(
                    filt_all[8 * g : 8 * g + 8, lanes], last_rows(value, others)
                )


def run_layer(place, streams, before, after, taps, shorts, matrices):
    channels = streams[0].shape[1]
    out_rows = jax.ShapeDtypeStruct((ROWS, channels), BF16)
    ext = pltpu.VMEM((272, WIDE), F32)
    vmem = pl.BlockSpec(memory_space=pltpu.VMEM)
    return pl.pallas_call(
        layer_kernel,
        in_specs=[pl.BlockSpec(memory_space=pltpu.SMEM)] + [vmem] * 11,
        out_specs=[vmem] * 6,
        out_shape=[out_rows] * 4
        + [
            jax.ShapeDtypeStruct((64, CHUNK, TILE), BF16),
            jax.ShapeDtypeStruct((8, channels), F32),
        ],
        scratch_shapes=[
            ext, ext, ext,
            pltpu.VMEM((OUT, WIDE), F32),
            pltpu.VMEM((ROWS, channels), F32),
            pltpu.VMEM((8, channels), F32),
            pltpu.VMEM((16, channels), F32),
        ],
        compiler_params=pltpu.CompilerParams(vmem_limit_bytes=VMEM_LIMIT),
        name="layer",
    )(place, *streams, before, after, taps, shorts, *matrices)


def sum_kernel(place_ref, part_ref, tile_ref, short_ref, late_ref):
    total = jnp.sum(part_ref[:, 0:EDGE].astype(F32), axis=0)
    tile_ref[...] = total[0:8] + total[8:16]
    total = jnp.sum(part_ref[:, EDGE:CHUNK].astype(F32), axis=0)
    short_ref[...] = jnp.broadcast_to(total[0:1] + total[1:2], (8, TILE))
    place, peers = place_ref[0], part_ref.shape[0]
    before = part_ref[jnp.maximum(place - 1, 0), EDGE:CHUNK].astype(F32)
    after = part_ref[jnp.minimum(place + 1, peers - 1), EDGE:CHUNK].astype(F32)
    late_ref[0:8] = jnp.where(place > 0, before, 0.0)
    late_ref[8:16] = jnp.where(place < peers - 1, after, 0.0)


def patch_kernel(late_ref, fix_ref, mixed_in, gq_in, gk_in, gv_in, mixed_ref, gq_ref, gk_ref, gv_ref):
    row = lax.broadcasted_iota(jnp.int32, (EDGE, TILE), 0)
    plan = (
        (0, 0, 0, mixed_in, mixed_ref),
        (1, 0, 0, gq_in, gq_ref),
        (2, 8, EDGE - 1, gk_in, gk_ref),
        (3, 8, EDGE - 1, gv_in, gv_ref),
    )
    for n, source, place, old_ref, new_ref in plan:
        for h in range(old_ref.shape[1] // TILE):
            lanes = slice(h * TILE, (h + 1) * TILE)
            late = late_ref[source + 2 + h : source + 3 + h]
            value = fix_ref[n : n + 1, lanes] + fix_ref[4 + n : 5 + n, lanes] * late
            old = old_ref[:, lanes].astype(F32)
            new_ref[:, lanes] = jnp.where(row == place, value, old).astype(BF16)


def patch(late, fix, outs):
    channels = outs[0].shape[1]

    def edge(block):
        return pl.BlockSpec((EDGE, channels), lambda i: (block, 0))

    edges = [edge(0), edge(0), edge(ROWS // EDGE - 1), edge(ROWS // EDGE - 1)]
    return pl.pallas_call(
        patch_kernel,
        grid=(1,),
        in_specs=[
            pl.BlockSpec(late.shape, lambda i: (0, 0)),
            pl.BlockSpec(fix.shape, lambda i: (0, 0)),
        ]
        + edges,
        out_specs=edges,
        out_shape=[jax.ShapeDtypeStruct(o.shape, o.dtype) for o in outs],
        input_output_aliases={2: 0, 3: 1, 4: 2, 5: 3},
        name="patch",
    )(late, fix, *outs)


def spread_kernel(tile_ref, short_ref, out_ref):
    chunk = as_chunk(tile_ref[...], last_rows(short_ref[0:1], jnp.zeros((8, TILE), F32)))
    out_ref[...] = jnp.broadcast_to(chunk[None], out_ref.shape)


def final_kernel(scale, groups, gathered_ref, filter_ref, short_ref):
    for h in range(4):
        for d in range(groups):
            for half in range(2):
                chunk = gathered_ref[h * 16 + d * 2 + half].astype(F32)
                start = (d * 4 + h) * TILE
                filter_ref[8 * half : 8 * half + 8, start : start + TILE] = (
                    chunk[0:8] + chunk[8:16]
                ) * scale
        for g in range(9):
            chunk = gathered_ref[h * 16 + g].astype(F32)
            short_ref[g : g + 1, h * TILE : (h + 1) * TILE] = (
                chunk[16:17] + chunk[17:18]
            ) * scale


def on_device(q_stream, k_stream, v_stream, filter_taps, short_taps, cotangent, *, matrices):
    groups, peers = lax.axis_size("dp"), lax.axis_size("ctx")

    def shifted(value, by):
        pairs = [(i, i + by) for i in range(peers) if 0 <= i + by < peers]
        return lax.ppermute(value, "ctx", pairs)

    right, left = pack(q_stream, k_stream, v_stream, cotangent)
    before = shifted(right, 1)
    after = shifted(left, -1)
    taps = lax.all_to_all(filter_taps, "dp", split_axis=1, concat_axis=0, tiled=True)
    place = lax.axis_index("ctx").astype(jnp.int32).reshape(1)

    *outs, part, fix = run_layer(
        place,
        (q_stream, k_stream, v_stream, cotangent),
        before,
        after,
        taps,
        short_taps,
        matrices,
    )

    part = lax.all_to_all(part, "ctx", split_axis=0, concat_axis=0, tiled=True)
    vmem = pl.BlockSpec(memory_space=pltpu.VMEM)
    tile, short, late = pl.pallas_call(
        sum_kernel,
        in_specs=[pl.BlockSpec(memory_space=pltpu.SMEM), vmem],
        out_specs=[vmem] * 3,
        out_shape=[
            jax.ShapeDtypeStruct((8, TILE), F32),
            jax.ShapeDtypeStruct((8, TILE), F32),
            jax.ShapeDtypeStruct((EDGE, TILE), F32),
        ],
        name="sum",
    )(place, part)

    pairs = [
        (d * peers + h * 16 + e * 2 + half, e * peers + h * 16 + d * 2 + half)
        for d in range(groups)
        for h in range(4)
        for e in range(groups)
        for half in range(2)
    ]
    tile = lax.ppermute(tile, ("dp", "ctx"), pairs)
    sent = pl.pallas_call(
        spread_kernel,
        out_shape=jax.ShapeDtypeStruct((peers, CHUNK, TILE), BF16),
        name="spread",
    )(tile, short)
    outs = patch(late, fix, outs)
    gathered = lax.all_to_all(sent, "ctx", split_axis=0, concat_axis=0, tiled=True)
    scale = 1.0 / math.sqrt(ROWS * peers)
    grad_filter, grad_short = pl.pallas_call(
        functools.partial(final_kernel, scale, groups),
        out_shape=[
            jax.ShapeDtypeStruct(filter_taps.shape, F32),
            jax.ShapeDtypeStruct(short_taps.shape, F32),
        ],
        name="final",
    )(gathered)
    return (*outs, grad_filter, grad_short)


def solution(mesh):
    streams = P("ctx", "dp")
    in_specs = (streams, streams, streams, P("dp", None), P(None, "dp"), streams)
    out_specs = (streams,) * 4 + (P("dp", None), P(None, "dp"))
    matrices = transform_matrices()
    return jax.shard_map(
        functools.partial(on_device, matrices=matrices),
        mesh=mesh,
        in_specs=in_specs,
        out_specs=out_specs,
        check_vma=False,
    )
```

time: 113 us -> 112 us (level)
  blocking collectives: 62.2 us -> 30.8 us
  Pallas kernels: 8.86 us -> 28.3 us
  waiting for transfers between devices: 8.32 us -> 17.4 us
  starting transfers between devices: 28.5 us -> 30.5 us
    all_to_all x1 -> x0, blocking collectives: 30.1 us -> none  [on_device(): lax.all_to_all(sent, 'ctx', split_axis=0, concat_axis=0, tiled=True)]
    pallas_call x2 -> x4, Pallas kernels: 5.62 us -> 25.1 us  [the longest x1 18.5 us: pack(): pl.pallas_call(pack_kernel, in_specs=[anywhere] * 4, out_specs=[anywhere]...]
    ppermute x8 -> x2, starting transfers between devices: 22.9 us -> 6.48 us  [shifted(): return lax.ppermute(value, 'ctx', pairs)]
    all_to_all x0 -> x1, starting transfers between devices: none -> 15 us  [on_device(): lax.all_to_all(sent, 'ctx', split_axis=0, concat_axis=0, tiled=True)]
    all_to_all x0 -> x1, waiting for transfers between devices: none -> 13.6 us  [on_device(): lax.all_to_all(sent, 'ctx', split_axis=0, concat_axis=0, tiled=True)]
    ppermute x8 -> x2, waiting for transfers between devices: 8.31 us -> 3.78 us  [shifted(): return lax.ppermute(value, 'ctx', pairs)]
    all_to_all x1, starting transfers between devices: 4.3 us -> 7.78 us  [on_device(): lax.all_to_all(filter_taps, 'dp', split_axis=1, concat_axis=0, tiled=True)]
    all_to_all x1, blocking collectives: 32.1 us -> 30.8 us  [on_device(): part = lax.all_to_all(part, 'ctx', split_axis=0, concat_axis=0, tiled=True)]
  transfers between devices with their start and end apart: 10 -> 5, of which waited for: 2 -> 2; matrix products, arithmetic and copies ran while one was open for 2% -> 0% of each run, Pallas kernels for 0% -> 18%
where the time goes in v2:
time: 112 us
  blocking collectives  30.8 us (28%)
  starting transfers between devices  30.5 us (27%)
  Pallas kernels  28.3 us (25%)
  waiting for transfers between devices  17.4 us (16%)
  local copies, waits for them, and re-layouts  3.69 us (3%)
    all_to_all x1, blocking collectives, on_device(): part = lax.all_to_all(part, 'ctx', split_axis=0, concat_axis=0, tiled=True)  30.8 us
    pallas_call x1, Pallas kernels, pack(): pl.pallas_call(pack_kernel, in_specs=[anywhere] * 4, out_specs=[anywhere]...  18.5 us
    all_to_all x1, starting transfers between devices, on_device(): lax.all_to_all(sent, 'ctx', split_axis=0, concat_axis=0, tiled=True)  15 us
    all_to_all x1, waiting for transfers between devices, on_device(): lax.all_to_all(sent, 'ctx', split_axis=0, concat_axis=0, tiled=True)  13.6 us
    all_to_all x1, starting transfers between devices, on_device(): lax.all_to_all(filter_taps, 'dp', split_axis=1, concat_axis=0, tiled=True)  7.78 us
    ppermute x2, starting transfers between devices, shifted(): return lax.ppermute(value, 'ctx', pairs)  6.48 us
    ppermute x2, waiting for transfers between devices, shifted(): return lax.ppermute(value, 'ctx', pairs)  3.78 us
    pallas_call x1, Pallas kernels, run_layer(): pl.pallas_call(layer_kernel, in_specs=[pl.BlockSpec(memory_space=pltpu.SM...  3.47 us
  transfers between devices with their start and end apart: 5, of which 2 were waited for; matrix products, arithmetic and copies ran while one was open for 0% of the time, Pallas kernels for 18%

profile of v2, /device:TPU:1, one launch (start us, length us, event | category | flops | bytes accessed | tf_op | source)
XLA Modules:
  0.0 111.5 jit_solution(8312547092705870619)
XLA Ops:
  0.6 0.0 copy-start.6
  0.6 1.7 %copy.22 = f32[2,8,8,512]{3,2,0,1:T(8,128)} copy(f32[2,8,8,512]{3,2,1,0:T(8,128)} %bitcast.9) | data formatting | bytes 524288 | tf_op jit(solution)/shard_map/all_to_all | solution.py:345
  2.4 0.0 copy-start.4
  2.4 0.0 copy-start.5
  2.4 0.0 copy-start.7
  2.4 7.8 %all-to-all-start = ((f32[16,8,512]{2,0,1:T(8,128)}), f32[16,8,512]{2,0,1:T(8,128)S(1)}, u32[]{:S(2)}, u32[]{:S(2)}) async-start(f32[16,8,512]{2,0,1:T(8,128)} %bitcast.7), calls=%async_computation | async-start | bytes 524288 | tf_op jit(solution)/shard_map/all_to_all | solution.py:345
  10.1 0.0 copy-start
  10.1 0.0 copy-start.1
  10.2 0.0 copy-start.2
  10.2 0.0 copy-start.3
  10.2 18.5 %pack.1 = (bf16[272,512]{1,0:T(8,128)(2,1)}, bf16[288,512]{1,0:T(8,128)(2,1)}) custom-call(bf16[128,512]{1,0:T(8,128)(2,1)} %q_ref.3, bf16[128,512]{1,0:T(8,128)(2,1)} %k_ref.3, bf16[128,512]{1,0:T(8,128)(2,1)} %v_ref.3, bf16[128,512]{1,0:T(8,128)(2,1)} %c_ref.3), custom_call_target="tpu_custom_call" | custom-call | tf_op jit(solution)/shard_map/pack/pallas_call | solution.py:95
  28.7 4.6 %collective-permute-start.1 = (bf16[288,512]{1,0:T(8,128)(2,1)}, bf16[288,512]{1,0:T(8,128)(2,1)S(1)}, u32[]{:S(2)}, u32[]{:S(2)}) collective-permute-start(bf16[288,512]{1,0:T(8,128)(2,1)} %get-tuple-element.24), channel_id=1, source_target_pairs={{1,0},{2,1},{3,2},{4,3},{5,4},{6,5},{7,6},{8,7},{9,8},{10,9},{11,1... | collective-permute-start | bytes 884744 | tf_op jit(solution)/shard_map/ppermute | solution.py:340
  33.3 1.9 %collective-permute-start = (bf16[272,512]{1,0:T(8,128)(2,1)}, bf16[272,512]{1,0:T(8,128)(2,1)S(1)}, u32[]{:S(2)}, u32[]{:S(2)}) collective-permute-start(bf16[272,512]{1,0:T(8,128)(2,1)} %get-tuple-element.23), channel_id=1, source_target_pairs={{0,1},{1,2},{2,3},{3,4},{4,5},{5,6},{6,7},{7,8},{8,9},{9,10},{10,1... | collective-permute-start | bytes 835592 | tf_op jit(solution)/shard_map/ppermute | solution.py:340
  35.2 3.8 %collective-permute-done.before_ref = bf16[272,512]{1,0:T(8,128)(2,1)S(1)} collective-permute-done((bf16[272,512]{1,0:T(8,128)(2,1)}, bf16[272,512]{1,0:T(8,128)(2,1)S(1)}, u32[]{:S(2)}, u32[]{:S(2)}) %collective-permute-start) | collective-permute-done | bytes 278560 | tf_op jit(solution)/shard_map/ppermute | solution.py:340
  39.0 0.0 collective-permute-done.1.after_ref
  39.0 0.0 all-to-all-done
  39.0 0.0 copy-done.6
  39.0 0.0 copy-done.4
  39.0 0.0 copy-done.5
  39.0 0.0 copy-done.7
  39.1 0.0 copy-done
  39.1 0.0 copy-done.1
  39.1 0.0 copy-done.2
  39.1 0.0 copy-done.3
  39.1 3.5 %layer.1 = (bf16[128,512]{1,0:T(8,128)(2,1)}, bf16[128,512]{1,0:T(8,128)(2,1)}, bf16[128,512]{1,0:T(8,128)(2,1)}, bf16[128,512]{1,0:T(8,128)(2,1)}, bf16[64,24,1...) custom-call(s32[1]{0:T(128)} %bitcast.place_ref, bf16[128,512]{1,0:T(8,128)(2,1)S(1)} %copy-done, ...), custom_call_target="tpu_custom_call" | custom-call | tf_op jit(solution)/shard_map/layer/pallas_call | solution.py:242
  42.6 0.0 copy-start.8
  42.6 0.6 copy-done.8
  43.2 30.8 %all_to_all.29.part_ref = bf16[64,24,128]{2,1,0:T(8,128)(2,1)} all-to-all(bf16[64,24,128]{2,1,0:T(8,128)(2,1)S(1)} %get-tuple-element.25), channel_id=1, replica_groups=mesh['dp'=8,'ctx'=64] {'ctx'}, dimensions={0} | all-to-all | bytes 786432 | tf_op jit(solution)/shard_map/all_to_all | solution.py:358
  73.9 1.7 %sum.1 = (f32[8,128]{1,0:T(8,128)}, f32[8,128]{1,0:T(8,128)}, f32[16,128]{1,0:T(8,128)}) custom-call(s32[1]{0:T(128)} %bitcast.place_ref, bf16[64,24,128]{2,1,0:T(8,128)(2,1)} %all_to_all.29.part_ref), custom_call_target="tpu_custom_call" | custom-call | tf_op jit(solution)/shard_map/sum/pallas_call | solution.py:360
  75.6 1.3 %collective-permute-start.2 = (f32[8,128]{1,0:T(8,128)}, f32[8,128]{1,0:T(8,128)S(1)}, u32[]{:S(2)}, u32[]{:S(2)}) collective-permute-start(f32[8,128]{1,0:T(8,128)} %get-tuple-element.36), channel_id=1, source_target_pairs={{0,0},{1,1},{2,64},{3,65},{4,128},{5,129},{6,192},{7,193},{8,256},... | collective-permute-start | bytes 12296 | tf_op jit(solution)/shard_map/ppermute | solution.py:379
  76.9 0.0 collective-permute-done.2.tile_ref
  76.9 0.0 copy-start.10
  76.9 0.6 copy-done.10
  77.5 1.5 %spread.1 = bf16[64,24,128]{2,1,0:T(8,128)(2,1)} custom-call(f32[8,128]{1,0:T(8,128)} %copy-done.10, f32[8,128]{1,0:T(8,128)} %get-tuple-element.37.short_ref), custom_call_target="tpu_custom_call" | custom-call | tf_op jit(solution)/shard_map/spread/pallas_call | solution.py:380
  79.0 15.0 %all-to-all-start.2 = ((bf16[64,24,128]{2,1,0:T(8,128)(2,1)}), bf16[64,24,128]{2,1,0:T(8,128)(2,1)S(1)}, u32[]{:S(2)}, u32[]{:S(2)}) async-start(bf16[64,24,128]{2,1,0:T(8,128)(2,1)} %spread.1), calls=%async_computation.2 | async-start | bytes 786432 | tf_op jit(solution)/shard_map/all_to_all | solution.py:386
  94.0 1.4 %patch.1 = (bf16[128,512]{1,0:T(8,128)(2,1)}, bf16[128,512]{1,0:T(8,128)(2,1)}, bf16[128,512]{1,0:T(8,128)(2,1)}, bf16[128,512]{1,0:T(8,128)(2,1)}) custom-call(f32[16,128]{1,0:T(8,128)} %get-tuple-element.26.late_ref, f32[8,512]{1,0:T(8,128)} %copy-done.8, ...), custom_call_target="tpu_custom_call", output_to_operand_aliasing={{0}: (2, {}), {1}: (3, {}), {2}: (4, {}), {3}: (5, {})} | custom-call | tf_op jit(solution)/shard_map/patch/pallas_call | solution.py:299
  95.4 13.6 %all-to-all-done.2.gathered_ref = bf16[64,24,128]{2,1,0:T(8,128)(2,1)S(1)} async-done(((bf16[64,24,128]{2,1,0:T(8,128)(2,1)}), bf16[64,24,128]{2,1,0:T(8,128)(2,1)S(1)}, u32[]{:S(2)}, u32[]{:S(2)}) %all-to-all-start.2) | async-done | bytes 393248 | tf_op jit(solution)/shard_map/all_to_all | solution.py:386
  109.0 0.0 copy-start.9
  109.0 0.8 copy-done.9
  109.8 1.8 %final.1 = (f32[16,4096]{1,0:T(8,128)}, f32[9,512]{1,0:T(8,128)}) custom-call(bf16[64,24,128]{2,1,0:T(8,128)(2,1)} %copy-done.9), custom_call_target="tpu_custom_call" | custom-call | tf_op jit(solution)/shard_map/final/pallas_call | solution.py:388
Async XLA Ops:
  0.6 38.4 %copy-start.6 = (bf16[2,136,256]{2,1,0:T(8,128)(2,1)S(1)}, bf16[2,136,256]{2,1,0:T(8,128)(2,1)}, u32[]{:S(2)}) copy-start(bf16[2,136,256]{2,1,0:T(8,128)(2,1)} %constant.11.clone.long_ref) | copy-start | bytes 417796
  2.4 36.7 %copy-start.4 = (bf16[2,256,256]{2,1,0:T(8,128)(2,1)S(1)}, bf16[2,256,256]{2,1,0:T(8,128)(2,1)}, u32[]{:S(2)}) copy-start(bf16[2,256,256]{2,1,0:T(8,128)(2,1)} %constant.10.clone.fwd_ref) | copy-start | bytes 786436
  2.4 36.7 %copy-start.5 = (bf16[2,136,256]{2,1,0:T(8,128)(2,1)S(1)}, bf16[2,136,256]{2,1,0:T(8,128)(2,1)}, u32[]{:S(2)}) copy-start(bf16[2,136,256]{2,1,0:T(8,128)(2,1)} %constant.12.clone.grad_ref) | copy-start | bytes 417796
  2.4 36.7 %copy-start.7 = (f32[9,512]{1,0:T(8,128)S(1)}, f32[9,512]{1,0:T(8,128)}, u32[]{:S(2)}) copy-start(f32[9,512]{1,0:T(8,128)} %s_ref.1) | copy-start | bytes 55300
  2.4 36.7 %all-to-all-start = ((f32[16,8,512]{2,0,1:T(8,128)}), f32[16,8,512]{2,0,1:T(8,128)S(1)}, u32[]{:S(2)}, u32[]{:S(2)}) async-start(f32[16,8,512]{2,0,1:T(8,128)} %bitcast.7), calls=%async_computation | async-start | bytes 524288 | tf_op jit(solution)/shard_map/all_to_all | solution.py:345
  10.1 28.9 %copy-start = (bf16[128,512]{1,0:T(8,128)(2,1)S(1)}, bf16[128,512]{1,0:T(8,128)(2,1)}, u32[]{:S(2)}) copy-start(bf16[128,512]{1,0:T(8,128)(2,1)} %q_ref.3) | copy-start | bytes 393220
  10.1 28.9 %copy-start.1 = (bf16[128,512]{1,0:T(8,128)(2,1)S(1)}, bf16[128,512]{1,0:T(8,128)(2,1)}, u32[]{:S(2)}) copy-start(bf16[128,512]{1,0:T(8,128)(2,1)} %k_ref.3) | copy-start | bytes 393220
  10.2 28.9 %copy-start.2 = (bf16[128,512]{1,0:T(8,128)(2,1)S(1)}, bf16[128,512]{1,0:T(8,128)(2,1)}, u32[]{:S(2)}) copy-start(bf16[128,512]{1,0:T(8,128)(2,1)} %v_ref.3) | copy-start | bytes 393220
  10.2 28.9 %copy-start.3 = (bf16[128,512]{1,0:T(8,128)(2,1)S(1)}, bf16[128,512]{1,0:T(8,128)(2,1)}, u32[]{:S(2)}) copy-start(bf16[128,512]{1,0:T(8,128)(2,1)} %c_ref.3) | copy-start | bytes 393220
  28.7 10.3 %collective-permute-start.1 = (bf16[288,512]{1,0:T(8,128)(2,1)}, bf16[288,512]{1,0:T(8,128)(2,1)S(1)}, u32[]{:S(2)}, u32[]{:S(2)}) collective-permute-start(bf16[288,512]{1,0:T(8,128)(2,1)} %get-tuple-element.24), channel_id=1, source_target_pairs={{1,0},{2,1},{3,2},{4,3},{5,4},{6,5},{7,6},{8,7},{9,8},{10,9},{11,1... | collective-permute-start | bytes 884744 | tf_op jit(solution)/shard_map/ppermute | solution.py:340
  33.3 5.7 %collective-permute-start = (bf16[272,512]{1,0:T(8,128)(2,1)}, bf16[272,512]{1,0:T(8,128)(2,1)S(1)}, u32[]{:S(2)}, u32[]{:S(2)}) collective-permute-start(bf16[272,512]{1,0:T(8,128)(2,1)} %get-tuple-element.23), channel_id=1, source_target_pairs={{0,1},{1,2},{2,3},{3,4},{4,5},{5,6},{6,7},{7,8},{8,9},{9,10},{10,1... | collective-permute-start | bytes 835592 | tf_op jit(solution)/shard_map/ppermute | solution.py:340
  42.6 0.6 copy-start.8
  75.6 1.3 %collective-permute-start.2 = (f32[8,128]{1,0:T(8,128)}, f32[8,128]{1,0:T(8,128)S(1)}, u32[]{:S(2)}, u32[]{:S(2)}) collective-permute-start(f32[8,128]{1,0:T(8,128)} %get-tuple-element.36), channel_id=1, source_target_pairs={{0,0},{1,1},{2,64},{3,65},{4,128},{5,129},{6,192},{7,193},{8,256},... | collective-permute-start | bytes 12296 | tf_op jit(solution)/shard_map/ppermute | solution.py:379
  76.9 0.6 copy-start.10
  79.0 30.0 %all-to-all-start.2 = ((bf16[64,24,128]{2,1,0:T(8,128)(2,1)}), bf16[64,24,128]{2,1,0:T(8,128)(2,1)S(1)}, u32[]{:S(2)}, u32[]{:S(2)}) async-start(bf16[64,24,128]{2,1,0:T(8,128)(2,1)} %spread.1), calls=%async_computation.2 | async-start | bytes 786432 | tf_op jit(solution)/shard_map/all_to_all | solution.py:386
  109.0 0.8 copy-start.9

commit v3 on v2

--- a/solution.py
+++ b/solution.py
@@ -71,36 +71,28 @@
     return jnp.concatenate([first, tile - first, last], 0).astype(BF16)
 
 
-def pack_kernel(q_ref, k_ref, v_ref, c_ref, right_ref, left_ref, sems):
+def pack_kernel(q_ref, k_ref, v_ref, c_ref, right_ref, left_ref):
     tail, head = pl.ds(ROWS - EDGE, EDGE), pl.ds(0, EDGE)
-    moves = [
-        (k_ref, right_ref.at[pl.ds(0, ROWS)]),
-        (v_ref, right_ref.at[pl.ds(ROWS, ROWS)]),
-        (q_ref.at[tail], right_ref.at[pl.ds(2 * ROWS, EDGE)]),
-        (q_ref, left_ref.at[pl.ds(0, ROWS)]),
-        (c_ref, left_ref.at[pl.ds(ROWS, ROWS)]),
-        (k_ref.at[head], left_ref.at[pl.ds(2 * ROWS, EDGE)]),
-        (v_ref.at[head], left_ref.at[pl.ds(2 * ROWS + EDGE, EDGE)]),
-    ]
-    copies = [pltpu.make_async_copy(a, b, sems.at[i]) for i, (a, b) in enumerate(moves)]
-    for copy in copies:
-        copy.start()
-    for copy in copies:
-        copy.wait()
+    right_ref[0:ROWS] = k_ref[...]
+    right_ref[ROWS : 2 * ROWS] = v_ref[...]
+    right_ref[2 * ROWS : 2 * ROWS + EDGE] = q_ref[tail]
+    left_ref[0:ROWS] = q_ref[...]
+    left_ref[ROWS : 2 * ROWS] = c_ref[...]
+    left_ref[2 * ROWS : 2 * ROWS + EDGE] = k_ref[head]
+    left_ref[2 * ROWS + EDGE : 2 * ROWS + 2 * EDGE] = v_ref[head]
 
 
 def pack(q_stream, k_stream, v_stream, cotangent):
     channels = q_stream.shape[1]
-    anywhere = pl.BlockSpec(memory_space=pl.ANY)
+    vmem = pl.BlockSpec(memory_space=pltpu.VMEM)
     return pl.pallas_call(
         pack_kernel,
-        in_specs=[anywhere] * 4,
-        out_specs=[anywhere] * 2,
+        in_specs=[vmem] * 4,
+        out_specs=[vmem] * 2,
         out_shape=[
             jax.ShapeDtypeStruct((2 * ROWS + EDGE, channels), BF16),
             jax.ShapeDtypeStruct((2 * ROWS + 2 * EDGE, channels), BF16),
         ],
-        scratch_shapes=[pltpu.SemaphoreType.DMA((7,))],
         name="pack",
     )(q_stream, k_stream, v_stream, cotangent)
 

time: 112 us -> 95.6 us (0.85)
  Pallas kernels: 28.3 us -> 11.8 us
    pallas_call x1, Pallas kernels: 18.5 us -> 1.99 us  [pack(): pl.pallas_call(pack_kernel, in_specs=[vmem] * 4, out_specs=[vmem] * 2, ou...]
  transfers between devices with their start and end apart: 5 -> 5, of which waited for: 2 -> 2; matrix products, arithmetic and copies ran while one was open for 0% -> 0% of each run, Pallas kernels for 18% -> 4%
where the time goes in v3:
time: 95.6 us; the launch traced here: 95 us
  blocking collectives  30.8 us (32%)
  starting transfers between devices  30.5 us (32%)
  waiting for transfers between devices  17.4 us (18%)
  Pallas kernels  11.8 us (12%)
  local copies, waits for them, and re-layouts  3.69 us (4%)
    all_to_all x1, blocking collectives, on_device(): part = lax.all_to_all(part, 'ctx', split_axis=0, concat_axis=0, tiled=True)  30.8 us
    all_to_all x1, starting transfers between devices, on_device(): lax.all_to_all(sent, 'ctx', split_axis=0, concat_axis=0, tiled=True)  15 us
    all_to_all x1, waiting for transfers between devices, on_device(): lax.all_to_all(sent, 'ctx', split_axis=0, concat_axis=0, tiled=True)  13.6 us
    all_to_all x1, starting transfers between devices, on_device(): lax.all_to_all(filter_taps, 'dp', split_axis=1, concat_axis=0, tiled=True)  7.78 us
    ppermute x2, starting transfers between devices, shifted(): return lax.ppermute(value, 'ctx', pairs)  6.48 us
    ppermute x2, waiting for transfers between devices, shifted(): return lax.ppermute(value, 'ctx', pairs)  3.78 us
    pallas_call x1, Pallas kernels, run_layer(): pl.pallas_call(layer_kernel, in_specs=[pl.BlockSpec(memory_space=pltpu.SM...  3.45 us
    unnamed x22, local copies, waits for them, and re-layouts  1.99 us
  transfers between devices with their start and end apart: 5, of which 2 were waited for; matrix products, arithmetic and copies ran while one was open for 0% of the time, Pallas kernels for 4%

profile of v3, /device:TPU:1, one launch (start us, length us, event | category | flops | bytes accessed | tf_op | source)
XLA Modules:
  0.0 95.0 jit_solution(17881412701460427283)
XLA Ops:
  0.6 0.0 copy-start.6
  0.6 1.7 %copy.22 = f32[2,8,8,512]{3,2,0,1:T(8,128)} copy(f32[2,8,8,512]{3,2,1,0:T(8,128)} %bitcast.9) | data formatting | bytes 524288 | tf_op jit(solution)/shard_map/all_to_all | solution.py:337
  2.4 0.0 copy-start.4
  2.4 0.0 copy-start.5
  2.4 0.0 copy-start.7
  2.4 7.8 %all-to-all-start = ((f32[16,8,512]{2,0,1:T(8,128)}), f32[16,8,512]{2,0,1:T(8,128)S(1)}, u32[]{:S(2)}, u32[]{:S(2)}) async-start(f32[16,8,512]{2,0,1:T(8,128)} %bitcast.7), calls=%async_computation | async-start | bytes 524288 | tf_op jit(solution)/shard_map/all_to_all | solution.py:337
  10.1 0.0 copy-start
  10.1 0.0 copy-start.1
  10.2 0.0 copy-start.2
  10.2 0.0 copy-start.3
  10.2 2.0 %pack.1 = (bf16[272,512]{1,0:T(8,128)(2,1)}, bf16[288,512]{1,0:T(8,128)(2,1)}) custom-call(bf16[128,512]{1,0:T(8,128)(2,1)} %q_ref.3, bf16[128,512]{1,0:T(8,128)(2,1)} %k_ref.3, bf16[128,512]{1,0:T(8,128)(2,1)} %v_ref.3, bf16[128,512]{1,0:T(8,128)(2,1)} %c_ref.3), custom_call_target="tpu_custom_call" | custom-call | tf_op jit(solution)/shard_map/pack/pallas_call | solution.py:88
  12.2 4.6 %collective-permute-start.1 = (bf16[288,512]{1,0:T(8,128)(2,1)}, bf16[288,512]{1,0:T(8,128)(2,1)S(1)}, u32[]{:S(2)}, u32[]{:S(2)}) collective-permute-start(bf16[288,512]{1,0:T(8,128)(2,1)} %get-tuple-element.24), channel_id=1, source_target_pairs={{1,0},{2,1},{3,2},{4,3},{5,4},{6,5},{7,6},{8,7},{9,8},{10,9},{11,1... | collective-permute-start | bytes 884744 | tf_op jit(solution)/shard_map/ppermute | solution.py:332
  16.7 1.9 %collective-permute-start = (bf16[272,512]{1,0:T(8,128)(2,1)}, bf16[272,512]{1,0:T(8,128)(2,1)S(1)}, u32[]{:S(2)}, u32[]{:S(2)}) collective-permute-start(bf16[272,512]{1,0:T(8,128)(2,1)} %get-tuple-element.23), channel_id=1, source_target_pairs={{0,1},{1,2},{2,3},{3,4},{4,5},{5,6},{6,7},{7,8},{8,9},{9,10},{10,1... | collective-permute-start | bytes 835592 | tf_op jit(solution)/shard_map/ppermute | solution.py:332
  18.7 3.8 %collective-permute-done.before_ref = bf16[272,512]{1,0:T(8,128)(2,1)S(1)} collective-permute-done((bf16[272,512]{1,0:T(8,128)(2,1)}, bf16[272,512]{1,0:T(8,128)(2,1)S(1)}, u32[]{:S(2)}, u32[]{:S(2)}) %collective-permute-start) | collective-permute-done | bytes 278560 | tf_op jit(solution)/shard_map/ppermute | solution.py:332
  22.4 0.0 collective-permute-done.1.after_ref
  22.4 0.0 all-to-all-done
  22.5 0.0 copy-done.6
  22.5 0.0 copy-done.4
  22.5 0.0 copy-done.5
  22.5 0.0 copy-done.7
  22.5 0.0 copy-done
  22.5 0.0 copy-done.1
  22.5 0.0 copy-done.2
  22.5 0.0 copy-done.3
  22.5 3.5 %layer.1 = (bf16[128,512]{1,0:T(8,128)(2,1)}, bf16[128,512]{1,0:T(8,128)(2,1)}, bf16[128,512]{1,0:T(8,128)(2,1)}, bf16[128,512]{1,0:T(8,128)(2,1)}, bf16[64,24,1...) custom-call(s32[1]{0:T(128)} %bitcast.place_ref, bf16[128,512]{1,0:T(8,128)(2,1)S(1)} %copy-done, ...), custom_call_target="tpu_custom_call" | custom-call | tf_op jit(solution)/shard_map/layer/pallas_call | solution.py:234
  26.0 0.0 copy-start.8
  26.0 0.6 copy-done.8
  26.6 30.8 %all_to_all.29.part_ref = bf16[64,24,128]{2,1,0:T(8,128)(2,1)} all-to-all(bf16[64,24,128]{2,1,0:T(8,128)(2,1)S(1)} %get-tuple-element.25), channel_id=1, replica_groups=mesh['dp'=8,'ctx'=64] {'ctx'}, dimensions={0} | all-to-all | bytes 786432 | tf_op jit(solution)/shard_map/all_to_all | solution.py:350
  57.4 1.7 %sum.1 = (f32[8,128]{1,0:T(8,128)}, f32[8,128]{1,0:T(8,128)}, f32[16,128]{1,0:T(8,128)}) custom-call(s32[1]{0:T(128)} %bitcast.place_ref, bf16[64,24,128]{2,1,0:T(8,128)(2,1)} %all_to_all.29.part_ref), custom_call_target="tpu_custom_call" | custom-call | tf_op jit(solution)/shard_map/sum/pallas_call | solution.py:352
  59.1 1.3 %collective-permute-start.2 = (f32[8,128]{1,0:T(8,128)}, f32[8,128]{1,0:T(8,128)S(1)}, u32[]{:S(2)}, u32[]{:S(2)}) collective-permute-start(f32[8,128]{1,0:T(8,128)} %get-tuple-element.36), channel_id=1, source_target_pairs={{0,0},{1,1},{2,64},{3,65},{4,128},{5,129},{6,192},{7,193},{8,256},... | collective-permute-start | bytes 12296 | tf_op jit(solution)/shard_map/ppermute | solution.py:371
  60.4 0.0 collective-permute-done.2.tile_ref
  60.4 0.0 copy-start.10
  60.4 0.6 copy-done.10
  61.0 1.5 %spread.1 = bf16[64,24,128]{2,1,0:T(8,128)(2,1)} custom-call(f32[8,128]{1,0:T(8,128)} %copy-done.10, f32[8,128]{1,0:T(8,128)} %get-tuple-element.37.short_ref), custom_call_target="tpu_custom_call" | custom-call | tf_op jit(solution)/shard_map/spread/pallas_call | solution.py:372
  62.4 15.0 %all-to-all-start.2 = ((bf16[64,24,128]{2,1,0:T(8,128)(2,1)}), bf16[64,24,128]{2,1,0:T(8,128)(2,1)S(1)}, u32[]{:S(2)}, u32[]{:S(2)}) async-start(bf16[64,24,128]{2,1,0:T(8,128)(2,1)} %spread.1), calls=%async_computation.2 | async-start | bytes 786432 | tf_op jit(solution)/shard_map/all_to_all | solution.py:378
  77.4 1.4 %patch.1 = (bf16[128,512]{1,0:T(8,128)(2,1)}, bf16[128,512]{1,0:T(8,128)(2,1)}, bf16[128,512]{1,0:T(8,128)(2,1)}, bf16[128,512]{1,0:T(8,128)(2,1)}) custom-call(f32[16,128]{1,0:T(8,128)} %get-tuple-element.26.late_ref, f32[8,512]{1,0:T(8,128)} %copy-done.8, ...), custom_call_target="tpu_custom_call", output_to_operand_aliasing={{0}: (2, {}), {1}: (3, {}), {2}: (4, {}), {3}: (5, {})} | custom-call | tf_op jit(solution)/shard_map/patch/pallas_call | solution.py:291
  78.8 13.6 %all-to-all-done.2.gathered_ref = bf16[64,24,128]{2,1,0:T(8,128)(2,1)S(1)} async-done(((bf16[64,24,128]{2,1,0:T(8,128)(2,1)}), bf16[64,24,128]{2,1,0:T(8,128)(2,1)S(1)}, u32[]{:S(2)}, u32[]{:S(2)}) %all-to-all-start.2) | async-done | bytes 393248 | tf_op jit(solution)/shard_map/all_to_all | solution.py:378
  92.5 0.0 copy-start.9
  92.5 0.8 copy-done.9
  93.2 1.8 %final.1 = (f32[16,4096]{1,0:T(8,128)}, f32[9,512]{1,0:T(8,128)}) custom-call(bf16[64,24,128]{2,1,0:T(8,128)(2,1)} %copy-done.9), custom_call_target="tpu_custom_call" | custom-call | tf_op jit(solution)/shard_map/final/pallas_call | solution.py:380
Async XLA Ops:
  0.6 21.8 %copy-start.6 = (bf16[2,136,256]{2,1,0:T(8,128)(2,1)S(1)}, bf16[2,136,256]{2,1,0:T(8,128)(2,1)}, u32[]{:S(2)}) copy-start(bf16[2,136,256]{2,1,0:T(8,128)(2,1)} %constant.11.clone.long_ref) | copy-start | bytes 417796
  2.4 20.1 %copy-start.4 = (bf16[2,256,256]{2,1,0:T(8,128)(2,1)S(1)}, bf16[2,256,256]{2,1,0:T(8,128)(2,1)}, u32[]{:S(2)}) copy-start(bf16[2,256,256]{2,1,0:T(8,128)(2,1)} %constant.10.clone.fwd_ref) | copy-start | bytes 786436
  2.4 20.1 %copy-start.5 = (bf16[2,136,256]{2,1,0:T(8,128)(2,1)S(1)}, bf16[2,136,256]{2,1,0:T(8,128)(2,1)}, u32[]{:S(2)}) copy-start(bf16[2,136,256]{2,1,0:T(8,128)(2,1)} %constant.12.clone.grad_ref) | copy-start | bytes 417796
  2.4 20.1 %copy-start.7 = (f32[9,512]{1,0:T(8,128)S(1)}, f32[9,512]{1,0:T(8,128)}, u32[]{:S(2)}) copy-start(f32[9,512]{1,0:T(8,128)} %s_ref.1) | copy-start | bytes 55300
  2.4 20.1 %all-to-all-start = ((f32[16,8,512]{2,0,1:T(8,128)}), f32[16,8,512]{2,0,1:T(8,128)S(1)}, u32[]{:S(2)}, u32[]{:S(2)}) async-start(f32[16,8,512]{2,0,1:T(8,128)} %bitcast.7), calls=%async_computation | async-start | bytes 524288 | tf_op jit(solution)/shard_map/all_to_all | solution.py:337
  10.1 12.3 %copy-start = (bf16[128,512]{1,0:T(8,128)(2,1)S(1)}, bf16[128,512]{1,0:T(8,128)(2,1)}, u32[]{:S(2)}) copy-start(bf16[128,512]{1,0:T(8,128)(2,1)} %q_ref.3) | copy-start | bytes 393220
  10.1 12.4 %copy-start.1 = (bf16[128,512]{1,0:T(8,128)(2,1)S(1)}, bf16[128,512]{1,0:T(8,128)(2,1)}, u32[]{:S(2)}) copy-start(bf16[128,512]{1,0:T(8,128)(2,1)} %k_ref.3) | copy-start | bytes 393220
  10.2 12.4 %copy-start.2 = (bf16[128,512]{1,0:T(8,128)(2,1)S(1)}, bf16[128,512]{1,0:T(8,128)(2,1)}, u32[]{:S(2)}) copy-start(bf16[128,512]{1,0:T(8,128)(2,1)} %v_ref.3) | copy-start | bytes 393220
  10.2 12.4 %copy-start.3 = (bf16[128,512]{1,0:T(8,128)(2,1)S(1)}, bf16[128,512]{1,0:T(8,128)(2,1)}, u32[]{:S(2)}) copy-start(bf16[128,512]{1,0:T(8,128)(2,1)} %c_ref.3) | copy-start | bytes 393220
  12.2 10.3 %collective-permute-start.1 = (bf16[288,512]{1,0:T(8,128)(2,1)}, bf16[288,512]{1,0:T(8,128)(2,1)S(1)}, u32[]{:S(2)}, u32[]{:S(2)}) collective-permute-start(bf16[288,512]{1,0:T(8,128)(2,1)} %get-tuple-element.24), channel_id=1, source_target_pairs={{1,0},{2,1},{3,2},{4,3},{5,4},{6,5},{7,6},{8,7},{9,8},{10,9},{11,1... | collective-permute-start | bytes 884744 | tf_op jit(solution)/shard_map/ppermute | solution.py:332
  16.7 5.7 %collective-permute-start = (bf16[272,512]{1,0:T(8,128)(2,1)}, bf16[272,512]{1,0:T(8,128)(2,1)S(1)}, u32[]{:S(2)}, u32[]{:S(2)}) collective-permute-start(bf16[272,512]{1,0:T(8,128)(2,1)} %get-tuple-element.23), channel_id=1, source_target_pairs={{0,1},{1,2},{2,3},{3,4},{4,5},{5,6},{6,7},{7,8},{8,9},{9,10},{10,1... | collective-permute-start | bytes 835592 | tf_op jit(solution)/shard_map/ppermute | solution.py:332
  26.0 0.6 copy-start.8
  59.1 1.3 %collective-permute-start.2 = (f32[8,128]{1,0:T(8,128)}, f32[8,128]{1,0:T(8,128)S(1)}, u32[]{:S(2)}, u32[]{:S(2)}) collective-permute-start(f32[8,128]{1,0:T(8,128)} %get-tuple-element.36), channel_id=1, source_target_pairs={{0,0},{1,1},{2,64},{3,65},{4,128},{5,129},{6,192},{7,193},{8,256},... | collective-permute-start | bytes 12296 | tf_op jit(solution)/shard_map/ppermute | solution.py:371
  60.4 0.6 copy-start.10
  62.4 30.0 %all-to-all-start.2 = ((bf16[64,24,128]{2,1,0:T(8,128)(2,1)}), bf16[64,24,128]{2,1,0:T(8,128)(2,1)S(1)}, u32[]{:S(2)}, u32[]{:S(2)}) async-start(bf16[64,24,128]{2,1,0:T(8,128)(2,1)} %spread.1), calls=%async_computation.2 | async-start | bytes 786432 | tf_op jit(solution)/shard_map/all_to_all | solution.py:378
  92.5 0.8 copy-start.9

commit v4 on v3

--- a/solution.py
+++ b/solution.py
@@ -20,8 +20,9 @@
 WIDE = 256
 EDGE = 16
 TILE = 128
-CHUNK = 24
-VMEM_LIMIT = 48 * 1024 * 1024
+CHUNK = 9
+VMEM_LIMIT = 24 * 1024 * 1024
+SMALL = pltpu.CompilerParams(vmem_limit_bytes=8 * 1024 * 1024)
 
 
 def two_parts(matrix):
@@ -58,17 +59,6 @@
     high, low = split(value)
     dot = functools.partial(jnp.dot, preferred_element_type=F32)
     return dot(matrix_high, high) + (dot(matrix_high, low) + dot(matrix_low, high))
-
-
-def last_rows(row_value, others):
-    first = row_value.astype(BF16).astype(F32)
-    row = lax.broadcasted_iota(jnp.int32, (8, TILE), 0)
-    return jnp.where(row == 0, first, jnp.where(row == 1, row_value - first, others))
-
-
-def as_chunk(tile, last):
-    first = tile.astype(BF16).astype(F32)
-    return jnp.concatenate([first, tile - first, last], 0).astype(BF16)
 
 
 def pack_kernel(q_ref, k_ref, v_ref, c_ref, right_ref, left_ref):
@@ -93,16 +83,16 @@
             jax.ShapeDtypeStruct((2 * ROWS + EDGE, channels), BF16),
             jax.ShapeDtypeStruct((2 * ROWS + 2 * EDGE, channels), BF16),
         ],
+        compiler_params=SMALL,
         name="pack",
     )(q_stream, k_stream, v_stream, cotangent)
 
 
 def layer_kernel(
-    place_ref,
     q_ref, k_ref, v_ref, c_ref, before_ref, after_ref,
     h_ref, s_ref, fwd_ref, long_ref, grad_ref,
-    mixed_ref, gq_ref, gk_ref, gv_ref, part_ref, fix_ref,
-    q_ext, k_ext, v_ext, e_ext, filt_all, late_all, short_all,
+    mixed_ref, gq_ref, gk_ref, gv_ref, part_ref, fix_ref, late_ref,
+    q_ext, k_ext, v_ext, e_ext, short_all,
 ):
     def f32(x):
         return x.astype(F32)
@@ -164,7 +154,7 @@
 
         long = dot3(long_ref[0], long_ref[1], times(x_f, h_f))
         pg = dot3(grad_ref[0], grad_ref[1], times_conj(lg_f, h_f))
-        filt_all[:, cols] = dot3(grad_ref[0, 0:ROWS], grad_ref[1, 0:ROWS], times_conj(lg_f, own_f))
+        filt = dot3(grad_ref[0, 0:ROWS], grad_ref[1, 0:ROWS], times_conj(lg_f, own_f))
 
         h0, h1, h127 = taps[0:1], taps[1:2], taps[127:128]
         p0, p1 = p_far[0:1], p_far[1:2]
@@ -194,8 +184,8 @@
         for j in range(3):
             short_all[j : j + 1, cols] += lacking * q_ext[136 - j : 137 - j]
 
-        late_all[0:1, cols] = p_own[1:2]
-        late_all[1:2, cols] = lg[128:129]
+        late_ref[0, :, cols] = p_own[1:2]
+        late_ref[1, :, cols] = lg[128:129]
         fix_ref[0:1, cols] = mixed[0:1]
         fix_ref[1:2, cols] = gq[0:1]
         fix_ref[2:3, cols] = gk[127:128]
@@ -205,83 +195,67 @@
         fix_ref[6:7, cols] = tap(1, 2) * h127 * a2[257:258]
         fix_ref[7:8, cols] = tap(2, 2) * h127 * a1[257:258]
 
-    place = place_ref[0]
-    row = lax.broadcasted_iota(jnp.int32, (8, TILE), 0)
-    late = []
-    for n in range(2):
-        rows = jnp.zeros((8, TILE), F32)
-        for h in range(4):
-            value = late_all[n : n + 1, h * TILE : (h + 1) * TILE]
-            rows = jnp.where(row == 2 + h, value, rows)
-        late.append(rows)
-    for m in range(4):
-        to_right = lax.rem(m + 64 - place, 4) == 1
-        others = jnp.where(to_right, late[0], late[1])
-        for g in range(m, 16, 4):
-            for h in range(4):
-                lanes = slice(h * TILE, (h + 1) * TILE)
-                value = short_all[g : g + 1, lanes] if g < 9 else jnp.zeros((1, TILE), F32)
-                part_ref[16 * h + g] = as_chunk(
-                    filt_all[8 * g : 8 * g + 8, lanes], last_rows(value, others)
-                )
-
-
-def run_layer(place, streams, before, after, taps, shorts, matrices):
+        for part in range(WIDE // TILE):
+            h = step * (WIDE // TILE) + part
+            lanes = slice(part * TILE, (part + 1) * TILE)
+            for g in range(16):
+                tile = filt[8 * g : 8 * g + 8, lanes]
+                part_ref[16 * h + g, 0:8] = tile.reshape(8, 1, TILE)
+                if g < 9:
+                    value = short_all[g : g + 1, h * TILE : (h + 1) * TILE]
+                else:
+                    value = jnp.zeros((1, TILE), F32)
+                part_ref[16 * h + g, 8] = value
+
+
+def run_layer(streams, before, after, taps, shorts, matrices):
     channels = streams[0].shape[1]
     out_rows = jax.ShapeDtypeStruct((ROWS, channels), BF16)
     ext = pltpu.VMEM((272, WIDE), F32)
     vmem = pl.BlockSpec(memory_space=pltpu.VMEM)
     return pl.pallas_call(
         layer_kernel,
-        in_specs=[pl.BlockSpec(memory_space=pltpu.SMEM)] + [vmem] * 11,
-        out_specs=[vmem] * 6,
+        in_specs=[vmem] * 11,
+        out_specs=[vmem] * 7,
         out_shape=[out_rows] * 4
         + [
-            jax.ShapeDtypeStruct((64, CHUNK, TILE), BF16),
+            jax.ShapeDtypeStruct((64, CHUNK, 1, TILE), F32),
             jax.ShapeDtypeStruct((8, channels), F32),
+            jax.ShapeDtypeStruct((2, 1, channels), F32),
         ],
         scratch_shapes=[
             ext, ext, ext,
             pltpu.VMEM((OUT, WIDE), F32),
-            pltpu.VMEM((ROWS, channels), F32),
-            pltpu.VMEM((8, channels), F32),
             pltpu.VMEM((16, channels), F32),
         ],
         compiler_params=pltpu.CompilerParams(vmem_limit_bytes=VMEM_LIMIT),
         name="layer",
-    )(place, *streams, before, after, taps, shorts, *matrices)
-
-
-def sum_kernel(place_ref, part_ref, tile_ref, short_ref, late_ref):
-    total = jnp.sum(part_ref[:, 0:EDGE].astype(F32), axis=0)
-    tile_ref[...] = total[0:8] + total[8:16]
-    total = jnp.sum(part_ref[:, EDGE:CHUNK].astype(F32), axis=0)
-    short_ref[...] = jnp.broadcast_to(total[0:1] + total[1:2], (8, TILE))
-    place, peers = place_ref[0], part_ref.shape[0]
-    before = part_ref[jnp.maximum(place - 1, 0), EDGE:CHUNK].astype(F32)
-    after = part_ref[jnp.minimum(place + 1, peers - 1), EDGE:CHUNK].astype(F32)
-    late_ref[0:8] = jnp.where(place > 0, before, 0.0)
-    late_ref[8:16] = jnp.where(place < peers - 1, after, 0.0)
-
-
-def patch_kernel(late_ref, fix_ref, mixed_in, gq_in, gk_in, gv_in, mixed_ref, gq_ref, gk_ref, gv_ref):
-    row = lax.broadcasted_iota(jnp.int32, (EDGE, TILE), 0)
+    )(*streams, before, after, taps, shorts, *matrices)
+
+
+def sum_kernel(part_ref, tile_ref, short_ref):
+    total = jnp.sum(part_ref[...], axis=0)
+    tile_ref[...] = total[0:8]
+    short_ref[...] = total[8:9]
+
+
+def patch_kernel(
+    p_ref, lg_ref, fix_ref, mixed_in, gq_in, gk_in, gv_in, mixed_ref, gq_ref, gk_ref, gv_ref
+):
+    row = lax.broadcasted_iota(jnp.int32, (EDGE, p_ref.shape[2]), 0)
     plan = (
-        (0, 0, 0, mixed_in, mixed_ref),
-        (1, 0, 0, gq_in, gq_ref),
-        (2, 8, EDGE - 1, gk_in, gk_ref),
-        (3, 8, EDGE - 1, gv_in, gv_ref),
+        (0, p_ref, 0, mixed_in, mixed_ref),
+        (1, p_ref, 0, gq_in, gq_ref),
+        (2, lg_ref, EDGE - 1, gk_in, gk_ref),
+        (3, lg_ref, EDGE - 1, gv_in, gv_ref),
     )
-    for n, source, place, old_ref, new_ref in plan:
-        for h in range(old_ref.shape[1] // TILE):
-            lanes = slice(h * TILE, (h + 1) * TILE)
-            late = late_ref[source + 2 + h : source + 3 + h]
-            value = fix_ref[n : n + 1, lanes] + fix_ref[4 + n : 5 + n, lanes] * late
-            old = old_ref[:, lanes].astype(F32)
-            new_ref[:, lanes] = jnp.where(row == place, value, old).astype(BF16)
-
-
-def patch(late, fix, outs):
+    for n, late_ref, place, old_ref, new_ref in plan:
+        value = fix_ref[n : n + 1] + fix_ref[4 + n : 5 + n] * late_ref[0]
+        old = old_ref[...].astype(F32)
+        new_ref[...] = jnp.where(row == place, value, old).astype(BF16)
+
+
+def patch(late_p, late_lg, fix, outs):
     channels = outs[0].shape[1]
 
     def edge(block):
@@ -292,36 +266,37 @@
         patch_kernel,
         grid=(1,),
         in_specs=[
-            pl.BlockSpec(late.shape, lambda i: (0, 0)),
+            pl.BlockSpec(late_p.shape, lambda i: (0, 0, 0)),
+            pl.BlockSpec(late_lg.shape, lambda i: (0, 0, 0)),
             pl.BlockSpec(fix.shape, lambda i: (0, 0)),
         ]
         + edges,
         out_specs=edges,
         out_shape=[jax.ShapeDtypeStruct(o.shape, o.dtype) for o in outs],
-        input_output_aliases={2: 0, 3: 1, 4: 2, 5: 3},
+        input_output_aliases={3: 0, 4: 1, 5: 2, 6: 3},
+        compiler_params=SMALL,
         name="patch",
-    )(late, fix, *outs)
-
-
-def spread_kernel(tile_ref, short_ref, out_ref):
-    chunk = as_chunk(tile_ref[...], last_rows(short_ref[0:1], jnp.zeros((8, TILE), F32)))
-    out_ref[...] = jnp.broadcast_to(chunk[None], out_ref.shape)
+    )(late_p, late_lg, fix, *outs)
+
+
+def spread_kernel(tile_ref, short_ref, late_ref, out_ref, p_ref, lg_ref):
+    peers = out_ref.shape[0]
+    out_ref[:, 0:8] = jnp.broadcast_to(tile_ref[...][None], (peers, 8, 1, TILE))
+    out_ref[:, 8:9] = jnp.broadcast_to(short_ref[...][None], (peers, 1, 1, TILE))
+    p_ref[...] = late_ref[0:1]
+    lg_ref[...] = late_ref[1:2]
 
 
 def final_kernel(scale, groups, gathered_ref, filter_ref, short_ref):
     for h in range(4):
         for d in range(groups):
             for half in range(2):
-                chunk = gathered_ref[h * 16 + d * 2 + half].astype(F32)
+                tile = gathered_ref[h * 16 + d * 2 + half, 0:8].reshape(8, TILE)
                 start = (d * 4 + h) * TILE
-                filter_ref[8 * half : 8 * half + 8, start : start + TILE] = (
-                    chunk[0:8] + chunk[8:16]
-                ) * scale
+                filter_ref[8 * half : 8 * half + 8, start : start + TILE] = tile * scale
         for g in range(9):
-            chunk = gathered_ref[h * 16 + g].astype(F32)
-            short_ref[g : g + 1, h * TILE : (h + 1) * TILE] = (
-                chunk[16:17] + chunk[17:18]
-            ) * scale
+            row = gathered_ref[h * 16 + g, 8] * scale
+            short_ref[g : g + 1, h * TILE : (h + 1) * TILE] = row
 
 
 def on_device(q_stream, k_stream, v_stream, filter_taps, short_taps, cotangent, *, matrices):
@@ -335,10 +310,8 @@
     before = shifted(right, 1)
     after = shifted(left, -1)
     taps = lax.all_to_all(filter_taps, "dp", split_axis=1, concat_axis=0, tiled=True)
-    place = lax.axis_index("ctx").astype(jnp.int32).reshape(1)
-
-    *outs, part, fix = run_layer(
-        place,
+
+    *outs, part, fix, late = run_layer(
         (q_stream, k_stream, v_stream, cotangent),
         before,
         after,
@@ -349,17 +322,17 @@
 
     part = lax.all_to_all(part, "ctx", split_axis=0, concat_axis=0, tiled=True)
     vmem = pl.BlockSpec(memory_space=pltpu.VMEM)
-    tile, short, late = pl.pallas_call(
+    tile, short = pl.pallas_call(
         sum_kernel,
-        in_specs=[pl.BlockSpec(memory_space=pltpu.SMEM), vmem],
-        out_specs=[vmem] * 3,
+        in_specs=[vmem],
+        out_specs=[vmem] * 2,
         out_shape=[
-            jax.ShapeDtypeStruct((8, TILE), F32),
-            jax.ShapeDtypeStruct((8, TILE), F32),
-            jax.ShapeDtypeStruct((EDGE, TILE), F32),
-        ],
+            jax.ShapeDtypeStruct((8, 1, TILE), F32),
+            jax.ShapeDtypeStruct((1, 1, TILE), F32),
+        ],
+        compiler_params=SMALL,
         name="sum",
-    )(place, part)
+    )(part)
 
     pairs = [
         (d * peers + h * 16 + e * 2 + half, e * peers + h * 16 + d * 2 + half)
@@ -369,12 +342,14 @@
         for half in range(2)
     ]
     tile = lax.ppermute(tile, ("dp", "ctx"), pairs)
-    sent = pl.pallas_call(
+    edge_row = jax.ShapeDtypeStruct((1, 1, q_stream.shape[1]), F32)
+    sent, late_p, late_lg = pl.pallas_call(
         spread_kernel,
-        out_shape=jax.ShapeDtypeStruct((peers, CHUNK, TILE), BF16),
+        out_shape=[jax.ShapeDtypeStruct((peers, CHUNK, 1, TILE), F32), edge_row, edge_row],
+        compiler_params=SMALL,
         name="spread",
-    )(tile, short)
-    outs = patch(late, fix, outs)
+    )(tile, short, late)
+    outs = patch(shifted(late_p, 1), shifted(late_lg, -1), fix, outs)
     gathered = lax.all_to_all(sent, "ctx", split_axis=0, concat_axis=0, tiled=True)
     scale = 1.0 / math.sqrt(ROWS * peers)
     grad_filter, grad_short = pl.pallas_call(
@@ -383,6 +358,7 @@
             jax.ShapeDtypeStruct(filter_taps.shape, F32),
             jax.ShapeDtypeStruct(short_taps.shape, F32),
         ],
+        compiler_params=SMALL,
         name="final",
     )(gathered)
     return (*outs, grad_filter, grad_short)

time: 95.6 us -> 85.1 us (0.89)
  waiting for transfers between devices: 17.4 us -> 10.3 us
  Pallas kernels: 11.8 us -> 6.89 us
  starting transfers between devices: 30.5 us -> 35.4 us
  local copies, waits for them, and re-layouts: 3.69 us -> 1.75 us
  blocking collectives: 30.8 us -> 29.4 us
    all_to_all x1, waiting for transfers between devices: 13.6 us -> 3.57 us  [on_device(): lax.all_to_all(sent, 'ctx', split_axis=0, concat_axis=0, tiled=True)]
    ppermute x2 -> x4, starting transfers between devices: 6.48 us -> 12.1 us  [shifted(): return lax.ppermute(value, 'ctx', pairs)]
    ppermute x2 -> x4, waiting for transfers between devices: 3.78 us -> 6.74 us  [shifted(): return lax.ppermute(value, 'ctx', pairs)]
    pallas_call x4, Pallas kernels: 8.04 us -> 5.92 us  [the longest x1 3.44 us: run_layer(): pl.pallas_call(layer_kernel, in_specs=[vmem] * 11, out_specs=[vmem] * 7,...]
    pallas_call x1, Pallas kernels: 1.99 us -> 0.04 us  [pack(): pl.pallas_call(pack_kernel, in_specs=[vmem] * 4, out_specs=[vmem] * 2, ou...]
    unnamed x22 -> x16, local copies, waits for them, and re-layouts: 1.99 us -> 0.04 us
    all_to_all x1, blocking collectives: 30.8 us -> 29.4 us  [on_device(): part = lax.all_to_all(part, 'ctx', split_axis=0, concat_axis=0, tiled=True)]
  transfers between devices with their start and end apart: 5 -> 7, of which waited for: 2 -> 3; matrix products, arithmetic and copies ran while one was open for 0% -> 0% of each run, Pallas kernels for 4% -> 2%
where the time goes in v4:
time: 85.1 us; the launch traced here: 84.6 us
  starting transfers between devices  35.4 us (42%)
  blocking collectives  29.4 us (35%)
  waiting for transfers between devices  10.3 us (12%)
  Pallas kernels  6.89 us (8%)
  local copies, waits for them, and re-layouts  1.75 us (2%)
    all_to_all x1, blocking collectives, on_device(): part = lax.all_to_all(part, 'ctx', split_axis=0, concat_axis=0, tiled=True)  29.4 us
    all_to_all x1, starting transfers between devices, on_device(): lax.all_to_all(sent, 'ctx', split_axis=0, concat_axis=0, tiled=True)  14.9 us
    ppermute x4, starting transfers between devices, shifted(): return lax.ppermute(value, 'ctx', pairs)  12.1 us
    all_to_all x1, starting transfers between devices, on_device(): lax.all_to_all(filter_taps, 'dp', split_axis=1, concat_axis=0, tiled=True)  7.79 us
    ppermute x4, waiting for transfers between devices, shifted(): return lax.ppermute(value, 'ctx', pairs)  6.74 us
    all_to_all x1, waiting for transfers between devices, on_device(): lax.all_to_all(sent, 'ctx', split_axis=0, concat_axis=0, tiled=True)  3.57 us
    pallas_call x1, Pallas kernels, run_layer(): pl.pallas_call(layer_kernel, in_specs=[vmem] * 11, out_specs=[vmem] * 7,...  3.44 us
    all_to_all x1, local copies, waits for them, and re-layouts, on_device(): lax.all_to_all(filter_taps, 'dp', split_axis=1, concat_axis=0, tiled=True)  1.71 us
  transfers between devices with their start and end apart: 7, of which 3 were waited for; matrix products, arithmetic and copies ran while one was open for 0% of the time, Pallas kernels for 2%

profile of v4, /device:TPU:1, one launch (start us, length us, event | category | flops | bytes accessed | tf_op | source)
XLA Modules:
  0.0 84.6 jit_solution(15512191959440344676)
XLA Ops:
  0.6 0.0 copy-start.6
  0.6 1.7 %copy.22 = f32[2,8,8,512]{3,2,0,1:T(8,128)} copy(f32[2,8,8,512]{3,2,1,0:T(8,128)} %bitcast.8) | data formatting | bytes 524288 | tf_op jit(solution)/shard_map/all_to_all | solution.py:312
  2.4 0.0 copy-start
  2.4 0.0 copy-start.1
  2.4 0.0 copy-start.2
  2.4 0.0 copy-start.3
  2.4 7.8 %all-to-all-start = ((f32[16,8,512]{2,0,1:T(8,128)}), f32[16,8,512]{2,0,1:T(8,128)S(1)}, u32[]{:S(2)}, u32[]{:S(2)}) async-start(f32[16,8,512]{2,0,1:T(8,128)} %bitcast.6), calls=%async_computation | async-start | bytes 524288 | tf_op jit(solution)/shard_map/all_to_all | solution.py:312
  10.2 0.0 copy-done
  10.2 0.0 copy-done.1
  10.2 0.0 copy-done.2
  10.2 0.0 copy-done.3
  10.2 0.0 copy-start.4
  10.2 0.0 copy-start.5
  10.2 0.0 copy-start.7
  10.3 4.7 %collective-permute-start.1 = (bf16[288,512]{1,0:T(8,128)(2,1)S(1)}, bf16[288,512]{1,0:T(8,128)(2,1)S(1)}, u32[]{:S(2)}, u32[]{:S(2)}) collective-permute-start(bf16[288,512]{1,0:T(8,128)(2,1)S(1)} %get-tuple-element.27), channel_id=1, source_target_pairs={{1,0},{2,1},{3,2},{4,3},{5,4},{6,5},{7,6},{8,7},{9,8},{10,9},{11,1... | collective-permute-start | bytes 884744 | tf_op jit(solution)/shard_map/ppermute | solution.py:307
  15.0 1.9 %collective-permute-start = (bf16[272,512]{1,0:T(8,128)(2,1)S(1)}, bf16[272,512]{1,0:T(8,128)(2,1)S(1)}, u32[]{:S(2)}, u32[]{:S(2)}) collective-permute-start(bf16[272,512]{1,0:T(8,128)(2,1)S(1)} %get-tuple-element.26), channel_id=1, source_target_pairs={{0,1},{1,2},{2,3},{3,4},{4,5},{5,6},{6,7},{7,8},{8,9},{9,10},{10,1... | collective-permute-start | bytes 835592 | tf_op jit(solution)/shard_map/ppermute | solution.py:307
  16.9 3.5 %collective-permute-done.before_ref = bf16[272,512]{1,0:T(8,128)(2,1)S(1)} collective-permute-done((bf16[272,512]{1,0:T(8,128)(2,1)S(1)}, bf16[272,512]{1,0:T(8,128)(2,1)S(1)}, u32[]{:S(2)}, u32[]{:S(2)}) %collective-permute-start) | collective-permute-done | bytes 278560 | tf_op jit(solution)/shard_map/ppermute | solution.py:307
  20.4 0.0 collective-permute-done.1.after_ref
  20.4 0.0 all-to-all-done
  20.4 0.0 copy-done.6
  20.4 0.0 copy-done.4
  20.4 0.0 copy-done.5
  20.4 0.0 copy-done.7
  20.4 3.4 %layer.1 = (bf16[128,512]{1,0:T(8,128)(2,1)}, bf16[128,512]{1,0:T(8,128)(2,1)}, bf16[128,512]{1,0:T(8,128)(2,1)}, bf16[128,512]{1,0:T(8,128)(2,1)}, f32[64,9,1,1...) custom-call(bf16[128,512]{1,0:T(8,128)(2,1)S(1)} %copy-done, bf16[128,512]{1,0:T(8,128)(2,1)S(1)} %copy-done.1, ...), custom_call_target="tpu_custom_call" | custom-call | tf_op jit(solution)/shard_map/layer/pallas_call | solution.py:216
  23.9 29.4 %all_to_all.29.part_ref = f32[64,9,1,128]{3,2,1,0:T(1,128)S(1)} all-to-all(f32[64,9,1,128]{3,2,1,0:T(1,128)S(1)} %get-tuple-element.28), channel_id=1, replica_groups=mesh['dp'=8,'ctx'=64] {'ctx'}, dimensions={0} | all-to-all | bytes 589824 | tf_op jit(solution)/shard_map/all_to_all | solution.py:323
  53.3 0.2 sum.1
  53.5 0.7 collective-permute-start.2
  54.2 0.0 collective-permute-done.2.tile_ref
  54.2 0.9 %spread.1 = (f32[64,9,1,128]{3,2,1,0:T(1,128)}, f32[1,1,512]{2,1,0:T(1,128)S(1)}, f32[1,1,512]{2,1,0:T(1,128)S(1)}) custom-call(f32[8,1,128]{2,1,0:T(1,128)S(1)} %collective-permute-done.2.tile_ref, f32[1,1,128]{2,1,0:T(1,128)S(1)} %get-tuple-element.30.short_ref, f32[2,1,512]{2,1,0:T(1,128)S(1)} %get-tuple-element.31.late_ref), custom_call_target="tpu_custom_call" | custom-call | tf_op jit(solution)/shard_map/spread/pallas_call | solution.py:346
  55.1 14.9 %all-to-all-start.2 = ((f32[64,9,1,128]{3,2,1,0:T(1,128)}), f32[64,9,1,128]{3,2,1,0:T(1,128)S(1)}, u32[]{:S(2)}, u32[]{:S(2)}) async-start(f32[64,9,1,128]{3,2,1,0:T(1,128)} %get-tuple-element.43), calls=%async_computation.2 | async-start | bytes 589824 | tf_op jit(solution)/shard_map/all_to_all | solution.py:353
  70.0 3.5 %collective-permute-start.3 = (f32[1,1,512]{2,1,0:T(1,128)S(1)}, f32[1,1,512]{2,1,0:T(1,128)S(1)}, u32[]{:S(2)}, u32[]{:S(2)}) collective-permute-start(f32[1,1,512]{2,1,0:T(1,128)S(1)} %get-tuple-element.32), channel_id=1, source_target_pairs={{0,1},{1,2},{2,3},{3,4},{4,5},{5,6},{6,7},{7,8},{8,9},{9,10},{10,1... | collective-permute-start | bytes 6152 | tf_op jit(solution)/shard_map/ppermute | solution.py:307
  73.5 1.9 %collective-permute-start.4 = (f32[1,1,512]{2,1,0:T(1,128)S(1)}, f32[1,1,512]{2,1,0:T(1,128)S(1)}, u32[]{:S(2)}, u32[]{:S(2)}) collective-permute-start(f32[1,1,512]{2,1,0:T(1,128)S(1)} %get-tuple-element.33), channel_id=1, source_target_pairs={{1,0},{2,1},{3,2},{4,3},{5,4},{6,5},{7,6},{8,7},{9,8},{10,9},{11,1... | collective-permute-start | bytes 6152 | tf_op jit(solution)/shard_map/ppermute | solution.py:307
  75.5 0.0 collective-permute-done.3.p_ref
  75.5 3.3 %collective-permute-done.4.lg_ref = f32[1,1,512]{2,1,0:T(1,128)S(1)} collective-permute-done((f32[1,1,512]{2,1,0:T(1,128)S(1)}, f32[1,1,512]{2,1,0:T(1,128)S(1)}, u32[]{:S(2)}, u32[]{:S(2)}) %collective-permute-start.4) | collective-permute-done | bytes 2080 | tf_op jit(solution)/shard_map/ppermute | solution.py:307
  78.7 1.4 %patch.1 = (bf16[128,512]{1,0:T(8,128)(2,1)}, bf16[128,512]{1,0:T(8,128)(2,1)}, bf16[128,512]{1,0:T(8,128)(2,1)}, bf16[128,512]{1,0:T(8,128)(2,1)}) custom-call(f32[1,1,512]{2,1,0:T(1,128)S(1)} %collective-permute-done.3.p_ref, ...), custom_call_target="tpu_custom_call", output_to_operand_aliasing={{0}: (3, {}), {1}: (4, {}), {2}: (5, {}), {3}: (6, {})} | custom-call | tf_op jit(solution)/shard_map/patch/pallas_call | solution.py:265
  80.1 3.6 %all-to-all-done.2.gathered_ref = f32[64,9,1,128]{3,2,1,0:T(1,128)S(1)} async-done(((f32[64,9,1,128]{3,2,1,0:T(1,128)}), f32[64,9,1,128]{3,2,1,0:T(1,128)S(1)}, u32[]{:S(2)}, u32[]{:S(2)}) %all-to-all-start.2) | async-done | bytes 294944 | tf_op jit(solution)/shard_map/all_to_all | solution.py:353
  83.7 0.9 %final.1 = (f32[16,4096]{1,0:T(8,128)}, f32[9,512]{1,0:T(8,128)}) custom-call(f32[64,9,1,128]{3,2,1,0:T(1,128)S(1)} %all-to-all-done.2.gathered_ref), custom_call_target="tpu_custom_call" | custom-call | tf_op jit(solution)/shard_map/final/pallas_call | solution.py:355
  (1 shorter events, 0.0 us)
Async XLA Ops:
  0.6 19.8 %copy-start.6 = (bf16[2,136,256]{2,1,0:T(8,128)(2,1)S(1)}, bf16[2,136,256]{2,1,0:T(8,128)(2,1)}, u32[]{:S(2)}) copy-start(bf16[2,136,256]{2,1,0:T(8,128)(2,1)} %constant.7.clone.long_ref) | copy-start | bytes 417796
  2.4 7.8 %copy-start = (bf16[128,512]{1,0:T(8,128)(2,1)S(1)}, bf16[128,512]{1,0:T(8,128)(2,1)}, u32[]{:S(2)}) copy-start(bf16[128,512]{1,0:T(8,128)(2,1)} %q_ref.3) | copy-start | bytes 393220
  2.4 7.8 %copy-start.1 = (bf16[128,512]{1,0:T(8,128)(2,1)S(1)}, bf16[128,512]{1,0:T(8,128)(2,1)}, u32[]{:S(2)}) copy-start(bf16[128,512]{1,0:T(8,128)(2,1)} %k_ref.3) | copy-start | bytes 393220
  2.4 7.8 %copy-start.2 = (bf16[128,512]{1,0:T(8,128)(2,1)S(1)}, bf16[128,512]{1,0:T(8,128)(2,1)}, u32[]{:S(2)}) copy-start(bf16[128,512]{1,0:T(8,128)(2,1)} %v_ref.3) | copy-start | bytes 393220
  2.4 7.8 %copy-start.3 = (bf16[128,512]{1,0:T(8,128)(2,1)S(1)}, bf16[128,512]{1,0:T(8,128)(2,1)}, u32[]{:S(2)}) copy-start(bf16[128,512]{1,0:T(8,128)(2,1)} %c_ref.3) | copy-start | bytes 393220
  2.4 18.0 %all-to-all-start = ((f32[16,8,512]{2,0,1:T(8,128)}), f32[16,8,512]{2,0,1:T(8,128)S(1)}, u32[]{:S(2)}, u32[]{:S(2)}) async-start(f32[16,8,512]{2,0,1:T(8,128)} %bitcast.6), calls=%async_computation | async-start | bytes 524288 | tf_op jit(solution)/shard_map/all_to_all | solution.py:312
  10.2 10.2 %copy-start.4 = (bf16[2,256,256]{2,1,0:T(8,128)(2,1)S(1)}, bf16[2,256,256]{2,1,0:T(8,128)(2,1)}, u32[]{:S(2)}) copy-start(bf16[2,256,256]{2,1,0:T(8,128)(2,1)} %constant.6.clone.fwd_ref) | copy-start | bytes 786436
  10.2 10.2 %copy-start.5 = (bf16[2,136,256]{2,1,0:T(8,128)(2,1)S(1)}, bf16[2,136,256]{2,1,0:T(8,128)(2,1)}, u32[]{:S(2)}) copy-start(bf16[2,136,256]{2,1,0:T(8,128)(2,1)} %constant.8.clone.grad_ref) | copy-start | bytes 417796
  10.2 10.2 %copy-start.7 = (f32[9,512]{1,0:T(8,128)S(1)}, f32[9,512]{1,0:T(8,128)}, u32[]{:S(2)}) copy-start(f32[9,512]{1,0:T(8,128)} %s_ref.1) | copy-start | bytes 55300
  10.3 10.1 %collective-permute-start.1 = (bf16[288,512]{1,0:T(8,128)(2,1)S(1)}, bf16[288,512]{1,0:T(8,128)(2,1)S(1)}, u32[]{:S(2)}, u32[]{:S(2)}) collective-permute-start(bf16[288,512]{1,0:T(8,128)(2,1)S(1)} %get-tuple-element.27), channel_id=1, source_target_pairs={{1,0},{2,1},{3,2},{4,3},{5,4},{6,5},{7,6},{8,7},{9,8},{10,9},{11,1... | collective-permute-start | bytes 884744 | tf_op jit(solution)/shard_map/ppermute | solution.py:307
  15.0 5.4 %collective-permute-start = (bf16[272,512]{1,0:T(8,128)(2,1)S(1)}, bf16[272,512]{1,0:T(8,128)(2,1)S(1)}, u32[]{:S(2)}, u32[]{:S(2)}) collective-permute-start(bf16[272,512]{1,0:T(8,128)(2,1)S(1)} %get-tuple-element.26), channel_id=1, source_target_pairs={{0,1},{1,2},{2,3},{3,4},{4,5},{5,6},{6,7},{7,8},{8,9},{9,10},{10,1... | collective-permute-start | bytes 835592 | tf_op jit(solution)/shard_map/ppermute | solution.py:307
  53.5 0.7 collective-permute-start.2
  55.1 28.6 %all-to-all-start.2 = ((f32[64,9,1,128]{3,2,1,0:T(1,128)}), f32[64,9,1,128]{3,2,1,0:T(1,128)S(1)}, u32[]{:S(2)}, u32[]{:S(2)}) async-start(f32[64,9,1,128]{3,2,1,0:T(1,128)} %get-tuple-element.43), calls=%async_computation.2 | async-start | bytes 589824 | tf_op jit(solution)/shard_map/all_to_all | solution.py:353
  70.0 5.5 %collective-permute-start.3 = (f32[1,1,512]{2,1,0:T(1,128)S(1)}, f32[1,1,512]{2,1,0:T(1,128)S(1)}, u32[]{:S(2)}, u32[]{:S(2)}) collective-permute-start(f32[1,1,512]{2,1,0:T(1,128)S(1)} %get-tuple-element.32), channel_id=1, source_target_pairs={{0,1},{1,2},{2,3},{3,4},{4,5},{5,6},{6,7},{7,8},{8,9},{9,10},{10,1... | collective-permute-start | bytes 6152 | tf_op jit(solution)/shard_map/ppermute | solution.py:307
  73.5 5.2 %collective-permute-start.4 = (f32[1,1,512]{2,1,0:T(1,128)S(1)}, f32[1,1,512]{2,1,0:T(1,128)S(1)}, u32[]{:S(2)}, u32[]{:S(2)}) collective-permute-start(f32[1,1,512]{2,1,0:T(1,128)S(1)} %get-tuple-element.33), channel_id=1, source_target_pairs={{1,0},{2,1},{3,2},{4,3},{5,4},{6,5},{7,6},{8,7},{9,8},{10,9},{11,1... | collective-permute-start | bytes 6152 | tf_op jit(solution)/shard_map/ppermute | solution.py:307

commit v5 on v4

--- a/solution.py
+++ b/solution.py
@@ -20,6 +20,7 @@
 WIDE = 256
 EDGE = 16
 TILE = 128
+FAR_ROWS = 288
 CHUNK = 9
 VMEM_LIMIT = 24 * 1024 * 1024
 SMALL = pltpu.CompilerParams(vmem_limit_bytes=8 * 1024 * 1024)
@@ -61,42 +62,62 @@
     return dot(matrix_high, high) + (dot(matrix_high, low) + dot(matrix_low, high))
 
 
-def pack_kernel(q_ref, k_ref, v_ref, c_ref, right_ref, left_ref):
-    tail, head = pl.ds(ROWS - EDGE, EDGE), pl.ds(0, EDGE)
-    right_ref[0:ROWS] = k_ref[...]
-    right_ref[ROWS : 2 * ROWS] = v_ref[...]
-    right_ref[2 * ROWS : 2 * ROWS + EDGE] = q_ref[tail]
-    left_ref[0:ROWS] = q_ref[...]
-    left_ref[ROWS : 2 * ROWS] = c_ref[...]
-    left_ref[2 * ROWS : 2 * ROWS + EDGE] = k_ref[head]
-    left_ref[2 * ROWS + EDGE : 2 * ROWS + 2 * EDGE] = v_ref[head]
-
-
-def pack(q_stream, k_stream, v_stream, cotangent):
+def pack_kernel(place_ref, q_ref, k_ref, v_ref, c_ref, far_ref, near_ref):
+    def to_right(ref):
+        ref[0:ROWS] = k_ref[...]
+        ref[ROWS : 2 * ROWS] = v_ref[...]
+        ref[2 * ROWS : 2 * ROWS + EDGE] = q_ref[ROWS - EDGE : ROWS]
+
+    def to_left(ref):
+        ref[0:ROWS] = q_ref[...]
+        ref[ROWS : 2 * ROWS] = c_ref[...]
+        ref[2 * ROWS : 2 * ROWS + EDGE] = k_ref[0:EDGE]
+        ref[2 * ROWS + EDGE : 2 * ROWS + 2 * EDGE] = v_ref[0:EDGE]
+
+    odd = lax.rem(place_ref[0], 2) == 1
+
+    @pl.when(odd)
+    def _():
+        to_right(far_ref)
+        to_left(near_ref)
+
+    @pl.when(jnp.logical_not(odd))
+    def _():
+        to_left(far_ref)
+        to_right(near_ref)
+
+
+def pack(place, q_stream, k_stream, v_stream, cotangent):
     channels = q_stream.shape[1]
     vmem = pl.BlockSpec(memory_space=pltpu.VMEM)
     return pl.pallas_call(
         pack_kernel,
-        in_specs=[vmem] * 4,
+        in_specs=[pl.BlockSpec(memory_space=pltpu.SMEM)] + [vmem] * 4,
         out_specs=[vmem] * 2,
         out_shape=[
-            jax.ShapeDtypeStruct((2 * ROWS + EDGE, channels), BF16),
+            jax.ShapeDtypeStruct((FAR_ROWS, channels), BF16),
             jax.ShapeDtypeStruct((2 * ROWS + 2 * EDGE, channels), BF16),
         ],
         compiler_params=SMALL,
         name="pack",
-    )(q_stream, k_stream, v_stream, cotangent)
+    )(place, q_stream, k_stream, v_stream, cotangent)
+
+
+def seat(h, owner, half):
+    return 16 * h + 8 * half + 2 * (owner % 4) + owner // 4
 
 
 def layer_kernel(
-    q_ref, k_ref, v_ref, c_ref, before_ref, after_ref,
+    place_ref,
+    q_ref, k_ref, v_ref, c_ref, far_ref, near_ref,
     h_ref, s_ref, fwd_ref, long_ref, grad_ref,
     mixed_ref, gq_ref, gk_ref, gv_ref, part_ref, fix_ref, late_ref,
-    q_ext, k_ext, v_ext, e_ext, short_all,
+    q_ext, k_ext, v_ext, c_next, e_ext, short_all,
 ):
     def f32(x):
         return x.astype(F32)
 
+    odd = lax.rem(place_ref[0], 2) == 1
     fh, fl = fwd_ref[0], fwd_ref[1]
     fh_half, fl_half = fh[:, 0:HALF], fl[:, 0:HALF]
     freq = lax.broadcasted_iota(jnp.int32, (HALF, WIDE), 0)
@@ -114,15 +135,27 @@
     for step in range(q_ref.shape[1] // WIDE):
         cols = pl.ds(step * WIDE, WIDE)
 
-        q_ext[0:8] = f32(before_ref[2 * ROWS : 2 * ROWS + EDGE, cols])[8:16]
+        def stage(before_ref, after_ref):
+            q_ext[0:8] = f32(before_ref[2 * ROWS : 2 * ROWS + EDGE, cols])[8:16]
+            q_ext[136:264] = f32(after_ref[0:ROWS, cols])
+            c_next[...] = f32(after_ref[ROWS : 2 * ROWS, cols])
+            for n, ext in ((0, k_ext), (1, v_ext)):
+                ext[8:136] = f32(before_ref[ROWS * n : ROWS * (n + 1), cols])
+                start = 2 * ROWS + EDGE * n
+                ext[264:272] = f32(after_ref[start : start + EDGE, cols])[0:8]
+
+        @pl.when(odd)
+        def _():
+            stage(near_ref, far_ref)
+
+        @pl.when(jnp.logical_not(odd))
+        def _():
+            stage(far_ref, near_ref)
+
         q_ext[8:136] = f32(q_ref[:, cols])
-        q_ext[136:264] = f32(after_ref[0:ROWS, cols])
-        for n, ext, own in ((0, k_ext, k_ref), (1, v_ext, v_ref)):
+        for ext, own in ((k_ext, k_ref), (v_ext, v_ref)):
             ext[0:8] = jnp.zeros((8, WIDE), F32)
-            ext[8:136] = f32(before_ref[ROWS * n : ROWS * (n + 1), cols])
             ext[136:264] = f32(own[:, cols])
-            start = 2 * ROWS + EDGE * n
-            ext[264:272] = f32(after_ref[start : start + EDGE, cols])[0:8]
 
         def tap(s, j):
             return s_ref[3 * s + j : 3 * s + j + 1, cols]
@@ -141,7 +174,7 @@
         p_before = jnp.concatenate([jnp.where(row < 2, 0.0, product[0:8]), product[8:128]], 0)
         p_own, p_far = product[128:256], product[256:264]
         cot = f32(c_ref[:, cols])
-        cot_next = f32(after_ref[ROWS : 2 * ROWS, cols])
+        cot_next = c_next[...]
         lg = jnp.concatenate([cot, cot_next], 0) * a0
 
         taps = h_ref[:, cols]
@@ -200,22 +233,22 @@
             lanes = slice(part * TILE, (part + 1) * TILE)
             for g in range(16):
                 tile = filt[8 * g : 8 * g + 8, lanes]
-                part_ref[16 * h + g, 0:8] = tile.reshape(8, 1, TILE)
+                part_ref[seat(h, g // 2, g % 2), 0:8] = tile.reshape(8, 1, TILE)
                 if g < 9:
                     value = short_all[g : g + 1, h * TILE : (h + 1) * TILE]
                 else:
                     value = jnp.zeros((1, TILE), F32)
-                part_ref[16 * h + g, 8] = value
-
-
-def run_layer(streams, before, after, taps, shorts, matrices):
+                part_ref[seat(h, g // 2, g % 2), 8] = value
+
+
+def run_layer(place, streams, far, near, taps, shorts, matrices):
     channels = streams[0].shape[1]
     out_rows = jax.ShapeDtypeStruct((ROWS, channels), BF16)
     ext = pltpu.VMEM((272, WIDE), F32)
     vmem = pl.BlockSpec(memory_space=pltpu.VMEM)
     return pl.pallas_call(
         layer_kernel,
-        in_specs=[vmem] * 11,
+        in_specs=[pl.BlockSpec(memory_space=pltpu.SMEM)] + [vmem] * 11,
         out_specs=[vmem] * 7,
         out_shape=[out_rows] * 4
         + [
@@ -225,12 +258,13 @@
         ],
         scratch_shapes=[
             ext, ext, ext,
+            pltpu.VMEM((ROWS, WIDE), F32),
             pltpu.VMEM((OUT, WIDE), F32),
             pltpu.VMEM((16, channels), F32),
         ],
         compiler_params=pltpu.CompilerParams(vmem_limit_bytes=VMEM_LIMIT),
         name="layer",
-    )(*streams, before, after, taps, shorts, *matrices)
+    )(place, *streams, far, near, taps, shorts, *matrices)
 
 
 def sum_kernel(part_ref, tile_ref, short_ref):
@@ -244,36 +278,25 @@
 ):
     row = lax.broadcasted_iota(jnp.int32, (EDGE, p_ref.shape[2]), 0)
     plan = (
-        (0, p_ref, 0, mixed_in, mixed_ref),
-        (1, p_ref, 0, gq_in, gq_ref),
-        (2, lg_ref, EDGE - 1, gk_in, gk_ref),
-        (3, lg_ref, EDGE - 1, gv_in, gv_ref),
+        (0, p_ref, 0, 0, mixed_in, mixed_ref),
+        (1, p_ref, 0, 0, gq_in, gq_ref),
+        (2, lg_ref, ROWS - EDGE, EDGE - 1, gk_in, gk_ref),
+        (3, lg_ref, ROWS - EDGE, EDGE - 1, gv_in, gv_ref),
     )
-    for n, late_ref, place, old_ref, new_ref in plan:
+    for n, late_ref, start, place, old_ref, new_ref in plan:
+        new_ref[...] = old_ref[...]
         value = fix_ref[n : n + 1] + fix_ref[4 + n : 5 + n] * late_ref[0]
-        old = old_ref[...].astype(F32)
-        new_ref[...] = jnp.where(row == place, value, old).astype(BF16)
+        old = old_ref[start : start + EDGE].astype(F32)
+        new_ref[start : start + EDGE] = jnp.where(row == place, value, old).astype(BF16)
 
 
 def patch(late_p, late_lg, fix, outs):
-    channels = outs[0].shape[1]
-
-    def edge(block):
-        return pl.BlockSpec((EDGE, channels), lambda i: (block, 0))
-
-    edges = [edge(0), edge(0), edge(ROWS // EDGE - 1), edge(ROWS // EDGE - 1)]
+    vmem = pl.BlockSpec(memory_space=pltpu.VMEM)
     return pl.pallas_call(
         patch_kernel,
-        grid=(1,),
-        in_specs=[
-            pl.BlockSpec(late_p.shape, lambda i: (0, 0, 0)),
-            pl.BlockSpec(late_lg.shape, lambda i: (0, 0, 0)),
-            pl.BlockSpec(fix.shape, lambda i: (0, 0)),
-        ]
-        + edges,
-        out_specs=edges,
+        in_specs=[vmem] * 7,
+        out_specs=[vmem] * 4,
         out_shape=[jax.ShapeDtypeStruct(o.shape, o.dtype) for o in outs],
-        input_output_aliases={3: 0, 4: 1, 5: 2, 6: 3},
         compiler_params=SMALL,
         name="patch",
     )(late_p, late_lg, fix, *outs)
@@ -291,11 +314,11 @@
     for h in range(4):
         for d in range(groups):
             for half in range(2):
-                tile = gathered_ref[h * 16 + d * 2 + half, 0:8].reshape(8, TILE)
+                tile = gathered_ref[seat(h, d, half), 0:8].reshape(8, TILE)
                 start = (d * 4 + h) * TILE
                 filter_ref[8 * half : 8 * half + 8, start : start + TILE] = tile * scale
         for g in range(9):
-            row = gathered_ref[h * 16 + g, 8] * scale
+            row = gathered_ref[seat(h, g // 2, g % 2), 8] * scale
             short_ref[g : g + 1, h * TILE : (h + 1) * TILE] = row
 
 
@@ -306,15 +329,19 @@
         pairs = [(i, i + by) for i in range(peers) if 0 <= i + by < peers]
         return lax.ppermute(value, "ctx", pairs)
 
-    right, left = pack(q_stream, k_stream, v_stream, cotangent)
-    before = shifted(right, 1)
-    after = shifted(left, -1)
+    place = lax.axis_index("ctx").astype(jnp.int32).reshape(1)
+    far, near = pack(place, q_stream, k_stream, v_stream, cotangent)
+    far = lax.ppermute(
+        far, "ctx", [(i, i + 1 if i % 2 else i - 1) for i in range(1, peers - 1)]
+    )
+    near = lax.ppermute(near, "ctx", [(i, i ^ 1) for i in range(peers)])
     taps = lax.all_to_all(filter_taps, "dp", split_axis=1, concat_axis=0, tiled=True)
 
     *outs, part, fix, late = run_layer(
+        place,
         (q_stream, k_stream, v_stream, cotangent),
-        before,
-        after,
+        far,
+        near,
         taps,
         short_taps,
         matrices,
@@ -335,7 +362,7 @@
     )(part)
 
     pairs = [
-        (d * peers + h * 16 + e * 2 + half, e * peers + h * 16 + d * 2 + half)
+        (d * peers + seat(h, e, half), e * peers + seat(h, d, half))
         for d in range(groups)
         for h in range(4)
         for e in range(groups)

time: 85.1 us -> 83.4 us (0.980)
  starting transfers between devices: 35.4 us -> 29.5 us
  waiting for transfers between devices: 10.3 us -> 14.6 us
  Pallas kernels: 6.89 us -> 5.95 us
  blocking collectives: 29.4 us -> 30.3 us
    all_to_all x1, starting transfers between devices: 14.9 us -> 5.42 us  [on_device(): lax.all_to_all(sent, 'ctx', split_axis=0, concat_axis=0, tiled=True)]
    ppermute x4 -> x2, starting transfers between devices: 12.1 us -> 5.46 us  [shifted(): return lax.ppermute(value, 'ctx', pairs)]
    ppermute x0 -> x2, starting transfers between devices: none -> 6.01 us  [the longest x1 4.09 us: on_device(): lax.ppermute(far, 'ctx', [(i, i + 1 if i % 2 else i - 1) for i in range(1...]
    ppermute x1, starting transfers between devices: 0.66 us -> 4.84 us  [on_device(): tile = lax.ppermute(tile, ('dp', 'ctx'), pairs)]
    ppermute x1, waiting for transfers between devices: 0.01 us -> 3.98 us  [on_device(): tile = lax.ppermute(tile, ('dp', 'ctx'), pairs)]
    ppermute x4 -> x2, waiting for transfers between devices: 6.74 us -> 3.27 us  [shifted(): return lax.ppermute(value, 'ctx', pairs)]
    ppermute x0 -> x2, waiting for transfers between devices: none -> 2.76 us  [the longest x1 2.76 us: on_device(): lax.ppermute(far, 'ctx', [(i, i + 1 if i % 2 else i - 1) for i in range(1...]
    pallas_call x3, Pallas kernels: 4.88 us -> 3.95 us  [the longest x1 3.08 us: run_layer(): pl.pallas_call(layer_kernel, in_specs=[pl.BlockSpec(memory_space=pltpu.SM...]
  transfers between devices with their start and end apart: 7 -> 7, of which waited for: 3 -> 5; matrix products, arithmetic and copies ran while one was open for 0% -> 0% of each run, Pallas kernels for 2% -> 1%
where the time goes in v5:
time: 83.4 us; the launch traced here: 82.9 us
  blocking collectives  30.3 us (36%)
  starting transfers between devices  29.5 us (35%)
  waiting for transfers between devices  14.6 us (18%)
  Pallas kernels  5.95 us (7%)
  local copies, waits for them, and re-layouts  1.75 us (2%)
    all_to_all x1, blocking collectives, on_device(): part = lax.all_to_all(part, 'ctx', split_axis=0, concat_axis=0, tiled=True)  30.3 us
    all_to_all x1, starting transfers between devices, on_device(): lax.all_to_all(filter_taps, 'dp', split_axis=1, concat_axis=0, tiled=True)  7.79 us
    ppermute x2, starting transfers between devices, shifted(): return lax.ppermute(value, 'ctx', pairs)  5.46 us
    all_to_all x1, starting transfers between devices, on_device(): lax.all_to_all(sent, 'ctx', split_axis=0, concat_axis=0, tiled=True)  5.42 us
    ppermute x1, starting transfers between devices, on_device(): tile = lax.ppermute(tile, ('dp', 'ctx'), pairs)  4.84 us
    all_to_all x1, waiting for transfers between devices, on_device(): lax.all_to_all(sent, 'ctx', split_axis=0, concat_axis=0, tiled=True)  4.15 us
    ppermute x1, starting transfers between devices, on_device(): lax.ppermute(far, 'ctx', [(i, i + 1 if i % 2 else i - 1) for i in range(1...  4.09 us
    ppermute x1, waiting for transfers between devices, on_device(): tile = lax.ppermute(tile, ('dp', 'ctx'), pairs)  3.98 us
  transfers between devices with their start and end apart: 7, of which 5 were waited for; matrix products, arithmetic and copies ran while one was open for 0% of the time, Pallas kernels for 1%

profile of v5, /device:TPU:1, one launch (start us, length us, event | category | flops | bytes accessed | tf_op | source)
XLA Modules:
  0.0 82.9 jit_solution(3534082877801110205)
XLA Ops:
  0.6 0.0 copy-start.6
  0.6 1.7 %copy.18 = f32[2,8,8,512]{3,2,0,1:T(8,128)} copy(f32[2,8,8,512]{3,2,1,0:T(8,128)} %bitcast.9) | data formatting | bytes 524288 | tf_op jit(solution)/shard_map/all_to_all | solution.py:338
  2.4 0.0 copy-start
  2.4 0.0 copy-start.1
  2.4 0.0 copy-start.2
  2.4 0.0 copy-start.3
  2.4 7.8 %all-to-all-start = ((f32[16,8,512]{2,0,1:T(8,128)}), f32[16,8,512]{2,0,1:T(8,128)S(1)}, u32[]{:S(2)}, u32[]{:S(2)}) async-start(f32[16,8,512]{2,0,1:T(8,128)} %bitcast.7), calls=%async_computation | async-start | bytes 524288 | tf_op jit(solution)/shard_map/all_to_all | solution.py:338
  10.2 0.0 copy-done
  10.2 0.0 copy-done.1
  10.2 0.0 copy-done.2
  10.2 0.0 copy-done.3
  10.2 0.0 copy-start.4
  10.2 0.0 copy-start.5
  10.2 0.0 copy-start.7
  10.2 0.1 pack.1
  10.3 4.1 %collective-permute-start = (bf16[288,512]{1,0:T(8,128)(2,1)S(1)}, bf16[288,512]{1,0:T(8,128)(2,1)S(1)}, u32[]{:S(2)}, u32[]{:S(2)}) collective-permute-start(bf16[288,512]{1,0:T(8,128)(2,1)S(1)} %get-tuple-element.26), channel_id=1, source_target_pairs={{1,2},{2,1},{3,4},{4,3},{5,6},{6,5},{7,8},{8,7},{9,10},{10,9},{11,... | collective-permute-start | bytes 884744 | tf_op jit(solution)/shard_map/ppermute | solution.py:334
  14.4 1.9 %collective-permute-start.1 = (bf16[288,512]{1,0:T(8,128)(2,1)S(1)}, bf16[288,512]{1,0:T(8,128)(2,1)S(1)}, u32[]{:S(2)}, u32[]{:S(2)}) collective-permute-start(bf16[288,512]{1,0:T(8,128)(2,1)S(1)} %get-tuple-element.27), channel_id=1, source_target_pairs={{0,1},{1,0},{2,3},{3,2},{4,5},{5,4},{6,7},{7,6},{8,9},{9,8},{10,11... | collective-permute-start | bytes 884744 | tf_op jit(solution)/shard_map/ppermute | solution.py:337
  16.3 2.8 %collective-permute-done.far_ref = bf16[288,512]{1,0:T(8,128)(2,1)S(1)} collective-permute-done((bf16[288,512]{1,0:T(8,128)(2,1)S(1)}, bf16[288,512]{1,0:T(8,128)(2,1)S(1)}, u32[]{:S(2)}, u32[]{:S(2)}) %collective-permute-start) | collective-permute-done | bytes 294944 | tf_op jit(solution)/shard_map/ppermute | solution.py:334
  19.1 0.0 collective-permute-done.1.near_ref
  19.1 0.5 all-to-all-done
  19.6 0.0 copy-done.6
  19.6 0.0 copy-done.4
  19.6 0.0 copy-done.5
  19.6 0.0 copy-done.7
  19.6 3.1 %layer.1 = (bf16[128,512]{1,0:T(8,128)(2,1)S(1)}, bf16[128,512]{1,0:T(8,128)(2,1)S(1)}, bf16[128,512]{1,0:T(8,128)(2,1)S(1)}, bf16[128,512]{1,0:T(8,128)(2,1)S(1...) custom-call(s32[1]{0:T(128)} %bitcast.place_ref, bf16[128,512]{1,0:T(8,128)(2,1)S(1)} %copy-done, ...), custom_call_target="tpu_custom_call" | custom-call | tf_op jit(solution)/shard_map/layer/pallas_call | solution.py:249
  22.7 30.3 %all_to_all.29.part_ref = f32[64,9,1,128]{3,2,1,0:T(1,128)S(1)} all-to-all(f32[64,9,1,128]{3,2,1,0:T(1,128)S(1)} %get-tuple-element.28), channel_id=1, replica_groups=mesh['dp'=8,'ctx'=64] {'ctx'}, dimensions={0} | all-to-all | bytes 589824 | tf_op jit(solution)/shard_map/all_to_all | solution.py:350
  52.9 0.2 sum.1
  53.2 4.8 %collective-permute-start.2 = (f32[8,1,128]{2,1,0:T(1,128)S(1)}, f32[8,1,128]{2,1,0:T(1,128)S(1)}, u32[]{:S(2)}, u32[]{:S(2)}) collective-permute-start(f32[8,1,128]{2,1,0:T(1,128)S(1)} %get-tuple-element.29), channel_id=1, source_target_pairs={{0,0},{8,8},{2,64},{10,72},{4,128},{12,136},{6,192},{14,200},{1,25... | collective-permute-start | bytes 12296 | tf_op jit(solution)/shard_map/ppermute | solution.py:371
  58.0 4.0 %collective-permute-done.2.tile_ref = f32[8,1,128]{2,1,0:T(1,128)S(1)} collective-permute-done((f32[8,1,128]{2,1,0:T(1,128)S(1)}, f32[8,1,128]{2,1,0:T(1,128)S(1)}, u32[]{:S(2)}, u32[]{:S(2)}) %collective-permute-start.2) | collective-permute-done | bytes 4128 | tf_op jit(solution)/shard_map/ppermute | solution.py:371
  62.0 0.9 %spread.1 = (f32[64,9,1,128]{3,2,1,0:T(1,128)}, f32[1,1,512]{2,1,0:T(1,128)S(1)}, f32[1,1,512]{2,1,0:T(1,128)S(1)}) custom-call(f32[8,1,128]{2,1,0:T(1,128)S(1)} %collective-permute-done.2.tile_ref, f32[1,1,128]{2,1,0:T(1,128)S(1)} %get-tuple-element.30.short_ref, f32[2,1,512]{2,1,0:T(1,128)S(1)} %get-tuple-element.31.late_ref), custom_call_target="tpu_custom_call" | custom-call | tf_op jit(solution)/shard_map/spread/pallas_call | solution.py:373
  62.9 5.4 %all-to-all-start.2 = ((f32[64,9,1,128]{3,2,1,0:T(1,128)}), f32[64,9,1,128]{3,2,1,0:T(1,128)S(1)}, u32[]{:S(2)}, u32[]{:S(2)}) async-start(f32[64,9,1,128]{3,2,1,0:T(1,128)} %get-tuple-element.43), calls=%async_computation.2 | async-start | bytes 589824 | tf_op jit(solution)/shard_map/all_to_all | solution.py:380
  68.3 3.5 %collective-permute-start.3 = (f32[1,1,512]{2,1,0:T(1,128)S(1)}, f32[1,1,512]{2,1,0:T(1,128)S(1)}, u32[]{:S(2)}, u32[]{:S(2)}) collective-permute-start(f32[1,1,512]{2,1,0:T(1,128)S(1)} %get-tuple-element.32), channel_id=1, source_target_pairs={{0,1},{1,2},{2,3},{3,4},{4,5},{5,6},{6,7},{7,8},{8,9},{9,10},{10,1... | collective-permute-start | bytes 6152 | tf_op jit(solution)/shard_map/ppermute | solution.py:330
  71.8 1.9 %collective-permute-start.4 = (f32[1,1,512]{2,1,0:T(1,128)S(1)}, f32[1,1,512]{2,1,0:T(1,128)S(1)}, u32[]{:S(2)}, u32[]{:S(2)}) collective-permute-start(f32[1,1,512]{2,1,0:T(1,128)S(1)} %get-tuple-element.33), channel_id=1, source_target_pairs={{1,0},{2,1},{3,2},{4,3},{5,4},{6,5},{7,6},{8,7},{9,8},{10,9},{11,1... | collective-permute-start | bytes 6152 | tf_op jit(solution)/shard_map/ppermute | solution.py:330
  73.8 0.0 collective-permute-done.3.p_ref
  73.8 3.3 %collective-permute-done.4.lg_ref = f32[1,1,512]{2,1,0:T(1,128)S(1)} collective-permute-done((f32[1,1,512]{2,1,0:T(1,128)S(1)}, f32[1,1,512]{2,1,0:T(1,128)S(1)}, u32[]{:S(2)}, u32[]{:S(2)}) %collective-permute-start.4) | collective-permute-done | bytes 2080 | tf_op jit(solution)/shard_map/ppermute | solution.py:330
  77.0 0.8 patch.1
  77.9 4.1 %all-to-all-done.2.gathered_ref = f32[64,9,1,128]{3,2,1,0:T(1,128)S(1)} async-done(((f32[64,9,1,128]{3,2,1,0:T(1,128)}), f32[64,9,1,128]{3,2,1,0:T(1,128)S(1)}, u32[]{:S(2)}, u32[]{:S(2)}) %all-to-all-start.2) | async-done | bytes 294944 | tf_op jit(solution)/shard_map/all_to_all | solution.py:380
  82.0 0.9 %final.1 = (f32[16,4096]{1,0:T(8,128)}, f32[9,512]{1,0:T(8,128)}) custom-call(f32[64,9,1,128]{3,2,1,0:T(1,128)S(1)} %all-to-all-done.2.gathered_ref), custom_call_target="tpu_custom_call" | custom-call | tf_op jit(solution)/shard_map/final/pallas_call | solution.py:382
Async XLA Ops:
  0.6 18.9 %copy-start.6 = (bf16[2,136,256]{2,1,0:T(8,128)(2,1)S(1)}, bf16[2,136,256]{2,1,0:T(8,128)(2,1)}, u32[]{:S(2)}) copy-start(bf16[2,136,256]{2,1,0:T(8,128)(2,1)} %constant.11.clone.long_ref) | copy-start | bytes 417796
  2.4 7.8 %copy-start = (bf16[128,512]{1,0:T(8,128)(2,1)S(1)}, bf16[128,512]{1,0:T(8,128)(2,1)}, u32[]{:S(2)}) copy-start(bf16[128,512]{1,0:T(8,128)(2,1)} %q_ref.3) | copy-start | bytes 393220
  2.4 7.8 %copy-start.1 = (bf16[128,512]{1,0:T(8,128)(2,1)S(1)}, bf16[128,512]{1,0:T(8,128)(2,1)}, u32[]{:S(2)}) copy-start(bf16[128,512]{1,0:T(8,128)(2,1)} %k_ref.3) | copy-start | bytes 393220
  2.4 7.8 %copy-start.2 = (bf16[128,512]{1,0:T(8,128)(2,1)S(1)}, bf16[128,512]{1,0:T(8,128)(2,1)}, u32[]{:S(2)}) copy-start(bf16[128,512]{1,0:T(8,128)(2,1)} %v_ref.3) | copy-start | bytes 393220
  2.4 7.8 %copy-start.3 = (bf16[128,512]{1,0:T(8,128)(2,1)S(1)}, bf16[128,512]{1,0:T(8,128)(2,1)}, u32[]{:S(2)}) copy-start(bf16[128,512]{1,0:T(8,128)(2,1)} %c_ref.3) | copy-start | bytes 393220
  2.4 17.2 %all-to-all-start = ((f32[16,8,512]{2,0,1:T(8,128)}), f32[16,8,512]{2,0,1:T(8,128)S(1)}, u32[]{:S(2)}, u32[]{:S(2)}) async-start(f32[16,8,512]{2,0,1:T(8,128)} %bitcast.7), calls=%async_computation | async-start | bytes 524288 | tf_op jit(solution)/shard_map/all_to_all | solution.py:338
  10.2 9.4 %copy-start.4 = (bf16[2,256,256]{2,1,0:T(8,128)(2,1)S(1)}, bf16[2,256,256]{2,1,0:T(8,128)(2,1)}, u32[]{:S(2)}) copy-start(bf16[2,256,256]{2,1,0:T(8,128)(2,1)} %constant.10.clone.fwd_ref) | copy-start | bytes 786436
  10.2 9.4 %copy-start.5 = (bf16[2,136,256]{2,1,0:T(8,128)(2,1)S(1)}, bf16[2,136,256]{2,1,0:T(8,128)(2,1)}, u32[]{:S(2)}) copy-start(bf16[2,136,256]{2,1,0:T(8,128)(2,1)} %constant.12.clone.grad_ref) | copy-start | bytes 417796
  10.2 9.4 %copy-start.7 = (f32[9,512]{1,0:T(8,128)S(1)}, f32[9,512]{1,0:T(8,128)}, u32[]{:S(2)}) copy-start(f32[9,512]{1,0:T(8,128)} %s_ref.1) | copy-start | bytes 55300
  10.3 8.8 %collective-permute-start = (bf16[288,512]{1,0:T(8,128)(2,1)S(1)}, bf16[288,512]{1,0:T(8,128)(2,1)S(1)}, u32[]{:S(2)}, u32[]{:S(2)}) collective-permute-start(bf16[288,512]{1,0:T(8,128)(2,1)S(1)} %get-tuple-element.26), channel_id=1, source_target_pairs={{1,2},{2,1},{3,4},{4,3},{5,6},{6,5},{7,8},{8,7},{9,10},{10,9},{11,... | collective-permute-start | bytes 884744 | tf_op jit(solution)/shard_map/ppermute | solution.py:334
  14.4 4.7 %collective-permute-start.1 = (bf16[288,512]{1,0:T(8,128)(2,1)S(1)}, bf16[288,512]{1,0:T(8,128)(2,1)S(1)}, u32[]{:S(2)}, u32[]{:S(2)}) collective-permute-start(bf16[288,512]{1,0:T(8,128)(2,1)S(1)} %get-tuple-element.27), channel_id=1, source_target_pairs={{0,1},{1,0},{2,3},{3,2},{4,5},{5,4},{6,7},{7,6},{8,9},{9,8},{10,11... | collective-permute-start | bytes 884744 | tf_op jit(solution)/shard_map/ppermute | solution.py:337
  53.2 8.8 %collective-permute-start.2 = (f32[8,1,128]{2,1,0:T(1,128)S(1)}, f32[8,1,128]{2,1,0:T(1,128)S(1)}, u32[]{:S(2)}, u32[]{:S(2)}) collective-permute-start(f32[8,1,128]{2,1,0:T(1,128)S(1)} %get-tuple-element.29), channel_id=1, source_target_pairs={{0,0},{8,8},{2,64},{10,72},{4,128},{12,136},{6,192},{14,200},{1,25... | collective-permute-start | bytes 12296 | tf_op jit(solution)/shard_map/ppermute | solution.py:371
  62.9 19.1 %all-to-all-start.2 = ((f32[64,9,1,128]{3,2,1,0:T(1,128)}), f32[64,9,1,128]{3,2,1,0:T(1,128)S(1)}, u32[]{:S(2)}, u32[]{:S(2)}) async-start(f32[64,9,1,128]{3,2,1,0:T(1,128)} %get-tuple-element.43), calls=%async_computation.2 | async-start | bytes 589824 | tf_op jit(solution)/shard_map/all_to_all | solution.py:380
  68.3 5.5 %collective-permute-start.3 = (f32[1,1,512]{2,1,0:T(1,128)S(1)}, f32[1,1,512]{2,1,0:T(1,128)S(1)}, u32[]{:S(2)}, u32[]{:S(2)}) collective-permute-start(f32[1,1,512]{2,1,0:T(1,128)S(1)} %get-tuple-element.32), channel_id=1, source_target_pairs={{0,1},{1,2},{2,3},{3,4},{4,5},{5,6},{6,7},{7,8},{8,9},{9,10},{10,1... | collective-permute-start | bytes 6152 | tf_op jit(solution)/shard_map/ppermute | solution.py:330
  71.8 5.2 %collective-permute-start.4 = (f32[1,1,512]{2,1,0:T(1,128)S(1)}, f32[1,1,512]{2,1,0:T(1,128)S(1)}, u32[]{:S(2)}, u32[]{:S(2)}) collective-permute-start(f32[1,1,512]{2,1,0:T(1,128)S(1)} %get-tuple-element.33), channel_id=1, source_target_pairs={{1,0},{2,1},{3,2},{4,3},{5,4},{6,5},{7,6},{8,7},{9,8},{10,9},{11,1... | collective-permute-start | bytes 6152 | tf_op jit(solution)/shard_map/ppermute | solution.py:330

commit v6 on v5

--- a/solution.py
+++ b/solution.py
@@ -29,7 +29,7 @@
 def two_parts(matrix):
     high = matrix.astype(ml_dtypes.bfloat16)
     low = (matrix - high.astype(np.float64)).astype(ml_dtypes.bfloat16)
-    return np.stack([high, low])
+    return np.concatenate([high, low, high], 1)
 
 
 def transform_matrices():
@@ -56,10 +56,10 @@
     return high, low
 
 
-def dot3(matrix_high, matrix_low, value):
+def dot3(matrix, value):
     high, low = split(value)
-    dot = functools.partial(jnp.dot, preferred_element_type=F32)
-    return dot(matrix_high, high) + (dot(matrix_high, low) + dot(matrix_low, high))
+    parts = jnp.concatenate([high, high, low], 0)
+    return jnp.dot(matrix, parts, preferred_element_type=F32)
 
 
 def pack_kernel(place_ref, q_ref, k_ref, v_ref, c_ref, far_ref, near_ref):
@@ -118,8 +118,7 @@
         return x.astype(F32)
 
     odd = lax.rem(place_ref[0], 2) == 1
-    fh, fl = fwd_ref[0], fwd_ref[1]
-    fh_half, fl_half = fh[:, 0:HALF], fl[:, 0:HALF]
+    half = jnp.concatenate([fwd_ref[:, PERIOD * n : PERIOD * n + HALF] for n in range(3)], 1)
     freq = lax.broadcasted_iota(jnp.int32, (HALF, WIDE), 0)
     sign = jnp.where(freq % 2 == 0, 1.0, -1.0).astype(F32)
     row = lax.broadcasted_iota(jnp.int32, (8, WIDE), 0)
@@ -178,16 +177,16 @@
         lg = jnp.concatenate([cot, cot_next], 0) * a0
 
         taps = h_ref[:, cols]
-        own_f = dot3(fh_half, fl_half, p_own)
-        before_f = dot3(fh_half, fl_half, p_before)
+        own_f = dot3(half, p_own)
+        before_f = dot3(half, p_before)
         moved_f = jnp.concatenate([own_f[HALF:] * sign, own_f[0:HALF] * -sign], 0)
         x_f = before_f + moved_f
-        lg_f = dot3(fh, fl, lg)
-        h_f = dot3(fh_half, fl_half, taps)
-
-        long = dot3(long_ref[0], long_ref[1], times(x_f, h_f))
-        pg = dot3(grad_ref[0], grad_ref[1], times_conj(lg_f, h_f))
-        filt = dot3(grad_ref[0, 0:ROWS], grad_ref[1, 0:ROWS], times_conj(lg_f, own_f))
+        lg_f = dot3(fwd_ref[...], lg)
+        h_f = dot3(half, taps)
+
+        long = dot3(long_ref[...], times(x_f, h_f))
+        pg = dot3(grad_ref[...], times_conj(lg_f, h_f))
+        filt = dot3(grad_ref[0:ROWS], times_conj(lg_f, own_f))
 
         h0, h1, h127 = taps[0:1], taps[1:2], taps[127:128]
         p0, p1 = p_far[0:1], p_far[1:2]

time: 83.4 us -> 83.1 us (level)
  no operation moved by 1% of the time
where the time goes in v6:
time: 83.1 us; the launch traced here: 82.6 us
  blocking collectives  30.3 us (36%)
  starting transfers between devices  29.5 us (35%)
  waiting for transfers between devices  14.7 us (18%)
  Pallas kernels  5.61 us (7%)
  local copies, waits for them, and re-layouts  1.76 us (2%)
    all_to_all x1, blocking collectives, on_device(): part = lax.all_to_all(part, 'ctx', split_axis=0, concat_axis=0, tiled=True)  30.3 us
    all_to_all x1, starting transfers between devices, on_device(): lax.all_to_all(filter_taps, 'dp', split_axis=1, concat_axis=0, tiled=True)  7.79 us
    ppermute x2, starting transfers between devices, shifted(): return lax.ppermute(value, 'ctx', pairs)  5.46 us
    all_to_all x1, starting transfers between devices, on_device(): lax.all_to_all(sent, 'ctx', split_axis=0, concat_axis=0, tiled=True)  5.42 us
    ppermute x1, starting transfers between devices, on_device(): tile = lax.ppermute(tile, ('dp', 'ctx'), pairs)  4.82 us
    all_to_all x1, waiting for transfers between devices, on_device(): lax.all_to_all(sent, 'ctx', split_axis=0, concat_axis=0, tiled=True)  4.15 us
    ppermute x1, starting transfers between devices, on_device(): lax.ppermute(far, 'ctx', [(i, i + 1 if i % 2 else i - 1) for i in range(1...  4.09 us
    ppermute x1, waiting for transfers between devices, on_device(): tile = lax.ppermute(tile, ('dp', 'ctx'), pairs)  4 us
  transfers between devices with their start and end apart: 7, of which 5 were waited for; matrix products, arithmetic and copies ran while one was open for 0% of the time, Pallas kernels for 1%

profile of v6, /device:TPU:1, one launch (start us, length us, event | category | flops | bytes accessed | tf_op | source)
XLA Modules:
  0.0 82.6 jit_solution(2855831337152656673)
XLA Ops:
  0.6 0.0 copy-start.5
  0.6 0.0 copy-start.6
  0.7 1.7 %copy.18 = f32[2,8,8,512]{3,2,0,1:T(8,128)} copy(f32[2,8,8,512]{3,2,1,0:T(8,128)} %bitcast.9) | data formatting | bytes 524288 | tf_op jit(solution)/shard_map/all_to_all | solution.py:337
  2.4 0.0 copy-start
  2.4 0.0 copy-start.1
  2.4 0.0 copy-start.2
  2.4 0.0 copy-start.3
  2.4 7.8 %all-to-all-start = ((f32[16,8,512]{2,0,1:T(8,128)}), f32[16,8,512]{2,0,1:T(8,128)S(1)}, u32[]{:S(2)}, u32[]{:S(2)}) async-start(f32[16,8,512]{2,0,1:T(8,128)} %bitcast.7), calls=%async_computation | async-start | bytes 524288 | tf_op jit(solution)/shard_map/all_to_all | solution.py:337
  10.2 0.0 copy-start.4
  10.2 0.0 copy-done
  10.2 0.0 copy-done.1
  10.2 0.0 copy-done.2
  10.2 0.0 copy-done.3
  10.2 0.0 copy-start.7
  10.2 0.1 pack.1
  10.3 4.1 %collective-permute-start = (bf16[288,512]{1,0:T(8,128)(2,1)S(1)}, bf16[288,512]{1,0:T(8,128)(2,1)S(1)}, u32[]{:S(2)}, u32[]{:S(2)}) collective-permute-start(bf16[288,512]{1,0:T(8,128)(2,1)S(1)} %get-tuple-element.26), channel_id=1, source_target_pairs={{1,2},{2,1},{3,4},{4,3},{5,6},{6,5},{7,8},{8,7},{9,10},{10,9},{11,... | collective-permute-start | bytes 884744 | tf_op jit(solution)/shard_map/ppermute | solution.py:333
  14.4 1.9 %collective-permute-start.1 = (bf16[288,512]{1,0:T(8,128)(2,1)S(1)}, bf16[288,512]{1,0:T(8,128)(2,1)S(1)}, u32[]{:S(2)}, u32[]{:S(2)}) collective-permute-start(bf16[288,512]{1,0:T(8,128)(2,1)S(1)} %get-tuple-element.27), channel_id=1, source_target_pairs={{0,1},{1,0},{2,3},{3,2},{4,5},{5,4},{6,7},{7,6},{8,9},{9,8},{10,11... | collective-permute-start | bytes 884744 | tf_op jit(solution)/shard_map/ppermute | solution.py:336
  16.3 2.8 %collective-permute-done.far_ref = bf16[288,512]{1,0:T(8,128)(2,1)S(1)} collective-permute-done((bf16[288,512]{1,0:T(8,128)(2,1)S(1)}, bf16[288,512]{1,0:T(8,128)(2,1)S(1)}, u32[]{:S(2)}, u32[]{:S(2)}) %collective-permute-start) | collective-permute-done | bytes 294944 | tf_op jit(solution)/shard_map/ppermute | solution.py:333
  19.1 0.0 collective-permute-done.1.near_ref
  19.1 0.5 all-to-all-done
  19.6 0.0 copy-done.5
  19.6 0.0 copy-done.6
  19.6 0.0 copy-done.4
  19.6 0.0 copy-done.7
  19.6 2.7 %layer.1 = (bf16[128,512]{1,0:T(8,128)(2,1)S(1)}, bf16[128,512]{1,0:T(8,128)(2,1)S(1)}, bf16[128,512]{1,0:T(8,128)(2,1)S(1)}, bf16[128,512]{1,0:T(8,128)(2,1)S(1...) custom-call(s32[1]{0:T(128)} %bitcast.place_ref, bf16[128,512]{1,0:T(8,128)(2,1)S(1)} %copy-done, ...), custom_call_target="tpu_custom_call" | custom-call | tf_op jit(solution)/shard_map/layer/pallas_call | solution.py:248
  22.4 30.3 %all_to_all.29.part_ref = f32[64,9,1,128]{3,2,1,0:T(1,128)S(1)} all-to-all(f32[64,9,1,128]{3,2,1,0:T(1,128)S(1)} %get-tuple-element.28), channel_id=1, replica_groups=mesh['dp'=8,'ctx'=64] {'ctx'}, dimensions={0} | all-to-all | bytes 589824 | tf_op jit(solution)/shard_map/all_to_all | solution.py:349
  52.6 0.2 sum.1
  52.9 4.8 %collective-permute-start.2 = (f32[8,1,128]{2,1,0:T(1,128)S(1)}, f32[8,1,128]{2,1,0:T(1,128)S(1)}, u32[]{:S(2)}, u32[]{:S(2)}) collective-permute-start(f32[8,1,128]{2,1,0:T(1,128)S(1)} %get-tuple-element.29), channel_id=1, source_target_pairs={{0,0},{8,8},{2,64},{10,72},{4,128},{12,136},{6,192},{14,200},{1,25... | collective-permute-start | bytes 12296 | tf_op jit(solution)/shard_map/ppermute | solution.py:370
  57.7 4.0 %collective-permute-done.2.tile_ref = f32[8,1,128]{2,1,0:T(1,128)S(1)} collective-permute-done((f32[8,1,128]{2,1,0:T(1,128)S(1)}, f32[8,1,128]{2,1,0:T(1,128)S(1)}, u32[]{:S(2)}, u32[]{:S(2)}) %collective-permute-start.2) | collective-permute-done | bytes 4128 | tf_op jit(solution)/shard_map/ppermute | solution.py:370
  61.7 0.9 %spread.1 = (f32[64,9,1,128]{3,2,1,0:T(1,128)}, f32[1,1,512]{2,1,0:T(1,128)S(1)}, f32[1,1,512]{2,1,0:T(1,128)S(1)}) custom-call(f32[8,1,128]{2,1,0:T(1,128)S(1)} %collective-permute-done.2.tile_ref, f32[1,1,128]{2,1,0:T(1,128)S(1)} %get-tuple-element.30.short_ref, f32[2,1,512]{2,1,0:T(1,128)S(1)} %get-tuple-element.31.late_ref), custom_call_target="tpu_custom_call" | custom-call | tf_op jit(solution)/shard_map/spread/pallas_call | solution.py:372
  62.6 5.4 %all-to-all-start.2 = ((f32[64,9,1,128]{3,2,1,0:T(1,128)}), f32[64,9,1,128]{3,2,1,0:T(1,128)S(1)}, u32[]{:S(2)}, u32[]{:S(2)}) async-start(f32[64,9,1,128]{3,2,1,0:T(1,128)} %get-tuple-element.43), calls=%async_computation.2 | async-start | bytes 589824 | tf_op jit(solution)/shard_map/all_to_all | solution.py:379
  68.0 3.5 %collective-permute-start.3 = (f32[1,1,512]{2,1,0:T(1,128)S(1)}, f32[1,1,512]{2,1,0:T(1,128)S(1)}, u32[]{:S(2)}, u32[]{:S(2)}) collective-permute-start(f32[1,1,512]{2,1,0:T(1,128)S(1)} %get-tuple-element.32), channel_id=1, source_target_pairs={{0,1},{1,2},{2,3},{3,4},{4,5},{5,6},{6,7},{7,8},{8,9},{9,10},{10,1... | collective-permute-start | bytes 6152 | tf_op jit(solution)/shard_map/ppermute | solution.py:329
  71.5 1.9 %collective-permute-start.4 = (f32[1,1,512]{2,1,0:T(1,128)S(1)}, f32[1,1,512]{2,1,0:T(1,128)S(1)}, u32[]{:S(2)}, u32[]{:S(2)}) collective-permute-start(f32[1,1,512]{2,1,0:T(1,128)S(1)} %get-tuple-element.33), channel_id=1, source_target_pairs={{1,0},{2,1},{3,2},{4,3},{5,4},{6,5},{7,6},{8,7},{9,8},{10,9},{11,1... | collective-permute-start | bytes 6152 | tf_op jit(solution)/shard_map/ppermute | solution.py:329
  73.5 0.0 collective-permute-done.3.p_ref
  73.5 3.3 %collective-permute-done.4.lg_ref = f32[1,1,512]{2,1,0:T(1,128)S(1)} collective-permute-done((f32[1,1,512]{2,1,0:T(1,128)S(1)}, f32[1,1,512]{2,1,0:T(1,128)S(1)}, u32[]{:S(2)}, u32[]{:S(2)}) %collective-permute-start.4) | collective-permute-done | bytes 2080 | tf_op jit(solution)/shard_map/ppermute | solution.py:329
  76.7 0.8 patch.1
  77.6 4.1 %all-to-all-done.2.gathered_ref = f32[64,9,1,128]{3,2,1,0:T(1,128)S(1)} async-done(((f32[64,9,1,128]{3,2,1,0:T(1,128)}), f32[64,9,1,128]{3,2,1,0:T(1,128)S(1)}, u32[]{:S(2)}, u32[]{:S(2)}) %all-to-all-start.2) | async-done | bytes 294944 | tf_op jit(solution)/shard_map/all_to_all | solution.py:379
  81.7 0.9 %final.1 = (f32[16,4096]{1,0:T(8,128)}, f32[9,512]{1,0:T(8,128)}) custom-call(f32[64,9,1,128]{3,2,1,0:T(1,128)S(1)} %all-to-all-done.2.gathered_ref), custom_call_target="tpu_custom_call" | custom-call | tf_op jit(solution)/shard_map/final/pallas_call | solution.py:381
Async XLA Ops:
  0.6 19.0 %copy-start.5 = (bf16[136,768]{1,0:T(8,128)(2,1)S(1)}, bf16[136,768]{1,0:T(8,128)(2,1)}, u32[]{:S(2)}) copy-start(bf16[136,768]{1,0:T(8,128)(2,1)} %constant.12.clone.grad_ref) | copy-start | bytes 626692
  0.6 19.0 %copy-start.6 = (bf16[136,768]{1,0:T(8,128)(2,1)S(1)}, bf16[136,768]{1,0:T(8,128)(2,1)}, u32[]{:S(2)}) copy-start(bf16[136,768]{1,0:T(8,128)(2,1)} %constant.11.clone.long_ref) | copy-start | bytes 626692
  2.4 7.8 %copy-start = (bf16[128,512]{1,0:T(8,128)(2,1)S(1)}, bf16[128,512]{1,0:T(8,128)(2,1)}, u32[]{:S(2)}) copy-start(bf16[128,512]{1,0:T(8,128)(2,1)} %q_ref.3) | copy-start | bytes 393220
  2.4 7.8 %copy-start.1 = (bf16[128,512]{1,0:T(8,128)(2,1)S(1)}, bf16[128,512]{1,0:T(8,128)(2,1)}, u32[]{:S(2)}) copy-start(bf16[128,512]{1,0:T(8,128)(2,1)} %k_ref.3) | copy-start | bytes 393220
  2.4 7.8 %copy-start.2 = (bf16[128,512]{1,0:T(8,128)(2,1)S(1)}, bf16[128,512]{1,0:T(8,128)(2,1)}, u32[]{:S(2)}) copy-start(bf16[128,512]{1,0:T(8,128)(2,1)} %v_ref.3) | copy-start | bytes 393220
  2.4 7.8 %copy-start.3 = (bf16[128,512]{1,0:T(8,128)(2,1)S(1)}, bf16[128,512]{1,0:T(8,128)(2,1)}, u32[]{:S(2)}) copy-start(bf16[128,512]{1,0:T(8,128)(2,1)} %c_ref.3) | copy-start | bytes 393220
  2.4 17.2 %all-to-all-start = ((f32[16,8,512]{2,0,1:T(8,128)}), f32[16,8,512]{2,0,1:T(8,128)S(1)}, u32[]{:S(2)}, u32[]{:S(2)}) async-start(f32[16,8,512]{2,0,1:T(8,128)} %bitcast.7), calls=%async_computation | async-start | bytes 524288 | tf_op jit(solution)/shard_map/all_to_all | solution.py:337
  10.2 9.4 %copy-start.4 = (bf16[256,768]{1,0:T(8,128)(2,1)S(1)}, bf16[256,768]{1,0:T(8,128)(2,1)}, u32[]{:S(2)}) copy-start(bf16[256,768]{1,0:T(8,128)(2,1)} %constant.10.clone.fwd_ref) | copy-start | bytes 1179652
  10.2 9.4 %copy-start.7 = (f32[9,512]{1,0:T(8,128)S(1)}, f32[9,512]{1,0:T(8,128)}, u32[]{:S(2)}) copy-start(f32[9,512]{1,0:T(8,128)} %s_ref.1) | copy-start | bytes 55300
  10.3 8.8 %collective-permute-start = (bf16[288,512]{1,0:T(8,128)(2,1)S(1)}, bf16[288,512]{1,0:T(8,128)(2,1)S(1)}, u32[]{:S(2)}, u32[]{:S(2)}) collective-permute-start(bf16[288,512]{1,0:T(8,128)(2,1)S(1)} %get-tuple-element.26), channel_id=1, source_target_pairs={{1,2},{2,1},{3,4},{4,3},{5,6},{6,5},{7,8},{8,7},{9,10},{10,9},{11,... | collective-permute-start | bytes 884744 | tf_op jit(solution)/shard_map/ppermute | solution.py:333
  14.4 4.7 %collective-permute-start.1 = (bf16[288,512]{1,0:T(8,128)(2,1)S(1)}, bf16[288,512]{1,0:T(8,128)(2,1)S(1)}, u32[]{:S(2)}, u32[]{:S(2)}) collective-permute-start(bf16[288,512]{1,0:T(8,128)(2,1)S(1)} %get-tuple-element.27), channel_id=1, source_target_pairs={{0,1},{1,0},{2,3},{3,2},{4,5},{5,4},{6,7},{7,6},{8,9},{9,8},{10,11... | collective-permute-start | bytes 884744 | tf_op jit(solution)/shard_map/ppermute | solution.py:336
  52.9 8.8 %collective-permute-start.2 = (f32[8,1,128]{2,1,0:T(1,128)S(1)}, f32[8,1,128]{2,1,0:T(1,128)S(1)}, u32[]{:S(2)}, u32[]{:S(2)}) collective-permute-start(f32[8,1,128]{2,1,0:T(1,128)S(1)} %get-tuple-element.29), channel_id=1, source_target_pairs={{0,0},{8,8},{2,64},{10,72},{4,128},{12,136},{6,192},{14,200},{1,25... | collective-permute-start | bytes 12296 | tf_op jit(solution)/shard_map/ppermute | solution.py:370
  62.6 19.1 %all-to-all-start.2 = ((f32[64,9,1,128]{3,2,1,0:T(1,128)}), f32[64,9,1,128]{3,2,1,0:T(1,128)S(1)}, u32[]{:S(2)}, u32[]{:S(2)}) async-start(f32[64,9,1,128]{3,2,1,0:T(1,128)} %get-tuple-element.43), calls=%async_computation.2 | async-start | bytes 589824 | tf_op jit(solution)/shard_map/all_to_all | solution.py:379
  68.0 5.5 %collective-permute-start.3 = (f32[1,1,512]{2,1,0:T(1,128)S(1)}, f32[1,1,512]{2,1,0:T(1,128)S(1)}, u32[]{:S(2)}, u32[]{:S(2)}) collective-permute-start(f32[1,1,512]{2,1,0:T(1,128)S(1)} %get-tuple-element.32), channel_id=1, source_target_pairs={{0,1},{1,2},{2,3},{3,4},{4,5},{5,6},{6,7},{7,8},{8,9},{9,10},{10,1... | collective-permute-start | bytes 6152 | tf_op jit(solution)/shard_map/ppermute | solution.py:329
  71.5 5.2 %collective-permute-start.4 = (f32[1,1,512]{2,1,0:T(1,128)S(1)}, f32[1,1,512]{2,1,0:T(1,128)S(1)}, u32[]{:S(2)}, u32[]{:S(2)}) collective-permute-start(f32[1,1,512]{2,1,0:T(1,128)S(1)} %get-tuple-element.33), channel_id=1, source_target_pairs={{1,0},{2,1},{3,2},{4,3},{5,4},{6,5},{7,6},{8,7},{9,8},{10,9},{11,1... | collective-permute-start | bytes 6152 | tf_op jit(solution)/shard_map/ppermute | solution.py:329

commit v7 on v6

--- a/solution.py
+++ b/solution.py
@@ -111,8 +111,8 @@
     place_ref,
     q_ref, k_ref, v_ref, c_ref, far_ref, near_ref,
     h_ref, s_ref, fwd_ref, long_ref, grad_ref,
-    mixed_ref, gq_ref, gk_ref, gv_ref, part_ref, fix_ref, late_ref,
-    q_ext, k_ext, v_ext, c_next, e_ext, short_all,
+    mixed_ref, eq_ref, ek_ref, ev_ref, part_ref, fix_ref, late_ref,
+    q_ext, k_ext, v_ext, c_next, short_all,
 ):
     def f32(x):
         return x.astype(F32)
@@ -198,20 +198,17 @@
         mixed = a0[0:128] * long_own
         mixed_ref[:, cols] = mixed.astype(BF16)
 
-        def finish(s, err_own, err_far, ext, base, out_ref):
-            e_ext[0:128] = err_own
-            e_ext[128:136] = err_far
-            total = tap(s, 0) * err_own + tap(s, 1) * e_ext[1:129] + tap(s, 2) * e_ext[2:130]
-            out_ref[:, cols] = total.astype(BF16)
+        def finish(s, err_own, err_far, ext, base, err_ref):
+            err_ref[0:128, cols] = err_own
+            err_ref[128:136, cols] = err_far
             for j in range(3):
                 short_all[3 * s + j : 3 * s + j + 1, cols] = jnp.sum(
                     err_own * ext[base - j : base - j + 128], axis=0, keepdims=True
                 )
-            return total
-
-        gq = finish(0, cot * long_own, cot_next[0:8] * long_far, q_ext, 8, gq_ref)
-        gk = finish(1, pg_own * a2[128:256], pg_far * a2[256:264], k_ext, 136, gk_ref)
-        gv = finish(2, pg_own * a1[128:256], pg_far * a1[256:264], v_ext, 136, gv_ref)
+
+        finish(0, cot * long_own, cot_next[0:8] * long_far, q_ext, 8, eq_ref)
+        finish(1, pg_own * a2[128:256], pg_far * a2[256:264], k_ext, 136, ek_ref)
+        finish(2, pg_own * a1[128:256], pg_far * a1[256:264], v_ext, 136, ev_ref)
         lacking = cot_next[0:1] * h127 * p_own[1:2]
         for j in range(3):
             short_all[j : j + 1, cols] += lacking * q_ext[136 - j : 137 - j]
@@ -219,9 +216,7 @@
         late_ref[0, :, cols] = p_own[1:2]
         late_ref[1, :, cols] = lg[128:129]
         fix_ref[0:1, cols] = mixed[0:1]
-        fix_ref[1:2, cols] = gq[0:1]
-        fix_ref[2:3, cols] = gk[127:128]
-        fix_ref[3:4, cols] = gv[127:128]
+        fix_ref[1:4, cols] = jnp.zeros((3, WIDE), F32)
         fix_ref[4:5, cols] = a0[0:1] * h127
         fix_ref[5:6, cols] = tap(0, 0) * cot[0:1] * h127
         fix_ref[6:7, cols] = tap(1, 2) * h127 * a2[257:258]
@@ -249,7 +244,8 @@
         layer_kernel,
         in_specs=[pl.BlockSpec(memory_space=pltpu.SMEM)] + [vmem] * 11,
         out_specs=[vmem] * 7,
-        out_shape=[out_rows] * 4
+        out_shape=[out_rows]
+        + [jax.ShapeDtypeStruct((OUT, channels), F32)] * 3
         + [
             jax.ShapeDtypeStruct((64, CHUNK, 1, TILE), F32),
             jax.ShapeDtypeStruct((8, channels), F32),
@@ -258,7 +254,6 @@
         scratch_shapes=[
             ext, ext, ext,
             pltpu.VMEM((ROWS, WIDE), F32),
-            pltpu.VMEM((OUT, WIDE), F32),
             pltpu.VMEM((16, channels), F32),
         ],
         compiler_params=pltpu.CompilerParams(vmem_limit_bytes=VMEM_LIMIT),
@@ -273,32 +268,40 @@
 
 
 def patch_kernel(
-    p_ref, lg_ref, fix_ref, mixed_in, gq_in, gk_in, gv_in, mixed_ref, gq_ref, gk_ref, gv_ref
+    p_ref, lg_ref, fix_ref, s_ref, mixed_in, eq_ref, ek_ref, ev_ref,
+    mixed_ref, gq_ref, gk_ref, gv_ref,
 ):
-    row = lax.broadcasted_iota(jnp.int32, (EDGE, p_ref.shape[2]), 0)
-    plan = (
-        (0, p_ref, 0, 0, mixed_in, mixed_ref),
-        (1, p_ref, 0, 0, gq_in, gq_ref),
-        (2, lg_ref, ROWS - EDGE, EDGE - 1, gk_in, gk_ref),
-        (3, lg_ref, ROWS - EDGE, EDGE - 1, gv_in, gv_ref),
-    )
-    for n, late_ref, start, place, old_ref, new_ref in plan:
-        new_ref[...] = old_ref[...]
-        value = fix_ref[n : n + 1] + fix_ref[4 + n : 5 + n] * late_ref[0]
-        old = old_ref[start : start + EDGE].astype(F32)
-        new_ref[start : start + EDGE] = jnp.where(row == place, value, old).astype(BF16)
-
-
-def patch(late_p, late_lg, fix, outs):
+    channels = p_ref.shape[2]
+    row = lax.broadcasted_iota(jnp.int32, (EDGE, channels), 0)
+    mixed_ref[...] = mixed_in[...]
+    value = fix_ref[0:1] + fix_ref[4:5] * p_ref[0]
+    old = mixed_in[0:EDGE].astype(F32)
+    mixed_ref[0:EDGE] = jnp.where(row == 0, value, old).astype(BF16)
+    for s, err_ref, late_ref, place, out_ref in (
+        (0, eq_ref, p_ref, 0, gq_ref),
+        (1, ek_ref, lg_ref, ROWS - 1, gk_ref),
+        (2, ev_ref, lg_ref, ROWS - 1, gv_ref),
+    ):
+        late = fix_ref[5 + s : 6 + s] * late_ref[0]
+        for start in range(0, ROWS, EDGE):
+            total = s_ref[3 * s : 3 * s + 1] * err_ref[start : start + EDGE]
+            for j in (1, 2):
+                total += s_ref[3 * s + j : 3 * s + j + 1] * err_ref[start + j : start + j + EDGE]
+            if start <= place < start + EDGE:
+                total += jnp.where(row == place - start, late, 0.0)
+            out_ref[start : start + EDGE] = total.astype(BF16)
+
+
+def patch(late_p, late_lg, fix, shorts, mixed, errors):
     vmem = pl.BlockSpec(memory_space=pltpu.VMEM)
     return pl.pallas_call(
         patch_kernel,
-        in_specs=[vmem] * 7,
+        in_specs=[vmem] * 8,
         out_specs=[vmem] * 4,
-        out_shape=[jax.ShapeDtypeStruct(o.shape, o.dtype) for o in outs],
+        out_shape=[jax.ShapeDtypeStruct(mixed.shape, BF16)] * 4,
         compiler_params=SMALL,
         name="patch",
-    )(late_p, late_lg, fix, *outs)
+    )(late_p, late_lg, fix, shorts, mixed, *errors)
 
 
 def spread_kernel(tile_ref, short_ref, late_ref, out_ref, p_ref, lg_ref):
@@ -336,7 +339,7 @@
     near = lax.ppermute(near, "ctx", [(i, i ^ 1) for i in range(peers)])
     taps = lax.all_to_all(filter_taps, "dp", split_axis=1, concat_axis=0, tiled=True)
 
-    *outs, part, fix, late = run_layer(
+    mixed, *errors, part, fix, late = run_layer(
         place,
         (q_stream, k_stream, v_stream, cotangent),
         far,
@@ -375,7 +378,9 @@
         compiler_params=SMALL,
         name="spread",
     )(tile, short, late)
-    outs = patch(shifted(late_p, 1), shifted(late_lg, -1), fix, outs)
+    outs = patch(
+        shifted(late_p, 1), shifted(late_lg, -1), fix, short_taps, mixed, errors
+    )
     gathered = lax.all_to_all(sent, "ctx", split_axis=0, concat_axis=0, tiled=True)
     scale = 1.0 / math.sqrt(ROWS * peers)
     grad_filter, grad_short = pl.pallas_call(

time: 83.1 us -> 82.8 us (level)
  no operation moved by 1% of the time
where the time goes in v7:
time: 82.8 us; the launch traced here: 82.3 us
  blocking collectives  30.3 us (37%)
  starting transfers between devices  29.5 us (36%)
  waiting for transfers between devices  14.5 us (18%)
  Pallas kernels  5.46 us (7%)
  local copies, waits for them, and re-layouts  1.76 us (2%)
    all_to_all x1, blocking collectives, on_device(): part = lax.all_to_all(part, 'ctx', split_axis=0, concat_axis=0, tiled=True)  30.3 us
    all_to_all x1, starting transfers between devices, on_device(): lax.all_to_all(filter_taps, 'dp', split_axis=1, concat_axis=0, tiled=True)  7.79 us
    ppermute x2, starting transfers between devices, shifted(): return lax.ppermute(value, 'ctx', pairs)  5.46 us
    all_to_all x1, starting transfers between devices, on_device(): lax.all_to_all(sent, 'ctx', split_axis=0, concat_axis=0, tiled=True)  5.42 us
    ppermute x1, starting transfers between devices, on_device(): tile = lax.ppermute(tile, ('dp', 'ctx'), pairs)  4.81 us
    ppermute x1, starting transfers between devices, on_device(): lax.ppermute(far, 'ctx', [(i, i + 1 if i % 2 else i - 1) for i in range(1...  4.09 us
    ppermute x1, waiting for transfers between devices, on_device(): tile = lax.ppermute(tile, ('dp', 'ctx'), pairs)  4.01 us
    all_to_all x1, waiting for transfers between devices, on_device(): lax.all_to_all(sent, 'ctx', split_axis=0, concat_axis=0, tiled=True)  4 us
  transfers between devices with their start and end apart: 7, of which 5 were waited for; matrix products, arithmetic and copies ran while one was open for 0% of the time, Pallas kernels for 1%

profile of v7, /device:TPU:1, one launch (start us, length us, event | category | flops | bytes accessed | tf_op | source)
XLA Modules:
  0.0 82.3 jit_solution(9156675332578301528)
XLA Ops:
  0.6 0.0 copy-start.5
  0.6 0.0 copy-start.6
  0.7 1.7 %copy.18 = f32[2,8,8,512]{3,2,0,1:T(8,128)} copy(f32[2,8,8,512]{3,2,1,0:T(8,128)} %bitcast.9) | data formatting | bytes 524288 | tf_op jit(solution)/shard_map/all_to_all | solution.py:340
  2.4 0.0 copy-start
  2.4 0.0 copy-start.1
  2.4 0.0 copy-start.2
  2.4 0.0 copy-start.3
  2.4 7.8 %all-to-all-start = ((f32[16,8,512]{2,0,1:T(8,128)}), f32[16,8,512]{2,0,1:T(8,128)S(1)}, u32[]{:S(2)}, u32[]{:S(2)}) async-start(f32[16,8,512]{2,0,1:T(8,128)} %bitcast.7), calls=%async_computation | async-start | bytes 524288 | tf_op jit(solution)/shard_map/all_to_all | solution.py:340
  10.2 0.0 copy-start.4
  10.2 0.0 copy-done
  10.2 0.0 copy-done.1
  10.2 0.0 copy-done.2
  10.2 0.0 copy-done.3
  10.2 0.0 copy-start.7
  10.2 0.1 pack.1
  10.3 4.1 %collective-permute-start = (bf16[288,512]{1,0:T(8,128)(2,1)S(1)}, bf16[288,512]{1,0:T(8,128)(2,1)S(1)}, u32[]{:S(2)}, u32[]{:S(2)}) collective-permute-start(bf16[288,512]{1,0:T(8,128)(2,1)S(1)} %get-tuple-element.26), channel_id=1, source_target_pairs={{1,2},{2,1},{3,4},{4,3},{5,6},{6,5},{7,8},{8,7},{9,10},{10,9},{11,... | collective-permute-start | bytes 884744 | tf_op jit(solution)/shard_map/ppermute | solution.py:336
  14.4 1.9 %collective-permute-start.1 = (bf16[288,512]{1,0:T(8,128)(2,1)S(1)}, bf16[288,512]{1,0:T(8,128)(2,1)S(1)}, u32[]{:S(2)}, u32[]{:S(2)}) collective-permute-start(bf16[288,512]{1,0:T(8,128)(2,1)S(1)} %get-tuple-element.27), channel_id=1, source_target_pairs={{0,1},{1,0},{2,3},{3,2},{4,5},{5,4},{6,7},{7,6},{8,9},{9,8},{10,11... | collective-permute-start | bytes 884744 | tf_op jit(solution)/shard_map/ppermute | solution.py:339
  16.3 2.8 %collective-permute-done.far_ref = bf16[288,512]{1,0:T(8,128)(2,1)S(1)} collective-permute-done((bf16[288,512]{1,0:T(8,128)(2,1)S(1)}, bf16[288,512]{1,0:T(8,128)(2,1)S(1)}, u32[]{:S(2)}, u32[]{:S(2)}) %collective-permute-start) | collective-permute-done | bytes 294944 | tf_op jit(solution)/shard_map/ppermute | solution.py:336
  19.1 0.0 collective-permute-done.1.near_ref
  19.1 0.5 all-to-all-done
  19.6 0.0 copy-done.5
  19.6 0.0 copy-done.6
  19.6 0.0 copy-done.4
  19.6 0.0 copy-done.7
  19.6 2.4 %layer.1 = (bf16[128,512]{1,0:T(8,128)(2,1)S(1)}, f32[136,512]{1,0:T(8,128)S(1)}, f32[136,512]{1,0:T(8,128)S(1)}, f32[136,512]{1,0:T(8,128)S(1)}, f32[64,9,1,128...) custom-call(s32[1]{0:T(128)} %bitcast.place_ref, bf16[128,512]{1,0:T(8,128)(2,1)S(1)} %copy-done, ...), custom_call_target="tpu_custom_call" | custom-call | tf_op jit(solution)/shard_map/layer/pallas_call | solution.py:243
  22.1 30.3 %all_to_all.29.part_ref = f32[64,9,1,128]{3,2,1,0:T(1,128)S(1)} all-to-all(f32[64,9,1,128]{3,2,1,0:T(1,128)S(1)} %get-tuple-element.28), channel_id=1, replica_groups=mesh['dp'=8,'ctx'=64] {'ctx'}, dimensions={0} | all-to-all | bytes 589824 | tf_op jit(solution)/shard_map/all_to_all | solution.py:352
  52.3 0.2 sum.1
  52.6 4.8 %collective-permute-start.2 = (f32[8,1,128]{2,1,0:T(1,128)S(1)}, f32[8,1,128]{2,1,0:T(1,128)S(1)}, u32[]{:S(2)}, u32[]{:S(2)}) collective-permute-start(f32[8,1,128]{2,1,0:T(1,128)S(1)} %get-tuple-element.29), channel_id=1, source_target_pairs={{0,0},{8,8},{2,64},{10,72},{4,128},{12,136},{6,192},{14,200},{1,25... | collective-permute-start | bytes 12296 | tf_op jit(solution)/shard_map/ppermute | solution.py:373
  57.4 4.0 %collective-permute-done.2.tile_ref = f32[8,1,128]{2,1,0:T(1,128)S(1)} collective-permute-done((f32[8,1,128]{2,1,0:T(1,128)S(1)}, f32[8,1,128]{2,1,0:T(1,128)S(1)}, u32[]{:S(2)}, u32[]{:S(2)}) %collective-permute-start.2) | collective-permute-done | bytes 4128 | tf_op jit(solution)/shard_map/ppermute | solution.py:373
  61.4 0.9 %spread.1 = (f32[64,9,1,128]{3,2,1,0:T(1,128)}, f32[1,1,512]{2,1,0:T(1,128)S(1)}, f32[1,1,512]{2,1,0:T(1,128)S(1)}) custom-call(f32[8,1,128]{2,1,0:T(1,128)S(1)} %collective-permute-done.2.tile_ref, f32[1,1,128]{2,1,0:T(1,128)S(1)} %get-tuple-element.30.short_ref, f32[2,1,512]{2,1,0:T(1,128)S(1)} %get-tuple-element.31.late_ref), custom_call_target="tpu_custom_call" | custom-call | tf_op jit(solution)/shard_map/spread/pallas_call | solution.py:375
  62.3 5.4 %all-to-all-start.2 = ((f32[64,9,1,128]{3,2,1,0:T(1,128)}), f32[64,9,1,128]{3,2,1,0:T(1,128)S(1)}, u32[]{:S(2)}, u32[]{:S(2)}) async-start(f32[64,9,1,128]{3,2,1,0:T(1,128)} %get-tuple-element.43), calls=%async_computation.2 | async-start | bytes 589824 | tf_op jit(solution)/shard_map/all_to_all | solution.py:384
  67.7 3.5 %collective-permute-start.3 = (f32[1,1,512]{2,1,0:T(1,128)S(1)}, f32[1,1,512]{2,1,0:T(1,128)S(1)}, u32[]{:S(2)}, u32[]{:S(2)}) collective-permute-start(f32[1,1,512]{2,1,0:T(1,128)S(1)} %get-tuple-element.32), channel_id=1, source_target_pairs={{0,1},{1,2},{2,3},{3,4},{4,5},{5,6},{6,7},{7,8},{8,9},{9,10},{10,1... | collective-permute-start | bytes 6152 | tf_op jit(solution)/shard_map/ppermute | solution.py:332
  71.2 1.9 %collective-permute-start.4 = (f32[1,1,512]{2,1,0:T(1,128)S(1)}, f32[1,1,512]{2,1,0:T(1,128)S(1)}, u32[]{:S(2)}, u32[]{:S(2)}) collective-permute-start(f32[1,1,512]{2,1,0:T(1,128)S(1)} %get-tuple-element.33), channel_id=1, source_target_pairs={{1,0},{2,1},{3,2},{4,3},{5,4},{6,5},{7,6},{8,7},{9,8},{10,9},{11,1... | collective-permute-start | bytes 6152 | tf_op jit(solution)/shard_map/ppermute | solution.py:332
  73.2 0.0 collective-permute-done.3.p_ref
  73.2 3.3 %collective-permute-done.4.lg_ref = f32[1,1,512]{2,1,0:T(1,128)S(1)} collective-permute-done((f32[1,1,512]{2,1,0:T(1,128)S(1)}, f32[1,1,512]{2,1,0:T(1,128)S(1)}, u32[]{:S(2)}, u32[]{:S(2)}) %collective-permute-start.4) | collective-permute-done | bytes 2080 | tf_op jit(solution)/shard_map/ppermute | solution.py:332
  76.4 1.0 %patch.1 = (bf16[128,512]{1,0:T(8,128)(2,1)}, bf16[128,512]{1,0:T(8,128)(2,1)}, bf16[128,512]{1,0:T(8,128)(2,1)}, bf16[128,512]{1,0:T(8,128)(2,1)}) custom-call(f32[1,1,512]{2,1,0:T(1,128)S(1)} %collective-permute-done.3.p_ref, f32[1,1,512]{2,1,0:T(1,128)S(1)} %collective-permute-done.4.lg_ref, f32[8,512]{1,0:T(8,128)S(1)} %get-tuple-element.34.fix_ref, ...), custom_call_target="tpu_custom_call" | custom-call | tf_op jit(solution)/shard_map/patch/pallas_call | solution.py:297
  77.4 4.0 %all-to-all-done.2.gathered_ref = f32[64,9,1,128]{3,2,1,0:T(1,128)S(1)} async-done(((f32[64,9,1,128]{3,2,1,0:T(1,128)}), f32[64,9,1,128]{3,2,1,0:T(1,128)S(1)}, u32[]{:S(2)}, u32[]{:S(2)}) %all-to-all-start.2) | async-done | bytes 294944 | tf_op jit(solution)/shard_map/all_to_all | solution.py:384
  81.4 0.9 %final.1 = (f32[16,4096]{1,0:T(8,128)}, f32[9,512]{1,0:T(8,128)}) custom-call(f32[64,9,1,128]{3,2,1,0:T(1,128)S(1)} %all-to-all-done.2.gathered_ref), custom_call_target="tpu_custom_call" | custom-call | tf_op jit(solution)/shard_map/final/pallas_call | solution.py:386
Async XLA Ops:
  0.6 19.0 %copy-start.5 = (bf16[136,768]{1,0:T(8,128)(2,1)S(1)}, bf16[136,768]{1,0:T(8,128)(2,1)}, u32[]{:S(2)}) copy-start(bf16[136,768]{1,0:T(8,128)(2,1)} %constant.12.clone.grad_ref) | copy-start | bytes 626692
  0.6 19.0 %copy-start.6 = (bf16[136,768]{1,0:T(8,128)(2,1)S(1)}, bf16[136,768]{1,0:T(8,128)(2,1)}, u32[]{:S(2)}) copy-start(bf16[136,768]{1,0:T(8,128)(2,1)} %constant.11.clone.long_ref) | copy-start | bytes 626692
  2.4 7.8 %copy-start = (bf16[128,512]{1,0:T(8,128)(2,1)S(1)}, bf16[128,512]{1,0:T(8,128)(2,1)}, u32[]{:S(2)}) copy-start(bf16[128,512]{1,0:T(8,128)(2,1)} %q_ref.3) | copy-start | bytes 393220
  2.4 7.8 %copy-start.1 = (bf16[128,512]{1,0:T(8,128)(2,1)S(1)}, bf16[128,512]{1,0:T(8,128)(2,1)}, u32[]{:S(2)}) copy-start(bf16[128,512]{1,0:T(8,128)(2,1)} %k_ref.3) | copy-start | bytes 393220
  2.4 7.8 %copy-start.2 = (bf16[128,512]{1,0:T(8,128)(2,1)S(1)}, bf16[128,512]{1,0:T(8,128)(2,1)}, u32[]{:S(2)}) copy-start(bf16[128,512]{1,0:T(8,128)(2,1)} %v_ref.3) | copy-start | bytes 393220
  2.4 7.8 %copy-start.3 = (bf16[128,512]{1,0:T(8,128)(2,1)S(1)}, bf16[128,512]{1,0:T(8,128)(2,1)}, u32[]{:S(2)}) copy-start(bf16[128,512]{1,0:T(8,128)(2,1)} %c_ref.3) | copy-start | bytes 393220
  2.4 17.2 %all-to-all-start = ((f32[16,8,512]{2,0,1:T(8,128)}), f32[16,8,512]{2,0,1:T(8,128)S(1)}, u32[]{:S(2)}, u32[]{:S(2)}) async-start(f32[16,8,512]{2,0,1:T(8,128)} %bitcast.7), calls=%async_computation | async-start | bytes 524288 | tf_op jit(solution)/shard_map/all_to_all | solution.py:340
  10.2 9.4 %copy-start.4 = (bf16[256,768]{1,0:T(8,128)(2,1)S(1)}, bf16[256,768]{1,0:T(8,128)(2,1)}, u32[]{:S(2)}) copy-start(bf16[256,768]{1,0:T(8,128)(2,1)} %constant.10.clone.fwd_ref) | copy-start | bytes 1179652
  10.2 9.4 %copy-start.7 = (f32[9,512]{1,0:T(8,128)S(1)}, f32[9,512]{1,0:T(8,128)}, u32[]{:S(2)}) copy-start(f32[9,512]{1,0:T(8,128)} %s_ref.3) | copy-start | bytes 55300
  10.3 8.8 %collective-permute-start = (bf16[288,512]{1,0:T(8,128)(2,1)S(1)}, bf16[288,512]{1,0:T(8,128)(2,1)S(1)}, u32[]{:S(2)}, u32[]{:S(2)}) collective-permute-start(bf16[288,512]{1,0:T(8,128)(2,1)S(1)} %get-tuple-element.26), channel_id=1, source_target_pairs={{1,2},{2,1},{3,4},{4,3},{5,6},{6,5},{7,8},{8,7},{9,10},{10,9},{11,... | collective-permute-start | bytes 884744 | tf_op jit(solution)/shard_map/ppermute | solution.py:336
  14.4 4.7 %collective-permute-start.1 = (bf16[288,512]{1,0:T(8,128)(2,1)S(1)}, bf16[288,512]{1,0:T(8,128)(2,1)S(1)}, u32[]{:S(2)}, u32[]{:S(2)}) collective-permute-start(bf16[288,512]{1,0:T(8,128)(2,1)S(1)} %get-tuple-element.27), channel_id=1, source_target_pairs={{0,1},{1,0},{2,3},{3,2},{4,5},{5,4},{6,7},{7,6},{8,9},{9,8},{10,11... | collective-permute-start | bytes 884744 | tf_op jit(solution)/shard_map/ppermute | solution.py:339
  52.6 8.8 %collective-permute-start.2 = (f32[8,1,128]{2,1,0:T(1,128)S(1)}, f32[8,1,128]{2,1,0:T(1,128)S(1)}, u32[]{:S(2)}, u32[]{:S(2)}) collective-permute-start(f32[8,1,128]{2,1,0:T(1,128)S(1)} %get-tuple-element.29), channel_id=1, source_target_pairs={{0,0},{8,8},{2,64},{10,72},{4,128},{12,136},{6,192},{14,200},{1,25... | collective-permute-start | bytes 12296 | tf_op jit(solution)/shard_map/ppermute | solution.py:373
  62.3 19.1 %all-to-all-start.2 = ((f32[64,9,1,128]{3,2,1,0:T(1,128)}), f32[64,9,1,128]{3,2,1,0:T(1,128)S(1)}, u32[]{:S(2)}, u32[]{:S(2)}) async-start(f32[64,9,1,128]{3,2,1,0:T(1,128)} %get-tuple-element.43), calls=%async_computation.2 | async-start | bytes 589824 | tf_op jit(solution)/shard_map/all_to_all | solution.py:384
  67.7 5.5 %collective-permute-start.3 = (f32[1,1,512]{2,1,0:T(1,128)S(1)}, f32[1,1,512]{2,1,0:T(1,128)S(1)}, u32[]{:S(2)}, u32[]{:S(2)}) collective-permute-start(f32[1,1,512]{2,1,0:T(1,128)S(1)} %get-tuple-element.32), channel_id=1, source_target_pairs={{0,1},{1,2},{2,3},{3,4},{4,5},{5,6},{6,7},{7,8},{8,9},{9,10},{10,1... | collective-permute-start | bytes 6152 | tf_op jit(solution)/shard_map/ppermute | solution.py:332
  71.2 5.2 %collective-permute-start.4 = (f32[1,1,512]{2,1,0:T(1,128)S(1)}, f32[1,1,512]{2,1,0:T(1,128)S(1)}, u32[]{:S(2)}, u32[]{:S(2)}) collective-permute-start(f32[1,1,512]{2,1,0:T(1,128)S(1)} %get-tuple-element.33), channel_id=1, source_target_pairs={{1,0},{2,1},{3,2},{4,3},{5,4},{6,5},{7,6},{8,7},{9,8},{10,9},{11,1... | collective-permute-start | bytes 6152 | tf_op jit(solution)/shard_map/ppermute | solution.py:332

commit v8 on v7

--- a/solution.py
+++ b/solution.py
@@ -103,6 +103,13 @@
     )(place, q_stream, k_stream, v_stream, cotangent)
 
 
+def order_of(peers):
+    return [(i * 29 + 7) % peers for i in range(peers)]
+
+
+ORDER = order_of(64)
+
+
 def seat(h, owner, half):
     return 16 * h + 8 * half + 2 * (owner % 4) + owner // 4
 
@@ -227,12 +234,12 @@
             lanes = slice(part * TILE, (part + 1) * TILE)
             for g in range(16):
                 tile = filt[8 * g : 8 * g + 8, lanes]
-                part_ref[seat(h, g // 2, g % 2), 0:8] = tile.reshape(8, 1, TILE)
+                part_ref[ORDER.index(seat(h, g // 2, g % 2)), 0:8] = tile.reshape(8, 1, TILE)
                 if g < 9:
                     value = short_all[g : g + 1, h * TILE : (h + 1) * TILE]
                 else:
                     value = jnp.zeros((1, TILE), F32)
-                part_ref[seat(h, g // 2, g % 2), 8] = value
+                part_ref[ORDER.index(seat(h, g // 2, g % 2)), 8] = value
 
 
 def run_layer(place, streams, far, near, taps, shorts, matrices):
@@ -316,11 +323,11 @@
     for h in range(4):
         for d in range(groups):
             for half in range(2):
-                tile = gathered_ref[seat(h, d, half), 0:8].reshape(8, TILE)
+                tile = gathered_ref[ORDER.index(seat(h, d, half)), 0:8].reshape(8, TILE)
                 start = (d * 4 + h) * TILE
                 filter_ref[8 * half : 8 * half + 8, start : start + TILE] = tile * scale
         for g in range(9):
-            row = gathered_ref[seat(h, g // 2, g % 2), 8] * scale
+            row = gathered_ref[ORDER.index(seat(h, g // 2, g % 2)), 8] * scale
             short_ref[g : g + 1, h * TILE : (h + 1) * TILE] = row
 
 
@@ -349,7 +356,7 @@
         matrices,
     )
 
-    part = lax.all_to_all(part, "ctx", split_axis=0, concat_axis=0, tiled=True)
+    part = lax.all_to_all(part, "ctx", split_axis=0, concat_axis=0, tiled=True, axis_index_groups=[ORDER])
     vmem = pl.BlockSpec(memory_space=pltpu.VMEM)
     tile, short = pl.pallas_call(
         sum_kernel,
@@ -381,7 +388,7 @@
     outs = patch(
         shifted(late_p, 1), shifted(late_lg, -1), fix, short_taps, mixed, errors
     )
-    gathered = lax.all_to_all(sent, "ctx", split_axis=0, concat_axis=0, tiled=True)
+    gathered = lax.all_to_all(sent, "ctx", split_axis=0, concat_axis=0, tiled=True, axis_index_groups=[ORDER])
     scale = 1.0 / math.sqrt(ROWS * peers)
     grad_filter, grad_short = pl.pallas_call(
         functools.partial(final_kernel, scale, groups),

time: 82.8 us -> 80.2 us (0.969)
  waiting for transfers between devices: 14.5 us -> 11 us
  starting transfers between devices: 29.5 us -> 31.9 us
  blocking collectives: 30.3 us -> 28.9 us
    ppermute x1, waiting for transfers between devices: 4.01 us -> 1.84 us  [on_device(): tile = lax.ppermute(tile, ('dp', 'ctx'), pairs)]
    ppermute x1, starting transfers between devices: 4.81 us -> 6.98 us  [on_device(): tile = lax.ppermute(tile, ('dp', 'ctx'), pairs)]
    all_to_all x1, blocking collectives: 30.3 us -> 28.9 us  [on_device(): lax.all_to_all(part, 'ctx', split_axis=0, concat_axis=0, tiled=True, axis...]
    all_to_all x1, waiting for transfers between devices: 4 us -> 2.65 us  [on_device(): lax.all_to_all(sent, 'ctx', split_axis=0, concat_axis=0, tiled=True, axis...]
where the time goes in v8:
time: 80.2 us; the launch traced here: 79.8 us
  starting transfers between devices  31.9 us (40%)
  blocking collectives  28.9 us (36%)
  waiting for transfers between devices  11 us (14%)
  Pallas kernels  5.46 us (7%)
  local copies, waits for them, and re-layouts  1.76 us (2%)
    all_to_all x1, blocking collectives, on_device(): lax.all_to_all(part, 'ctx', split_axis=0, concat_axis=0, tiled=True, axis...  28.9 us
    all_to_all x1, starting transfers between devices, on_device(): lax.all_to_all(filter_taps, 'dp', split_axis=1, concat_axis=0, tiled=True)  7.79 us
    ppermute x1, starting transfers between devices, on_device(): tile = lax.ppermute(tile, ('dp', 'ctx'), pairs)  6.98 us
    all_to_all x1, starting transfers between devices, on_device(): lax.all_to_all(sent, 'ctx', split_axis=0, concat_axis=0, tiled=True, axis...  6.12 us
    ppermute x2, starting transfers between devices, shifted(): return lax.ppermute(value, 'ctx', pairs)  4.94 us
    ppermute x1, starting transfers between devices, on_device(): lax.ppermute(far, 'ctx', [(i, i + 1 if i % 2 else i - 1) for i in range(1...  4.09 us
    ppermute x2, waiting for transfers between devices, shifted(): return lax.ppermute(value, 'ctx', pairs)  3.27 us
    ppermute x1, waiting for transfers between devices, on_device(): lax.ppermute(far, 'ctx', [(i, i + 1 if i % 2 else i - 1) for i in range(1...  2.76 us
  transfers between devices with their start and end apart: 7, of which 5 were waited for; matrix products, arithmetic and copies ran while one was open for 0% of the time, Pallas kernels for 1%

profile of v8, /device:TPU:1, one launch (start us, length us, event | category | flops | bytes accessed | tf_op | source)
XLA Modules:
  0.0 79.8 jit_solution(17658018679048152280)
XLA Ops:
  0.6 0.0 copy-start.5
  0.6 0.0 copy-start.6
  0.7 1.7 %copy.18 = f32[2,8,8,512]{3,2,0,1:T(8,128)} copy(f32[2,8,8,512]{3,2,1,0:T(8,128)} %bitcast.9) | data formatting | bytes 524288 | tf_op jit(solution)/shard_map/all_to_all | solution.py:347
  2.4 0.0 copy-start
  2.4 0.0 copy-start.1
  2.4 0.0 copy-start.2
  2.4 0.0 copy-start.3
  2.4 7.8 %all-to-all-start = ((f32[16,8,512]{2,0,1:T(8,128)}), f32[16,8,512]{2,0,1:T(8,128)S(1)}, u32[]{:S(2)}, u32[]{:S(2)}) async-start(f32[16,8,512]{2,0,1:T(8,128)} %bitcast.7), calls=%async_computation | async-start | bytes 524288 | tf_op jit(solution)/shard_map/all_to_all | solution.py:347
  10.2 0.0 copy-start.4
  10.2 0.0 copy-done
  10.2 0.0 copy-done.1
  10.2 0.0 copy-done.2
  10.2 0.0 copy-done.3
  10.2 0.0 copy-start.7
  10.2 0.1 pack.1
  10.3 4.1 %collective-permute-start = (bf16[288,512]{1,0:T(8,128)(2,1)S(1)}, bf16[288,512]{1,0:T(8,128)(2,1)S(1)}, u32[]{:S(2)}, u32[]{:S(2)}) collective-permute-start(bf16[288,512]{1,0:T(8,128)(2,1)S(1)} %get-tuple-element.26), channel_id=1, source_target_pairs={{1,2},{2,1},{3,4},{4,3},{5,6},{6,5},{7,8},{8,7},{9,10},{10,9},{11,... | collective-permute-start | bytes 884744 | tf_op jit(solution)/shard_map/ppermute | solution.py:343
  14.4 1.9 %collective-permute-start.1 = (bf16[288,512]{1,0:T(8,128)(2,1)S(1)}, bf16[288,512]{1,0:T(8,128)(2,1)S(1)}, u32[]{:S(2)}, u32[]{:S(2)}) collective-permute-start(bf16[288,512]{1,0:T(8,128)(2,1)S(1)} %get-tuple-element.27), channel_id=1, source_target_pairs={{0,1},{1,0},{2,3},{3,2},{4,5},{5,4},{6,7},{7,6},{8,9},{9,8},{10,11... | collective-permute-start | bytes 884744 | tf_op jit(solution)/shard_map/ppermute | solution.py:346
  16.3 2.8 %collective-permute-done.far_ref = bf16[288,512]{1,0:T(8,128)(2,1)S(1)} collective-permute-done((bf16[288,512]{1,0:T(8,128)(2,1)S(1)}, bf16[288,512]{1,0:T(8,128)(2,1)S(1)}, u32[]{:S(2)}, u32[]{:S(2)}) %collective-permute-start) | collective-permute-done | bytes 294944 | tf_op jit(solution)/shard_map/ppermute | solution.py:343
  19.1 0.0 collective-permute-done.1.near_ref
  19.1 0.5 all-to-all-done
  19.6 0.0 copy-done.5
  19.6 0.0 copy-done.6
  19.6 0.0 copy-done.4
  19.6 0.0 copy-done.7
  19.6 2.4 %layer.1 = (bf16[128,512]{1,0:T(8,128)(2,1)S(1)}, f32[136,512]{1,0:T(8,128)S(1)}, f32[136,512]{1,0:T(8,128)S(1)}, f32[136,512]{1,0:T(8,128)S(1)}, f32[64,9,1,128...) custom-call(s32[1]{0:T(128)} %bitcast.place_ref, bf16[128,512]{1,0:T(8,128)(2,1)S(1)} %copy-done, ...), custom_call_target="tpu_custom_call" | custom-call | tf_op jit(solution)/shard_map/layer/pallas_call | solution.py:250
  22.1 28.9 %all_to_all.29.part_ref = f32[64,9,1,128]{3,2,1,0:T(1,128)S(1)} all-to-all(f32[64,9,1,128]{3,2,1,0:T(1,128)S(1)} %get-tuple-element.28), channel_id=1, replica_groups={{7,36,1,30,59,24,53,18,47,12,41,6,35,0,29,58,23,52,17,46,11,40,5,34,63,..., dimensions={0} | all-to-all | bytes 589824 | tf_op jit(solution)/shard_map/all_to_all | solution.py:359
  50.9 0.2 sum.1
  51.1 7.0 %collective-permute-start.2 = (f32[8,1,128]{2,1,0:T(1,128)S(1)}, f32[8,1,128]{2,1,0:T(1,128)S(1)}, u32[]{:S(2)}, u32[]{:S(2)}) collective-permute-start(f32[8,1,128]{2,1,0:T(1,128)S(1)} %get-tuple-element.29), channel_id=1, source_target_pairs={{0,0},{8,8},{2,64},{10,72},{4,128},{12,136},{6,192},{14,200},{1,25... | collective-permute-start | bytes 12296 | tf_op jit(solution)/shard_map/ppermute | solution.py:380
  58.1 1.8 %collective-permute-done.2.tile_ref = f32[8,1,128]{2,1,0:T(1,128)S(1)} collective-permute-done((f32[8,1,128]{2,1,0:T(1,128)S(1)}, f32[8,1,128]{2,1,0:T(1,128)S(1)}, u32[]{:S(2)}, u32[]{:S(2)}) %collective-permute-start.2) | collective-permute-done | bytes 4128 | tf_op jit(solution)/shard_map/ppermute | solution.py:380
  60.0 0.9 %spread.1 = (f32[64,9,1,128]{3,2,1,0:T(1,128)}, f32[1,1,512]{2,1,0:T(1,128)S(1)}, f32[1,1,512]{2,1,0:T(1,128)S(1)}) custom-call(f32[8,1,128]{2,1,0:T(1,128)S(1)} %collective-permute-done.2.tile_ref, f32[1,1,128]{2,1,0:T(1,128)S(1)} %get-tuple-element.30.short_ref, f32[2,1,512]{2,1,0:T(1,128)S(1)} %get-tuple-element.31.late_ref), custom_call_target="tpu_custom_call" | custom-call | tf_op jit(solution)/shard_map/spread/pallas_call | solution.py:382
  60.9 6.1 %all-to-all-start.2 = ((f32[64,9,1,128]{3,2,1,0:T(1,128)}), f32[64,9,1,128]{3,2,1,0:T(1,128)S(1)}, u32[]{:S(2)}, u32[]{:S(2)}) async-start(f32[64,9,1,128]{3,2,1,0:T(1,128)} %get-tuple-element.43), calls=%async_computation.2 | async-start | bytes 589824 | tf_op jit(solution)/shard_map/all_to_all | solution.py:391
  67.0 3.0 %collective-permute-start.3 = (f32[1,1,512]{2,1,0:T(1,128)S(1)}, f32[1,1,512]{2,1,0:T(1,128)S(1)}, u32[]{:S(2)}, u32[]{:S(2)}) collective-permute-start(f32[1,1,512]{2,1,0:T(1,128)S(1)} %get-tuple-element.32), channel_id=1, source_target_pairs={{0,1},{1,2},{2,3},{3,4},{4,5},{5,6},{6,7},{7,8},{8,9},{9,10},{10,1... | collective-permute-start | bytes 6152 | tf_op jit(solution)/shard_map/ppermute | solution.py:339
  70.0 1.9 %collective-permute-start.4 = (f32[1,1,512]{2,1,0:T(1,128)S(1)}, f32[1,1,512]{2,1,0:T(1,128)S(1)}, u32[]{:S(2)}, u32[]{:S(2)}) collective-permute-start(f32[1,1,512]{2,1,0:T(1,128)S(1)} %get-tuple-element.33), channel_id=1, source_target_pairs={{1,0},{2,1},{3,2},{4,3},{5,4},{6,5},{7,6},{8,7},{9,8},{10,9},{11,1... | collective-permute-start | bytes 6152 | tf_op jit(solution)/shard_map/ppermute | solution.py:339
  71.9 0.0 collective-permute-done.3.p_ref
  72.0 3.3 %collective-permute-done.4.lg_ref = f32[1,1,512]{2,1,0:T(1,128)S(1)} collective-permute-done((f32[1,1,512]{2,1,0:T(1,128)S(1)}, f32[1,1,512]{2,1,0:T(1,128)S(1)}, u32[]{:S(2)}, u32[]{:S(2)}) %collective-permute-start.4) | collective-permute-done | bytes 2080 | tf_op jit(solution)/shard_map/ppermute | solution.py:339
  75.2 1.0 %patch.1 = (bf16[128,512]{1,0:T(8,128)(2,1)}, bf16[128,512]{1,0:T(8,128)(2,1)}, bf16[128,512]{1,0:T(8,128)(2,1)}, bf16[128,512]{1,0:T(8,128)(2,1)}) custom-call(f32[1,1,512]{2,1,0:T(1,128)S(1)} %collective-permute-done.3.p_ref, f32[1,1,512]{2,1,0:T(1,128)S(1)} %collective-permute-done.4.lg_ref, f32[8,512]{1,0:T(8,128)S(1)} %get-tuple-element.34.fix_ref, ...), custom_call_target="tpu_custom_call" | custom-call | tf_op jit(solution)/shard_map/patch/pallas_call | solution.py:304
  76.2 2.7 %all-to-all-done.2.gathered_ref = f32[64,9,1,128]{3,2,1,0:T(1,128)S(1)} async-done(((f32[64,9,1,128]{3,2,1,0:T(1,128)}), f32[64,9,1,128]{3,2,1,0:T(1,128)S(1)}, u32[]{:S(2)}, u32[]{:S(2)}) %all-to-all-start.2) | async-done | bytes 294944 | tf_op jit(solution)/shard_map/all_to_all | solution.py:391
  78.8 0.9 %final.1 = (f32[16,4096]{1,0:T(8,128)}, f32[9,512]{1,0:T(8,128)}) custom-call(f32[64,9,1,128]{3,2,1,0:T(1,128)S(1)} %all-to-all-done.2.gathered_ref), custom_call_target="tpu_custom_call" | custom-call | tf_op jit(solution)/shard_map/final/pallas_call | solution.py:393
Async XLA Ops:
  0.6 19.0 %copy-start.5 = (bf16[136,768]{1,0:T(8,128)(2,1)S(1)}, bf16[136,768]{1,0:T(8,128)(2,1)}, u32[]{:S(2)}) copy-start(bf16[136,768]{1,0:T(8,128)(2,1)} %constant.12.clone.grad_ref) | copy-start | bytes 626692
  0.6 19.0 %copy-start.6 = (bf16[136,768]{1,0:T(8,128)(2,1)S(1)}, bf16[136,768]{1,0:T(8,128)(2,1)}, u32[]{:S(2)}) copy-start(bf16[136,768]{1,0:T(8,128)(2,1)} %constant.11.clone.long_ref) | copy-start | bytes 626692
  2.4 7.8 %copy-start = (bf16[128,512]{1,0:T(8,128)(2,1)S(1)}, bf16[128,512]{1,0:T(8,128)(2,1)}, u32[]{:S(2)}) copy-start(bf16[128,512]{1,0:T(8,128)(2,1)} %q_ref.3) | copy-start | bytes 393220
  2.4 7.8 %copy-start.1 = (bf16[128,512]{1,0:T(8,128)(2,1)S(1)}, bf16[128,512]{1,0:T(8,128)(2,1)}, u32[]{:S(2)}) copy-start(bf16[128,512]{1,0:T(8,128)(2,1)} %k_ref.3) | copy-start | bytes 393220
  2.4 7.8 %copy-start.2 = (bf16[128,512]{1,0:T(8,128)(2,1)S(1)}, bf16[128,512]{1,0:T(8,128)(2,1)}, u32[]{:S(2)}) copy-start(bf16[128,512]{1,0:T(8,128)(2,1)} %v_ref.3) | copy-start | bytes 393220
  2.4 7.8 %copy-start.3 = (bf16[128,512]{1,0:T(8,128)(2,1)S(1)}, bf16[128,512]{1,0:T(8,128)(2,1)}, u32[]{:S(2)}) copy-start(bf16[128,512]{1,0:T(8,128)(2,1)} %c_ref.3) | copy-start | bytes 393220
  2.4 17.2 %all-to-all-start = ((f32[16,8,512]{2,0,1:T(8,128)}), f32[16,8,512]{2,0,1:T(8,128)S(1)}, u32[]{:S(2)}, u32[]{:S(2)}) async-start(f32[16,8,512]{2,0,1:T(8,128)} %bitcast.7), calls=%async_computation | async-start | bytes 524288 | tf_op jit(solution)/shard_map/all_to_all | solution.py:347
  10.2 9.4 %copy-start.4 = (bf16[256,768]{1,0:T(8,128)(2,1)S(1)}, bf16[256,768]{1,0:T(8,128)(2,1)}, u32[]{:S(2)}) copy-start(bf16[256,768]{1,0:T(8,128)(2,1)} %constant.10.clone.fwd_ref) | copy-start | bytes 1179652
  10.2 9.4 %copy-start.7 = (f32[9,512]{1,0:T(8,128)S(1)}, f32[9,512]{1,0:T(8,128)}, u32[]{:S(2)}) copy-start(f32[9,512]{1,0:T(8,128)} %s_ref.3) | copy-start | bytes 55300
  10.3 8.8 %collective-permute-start = (bf16[288,512]{1,0:T(8,128)(2,1)S(1)}, bf16[288,512]{1,0:T(8,128)(2,1)S(1)}, u32[]{:S(2)}, u32[]{:S(2)}) collective-permute-start(bf16[288,512]{1,0:T(8,128)(2,1)S(1)} %get-tuple-element.26), channel_id=1, source_target_pairs={{1,2},{2,1},{3,4},{4,3},{5,6},{6,5},{7,8},{8,7},{9,10},{10,9},{11,... | collective-permute-start | bytes 884744 | tf_op jit(solution)/shard_map/ppermute | solution.py:343
  14.4 4.7 %collective-permute-start.1 = (bf16[288,512]{1,0:T(8,128)(2,1)S(1)}, bf16[288,512]{1,0:T(8,128)(2,1)S(1)}, u32[]{:S(2)}, u32[]{:S(2)}) collective-permute-start(bf16[288,512]{1,0:T(8,128)(2,1)S(1)} %get-tuple-element.27), channel_id=1, source_target_pairs={{0,1},{1,0},{2,3},{3,2},{4,5},{5,4},{6,7},{7,6},{8,9},{9,8},{10,11... | collective-permute-start | bytes 884744 | tf_op jit(solution)/shard_map/ppermute | solution.py:346
  51.1 8.8 %collective-permute-start.2 = (f32[8,1,128]{2,1,0:T(1,128)S(1)}, f32[8,1,128]{2,1,0:T(1,128)S(1)}, u32[]{:S(2)}, u32[]{:S(2)}) collective-permute-start(f32[8,1,128]{2,1,0:T(1,128)S(1)} %get-tuple-element.29), channel_id=1, source_target_pairs={{0,0},{8,8},{2,64},{10,72},{4,128},{12,136},{6,192},{14,200},{1,25... | collective-permute-start | bytes 12296 | tf_op jit(solution)/shard_map/ppermute | solution.py:380
  60.9 18.0 %all-to-all-start.2 = ((f32[64,9,1,128]{3,2,1,0:T(1,128)}), f32[64,9,1,128]{3,2,1,0:T(1,128)S(1)}, u32[]{:S(2)}, u32[]{:S(2)}) async-start(f32[64,9,1,128]{3,2,1,0:T(1,128)} %get-tuple-element.43), calls=%async_computation.2 | async-start | bytes 589824 | tf_op jit(solution)/shard_map/all_to_all | solution.py:391
  67.0 5.0 %collective-permute-start.3 = (f32[1,1,512]{2,1,0:T(1,128)S(1)}, f32[1,1,512]{2,1,0:T(1,128)S(1)}, u32[]{:S(2)}, u32[]{:S(2)}) collective-permute-start(f32[1,1,512]{2,1,0:T(1,128)S(1)} %get-tuple-element.32), channel_id=1, source_target_pairs={{0,1},{1,2},{2,3},{3,4},{4,5},{5,6},{6,7},{7,8},{8,9},{9,10},{10,1... | collective-permute-start | bytes 6152 | tf_op jit(solution)/shard_map/ppermute | solution.py:339
  70.0 5.2 %collective-permute-start.4 = (f32[1,1,512]{2,1,0:T(1,128)S(1)}, f32[1,1,512]{2,1,0:T(1,128)S(1)}, u32[]{:S(2)}, u32[]{:S(2)}) collective-permute-start(f32[1,1,512]{2,1,0:T(1,128)S(1)} %get-tuple-element.33), channel_id=1, source_target_pairs={{1,0},{2,1},{3,2},{4,3},{5,4},{6,5},{7,6},{8,7},{9,8},{10,9},{11,1... | collective-permute-start | bytes 6152 | tf_op jit(solution)/shard_map/ppermute | solution.py:339

commit v9 on v8

--- a/solution.py
+++ b/solution.py
@@ -104,7 +104,7 @@
 
 
 def order_of(peers):
-    return [(i * 29 + 7) % peers for i in range(peers)]
+    return [(i * 35 + 7) % peers for i in range(peers)]
 
 
 ORDER = order_of(64)

time: 80.2 us -> 79.9 us (level)
  no operation moved by 1% of the time
where the time goes in v9:
time: 79.9 us; the launch traced here: 79.5 us
  starting transfers between devices  31.9 us (40%)
  blocking collectives  28.8 us (36%)
  waiting for transfers between devices  10.8 us (14%)
  Pallas kernels  5.46 us (7%)
  local copies, waits for them, and re-layouts  1.76 us (2%)
    all_to_all x1, blocking collectives, on_device(): lax.all_to_all(part, 'ctx', split_axis=0, concat_axis=0, tiled=True, axis...  28.8 us
    all_to_all x1, starting transfers between devices, on_device(): lax.all_to_all(filter_taps, 'dp', split_axis=1, concat_axis=0, tiled=True)  7.79 us
    ppermute x1, starting transfers between devices, on_device(): tile = lax.ppermute(tile, ('dp', 'ctx'), pairs)  7.31 us
    all_to_all x1, starting transfers between devices, on_device(): lax.all_to_all(sent, 'ctx', split_axis=0, concat_axis=0, tiled=True, axis...  6.39 us
    ppermute x2, starting transfers between devices, shifted(): return lax.ppermute(value, 'ctx', pairs)  4.39 us
    ppermute x1, starting transfers between devices, on_device(): lax.ppermute(far, 'ctx', [(i, i + 1 if i % 2 else i - 1) for i in range(1...  4.09 us
    ppermute x2, waiting for transfers between devices, shifted(): return lax.ppermute(value, 'ctx', pairs)  3.26 us
    all_to_all x1, waiting for transfers between devices, on_device(): lax.all_to_all(sent, 'ctx', split_axis=0, concat_axis=0, tiled=True, axis...  2.79 us
  transfers between devices with their start and end apart: 7, of which 5 were waited for; matrix products, arithmetic and copies ran while one was open for 0% of the time, Pallas kernels for 1%

profile of v9, /device:TPU:1, one launch (start us, length us, event | category | flops | bytes accessed | tf_op | source)
XLA Modules:
  0.0 79.5 jit_solution(12990885021537572406)
XLA Ops:
  0.6 0.0 copy-start.5
  0.6 0.0 copy-start.6
  0.7 1.7 %copy.18 = f32[2,8,8,512]{3,2,0,1:T(8,128)} copy(f32[2,8,8,512]{3,2,1,0:T(8,128)} %bitcast.9) | data formatting | bytes 524288 | tf_op jit(solution)/shard_map/all_to_all | solution.py:347
  2.4 0.0 copy-start
  2.4 0.0 copy-start.1
  2.4 0.0 copy-start.2
  2.4 0.0 copy-start.3
  2.4 7.8 %all-to-all-start = ((f32[16,8,512]{2,0,1:T(8,128)}), f32[16,8,512]{2,0,1:T(8,128)S(1)}, u32[]{:S(2)}, u32[]{:S(2)}) async-start(f32[16,8,512]{2,0,1:T(8,128)} %bitcast.7), calls=%async_computation | async-start | bytes 524288 | tf_op jit(solution)/shard_map/all_to_all | solution.py:347
  10.2 0.0 copy-start.4
  10.2 0.0 copy-done
  10.2 0.0 copy-done.1
  10.2 0.0 copy-done.2
  10.2 0.0 copy-done.3
  10.2 0.0 copy-start.7
  10.2 0.1 pack.1
  10.3 4.1 %collective-permute-start = (bf16[288,512]{1,0:T(8,128)(2,1)S(1)}, bf16[288,512]{1,0:T(8,128)(2,1)S(1)}, u32[]{:S(2)}, u32[]{:S(2)}) collective-permute-start(bf16[288,512]{1,0:T(8,128)(2,1)S(1)} %get-tuple-element.26), channel_id=1, source_target_pairs={{1,2},{2,1},{3,4},{4,3},{5,6},{6,5},{7,8},{8,7},{9,10},{10,9},{11,... | collective-permute-start | bytes 884744 | tf_op jit(solution)/shard_map/ppermute | solution.py:343
  14.4 1.9 %collective-permute-start.1 = (bf16[288,512]{1,0:T(8,128)(2,1)S(1)}, bf16[288,512]{1,0:T(8,128)(2,1)S(1)}, u32[]{:S(2)}, u32[]{:S(2)}) collective-permute-start(bf16[288,512]{1,0:T(8,128)(2,1)S(1)} %get-tuple-element.27), channel_id=1, source_target_pairs={{0,1},{1,0},{2,3},{3,2},{4,5},{5,4},{6,7},{7,6},{8,9},{9,8},{10,11... | collective-permute-start | bytes 884744 | tf_op jit(solution)/shard_map/ppermute | solution.py:346
  16.3 2.8 %collective-permute-done.far_ref = bf16[288,512]{1,0:T(8,128)(2,1)S(1)} collective-permute-done((bf16[288,512]{1,0:T(8,128)(2,1)S(1)}, bf16[288,512]{1,0:T(8,128)(2,1)S(1)}, u32[]{:S(2)}, u32[]{:S(2)}) %collective-permute-start) | collective-permute-done | bytes 294944 | tf_op jit(solution)/shard_map/ppermute | solution.py:343
  19.1 0.0 collective-permute-done.1.near_ref
  19.1 0.5 all-to-all-done
  19.6 0.0 copy-done.5
  19.6 0.0 copy-done.6
  19.6 0.0 copy-done.4
  19.6 0.0 copy-done.7
  19.6 2.4 %layer.1 = (bf16[128,512]{1,0:T(8,128)(2,1)S(1)}, f32[136,512]{1,0:T(8,128)S(1)}, f32[136,512]{1,0:T(8,128)S(1)}, f32[136,512]{1,0:T(8,128)S(1)}, f32[64,9,1,128...) custom-call(s32[1]{0:T(128)} %bitcast.place_ref, bf16[128,512]{1,0:T(8,128)(2,1)S(1)} %copy-done, ...), custom_call_target="tpu_custom_call" | custom-call | tf_op jit(solution)/shard_map/layer/pallas_call | solution.py:250
  22.1 28.8 %all_to_all.29.part_ref = f32[64,9,1,128]{3,2,1,0:T(1,128)S(1)} all-to-all(f32[64,9,1,128]{3,2,1,0:T(1,128)S(1)} %get-tuple-element.28), channel_id=1, replica_groups={{7,42,13,48,19,54,25,60,31,2,37,8,43,14,49,20,55,26,61,32,3,38,9,44,15,..., dimensions={0} | all-to-all | bytes 589824 | tf_op jit(solution)/shard_map/all_to_all | solution.py:359
  50.8 0.2 sum.1
  51.0 7.3 %collective-permute-start.2 = (f32[8,1,128]{2,1,0:T(1,128)S(1)}, f32[8,1,128]{2,1,0:T(1,128)S(1)}, u32[]{:S(2)}, u32[]{:S(2)}) collective-permute-start(f32[8,1,128]{2,1,0:T(1,128)S(1)} %get-tuple-element.29), channel_id=1, source_target_pairs={{0,0},{8,8},{2,64},{10,72},{4,128},{12,136},{6,192},{14,200},{1,25... | collective-permute-start | bytes 12296 | tf_op jit(solution)/shard_map/ppermute | solution.py:380
  58.3 1.5 %collective-permute-done.2.tile_ref = f32[8,1,128]{2,1,0:T(1,128)S(1)} collective-permute-done((f32[8,1,128]{2,1,0:T(1,128)S(1)}, f32[8,1,128]{2,1,0:T(1,128)S(1)}, u32[]{:S(2)}, u32[]{:S(2)}) %collective-permute-start.2) | collective-permute-done | bytes 4128 | tf_op jit(solution)/shard_map/ppermute | solution.py:380
  59.8 0.9 %spread.1 = (f32[64,9,1,128]{3,2,1,0:T(1,128)}, f32[1,1,512]{2,1,0:T(1,128)S(1)}, f32[1,1,512]{2,1,0:T(1,128)S(1)}) custom-call(f32[8,1,128]{2,1,0:T(1,128)S(1)} %collective-permute-done.2.tile_ref, f32[1,1,128]{2,1,0:T(1,128)S(1)} %get-tuple-element.30.short_ref, f32[2,1,512]{2,1,0:T(1,128)S(1)} %get-tuple-element.31.late_ref), custom_call_target="tpu_custom_call" | custom-call | tf_op jit(solution)/shard_map/spread/pallas_call | solution.py:382
  60.7 6.4 %all-to-all-start.2 = ((f32[64,9,1,128]{3,2,1,0:T(1,128)}), f32[64,9,1,128]{3,2,1,0:T(1,128)S(1)}, u32[]{:S(2)}, u32[]{:S(2)}) async-start(f32[64,9,1,128]{3,2,1,0:T(1,128)} %get-tuple-element.43), calls=%async_computation.2 | async-start | bytes 589824 | tf_op jit(solution)/shard_map/all_to_all | solution.py:391
  67.1 2.5 %collective-permute-start.3 = (f32[1,1,512]{2,1,0:T(1,128)S(1)}, f32[1,1,512]{2,1,0:T(1,128)S(1)}, u32[]{:S(2)}, u32[]{:S(2)}) collective-permute-start(f32[1,1,512]{2,1,0:T(1,128)S(1)} %get-tuple-element.32), channel_id=1, source_target_pairs={{0,1},{1,2},{2,3},{3,4},{4,5},{5,6},{6,7},{7,8},{8,9},{9,10},{10,1... | collective-permute-start | bytes 6152 | tf_op jit(solution)/shard_map/ppermute | solution.py:339
  69.6 1.9 %collective-permute-start.4 = (f32[1,1,512]{2,1,0:T(1,128)S(1)}, f32[1,1,512]{2,1,0:T(1,128)S(1)}, u32[]{:S(2)}, u32[]{:S(2)}) collective-permute-start(f32[1,1,512]{2,1,0:T(1,128)S(1)} %get-tuple-element.33), channel_id=1, source_target_pairs={{1,0},{2,1},{3,2},{4,3},{5,4},{6,5},{7,6},{8,7},{9,8},{10,9},{11,1... | collective-permute-start | bytes 6152 | tf_op jit(solution)/shard_map/ppermute | solution.py:339
  71.5 0.0 collective-permute-done.3.p_ref
  71.5 3.3 %collective-permute-done.4.lg_ref = f32[1,1,512]{2,1,0:T(1,128)S(1)} collective-permute-done((f32[1,1,512]{2,1,0:T(1,128)S(1)}, f32[1,1,512]{2,1,0:T(1,128)S(1)}, u32[]{:S(2)}, u32[]{:S(2)}) %collective-permute-start.4) | collective-permute-done | bytes 2080 | tf_op jit(solution)/shard_map/ppermute | solution.py:339
  74.8 1.0 %patch.1 = (bf16[128,512]{1,0:T(8,128)(2,1)}, bf16[128,512]{1,0:T(8,128)(2,1)}, bf16[128,512]{1,0:T(8,128)(2,1)}, bf16[128,512]{1,0:T(8,128)(2,1)}) custom-call(f32[1,1,512]{2,1,0:T(1,128)S(1)} %collective-permute-done.3.p_ref, f32[1,1,512]{2,1,0:T(1,128)S(1)} %collective-permute-done.4.lg_ref, f32[8,512]{1,0:T(8,128)S(1)} %get-tuple-element.34.fix_ref, ...), custom_call_target="tpu_custom_call" | custom-call | tf_op jit(solution)/shard_map/patch/pallas_call | solution.py:304
  75.8 2.8 %all-to-all-done.2.gathered_ref = f32[64,9,1,128]{3,2,1,0:T(1,128)S(1)} async-done(((f32[64,9,1,128]{3,2,1,0:T(1,128)}), f32[64,9,1,128]{3,2,1,0:T(1,128)S(1)}, u32[]{:S(2)}, u32[]{:S(2)}) %all-to-all-start.2) | async-done | bytes 294944 | tf_op jit(solution)/shard_map/all_to_all | solution.py:391
  78.5 0.9 %final.1 = (f32[16,4096]{1,0:T(8,128)}, f32[9,512]{1,0:T(8,128)}) custom-call(f32[64,9,1,128]{3,2,1,0:T(1,128)S(1)} %all-to-all-done.2.gathered_ref), custom_call_target="tpu_custom_call" | custom-call | tf_op jit(solution)/shard_map/final/pallas_call | solution.py:393
Async XLA Ops:
  0.6 19.0 %copy-start.5 = (bf16[136,768]{1,0:T(8,128)(2,1)S(1)}, bf16[136,768]{1,0:T(8,128)(2,1)}, u32[]{:S(2)}) copy-start(bf16[136,768]{1,0:T(8,128)(2,1)} %constant.12.clone.grad_ref) | copy-start | bytes 626692
  0.6 19.0 %copy-start.6 = (bf16[136,768]{1,0:T(8,128)(2,1)S(1)}, bf16[136,768]{1,0:T(8,128)(2,1)}, u32[]{:S(2)}) copy-start(bf16[136,768]{1,0:T(8,128)(2,1)} %constant.11.clone.long_ref) | copy-start | bytes 626692
  2.4 7.8 %copy-start = (bf16[128,512]{1,0:T(8,128)(2,1)S(1)}, bf16[128,512]{1,0:T(8,128)(2,1)}, u32[]{:S(2)}) copy-start(bf16[128,512]{1,0:T(8,128)(2,1)} %q_ref.3) | copy-start | bytes 393220
  2.4 7.8 %copy-start.1 = (bf16[128,512]{1,0:T(8,128)(2,1)S(1)}, bf16[128,512]{1,0:T(8,128)(2,1)}, u32[]{:S(2)}) copy-start(bf16[128,512]{1,0:T(8,128)(2,1)} %k_ref.3) | copy-start | bytes 393220
  2.4 7.8 %copy-start.2 = (bf16[128,512]{1,0:T(8,128)(2,1)S(1)}, bf16[128,512]{1,0:T(8,128)(2,1)}, u32[]{:S(2)}) copy-start(bf16[128,512]{1,0:T(8,128)(2,1)} %v_ref.3) | copy-start | bytes 393220
  2.4 7.8 %copy-start.3 = (bf16[128,512]{1,0:T(8,128)(2,1)S(1)}, bf16[128,512]{1,0:T(8,128)(2,1)}, u32[]{:S(2)}) copy-start(bf16[128,512]{1,0:T(8,128)(2,1)} %c_ref.3) | copy-start | bytes 393220
  2.4 17.2 %all-to-all-start = ((f32[16,8,512]{2,0,1:T(8,128)}), f32[16,8,512]{2,0,1:T(8,128)S(1)}, u32[]{:S(2)}, u32[]{:S(2)}) async-start(f32[16,8,512]{2,0,1:T(8,128)} %bitcast.7), calls=%async_computation | async-start | bytes 524288 | tf_op jit(solution)/shard_map/all_to_all | solution.py:347
  10.2 9.4 %copy-start.4 = (bf16[256,768]{1,0:T(8,128)(2,1)S(1)}, bf16[256,768]{1,0:T(8,128)(2,1)}, u32[]{:S(2)}) copy-start(bf16[256,768]{1,0:T(8,128)(2,1)} %constant.10.clone.fwd_ref) | copy-start | bytes 1179652
  10.2 9.4 %copy-start.7 = (f32[9,512]{1,0:T(8,128)S(1)}, f32[9,512]{1,0:T(8,128)}, u32[]{:S(2)}) copy-start(f32[9,512]{1,0:T(8,128)} %s_ref.3) | copy-start | bytes 55300
  10.3 8.8 %collective-permute-start = (bf16[288,512]{1,0:T(8,128)(2,1)S(1)}, bf16[288,512]{1,0:T(8,128)(2,1)S(1)}, u32[]{:S(2)}, u32[]{:S(2)}) collective-permute-start(bf16[288,512]{1,0:T(8,128)(2,1)S(1)} %get-tuple-element.26), channel_id=1, source_target_pairs={{1,2},{2,1},{3,4},{4,3},{5,6},{6,5},{7,8},{8,7},{9,10},{10,9},{11,... | collective-permute-start | bytes 884744 | tf_op jit(solution)/shard_map/ppermute | solution.py:343
  14.4 4.7 %collective-permute-start.1 = (bf16[288,512]{1,0:T(8,128)(2,1)S(1)}, bf16[288,512]{1,0:T(8,128)(2,1)S(1)}, u32[]{:S(2)}, u32[]{:S(2)}) collective-permute-start(bf16[288,512]{1,0:T(8,128)(2,1)S(1)} %get-tuple-element.27), channel_id=1, source_target_pairs={{0,1},{1,0},{2,3},{3,2},{4,5},{5,4},{6,7},{7,6},{8,9},{9,8},{10,11... | collective-permute-start | bytes 884744 | tf_op jit(solution)/shard_map/ppermute | solution.py:346
  51.0 8.8 %collective-permute-start.2 = (f32[8,1,128]{2,1,0:T(1,128)S(1)}, f32[8,1,128]{2,1,0:T(1,128)S(1)}, u32[]{:S(2)}, u32[]{:S(2)}) collective-permute-start(f32[8,1,128]{2,1,0:T(1,128)S(1)} %get-tuple-element.29), channel_id=1, source_target_pairs={{0,0},{8,8},{2,64},{10,72},{4,128},{12,136},{6,192},{14,200},{1,25... | collective-permute-start | bytes 12296 | tf_op jit(solution)/shard_map/ppermute | solution.py:380
  60.7 17.8 %all-to-all-start.2 = ((f32[64,9,1,128]{3,2,1,0:T(1,128)}), f32[64,9,1,128]{3,2,1,0:T(1,128)S(1)}, u32[]{:S(2)}, u32[]{:S(2)}) async-start(f32[64,9,1,128]{3,2,1,0:T(1,128)} %get-tuple-element.43), calls=%async_computation.2 | async-start | bytes 589824 | tf_op jit(solution)/shard_map/all_to_all | solution.py:391
  67.1 4.4 %collective-permute-start.3 = (f32[1,1,512]{2,1,0:T(1,128)S(1)}, f32[1,1,512]{2,1,0:T(1,128)S(1)}, u32[]{:S(2)}, u32[]{:S(2)}) collective-permute-start(f32[1,1,512]{2,1,0:T(1,128)S(1)} %get-tuple-element.32), channel_id=1, source_target_pairs={{0,1},{1,2},{2,3},{3,4},{4,5},{5,6},{6,7},{7,8},{8,9},{9,10},{10,1... | collective-permute-start | bytes 6152 | tf_op jit(solution)/shard_map/ppermute | solution.py:339
  69.6 5.2 %collective-permute-start.4 = (f32[1,1,512]{2,1,0:T(1,128)S(1)}, f32[1,1,512]{2,1,0:T(1,128)S(1)}, u32[]{:S(2)}, u32[]{:S(2)}) collective-permute-start(f32[1,1,512]{2,1,0:T(1,128)S(1)} %get-tuple-element.33), channel_id=1, source_target_pairs={{1,0},{2,1},{3,2},{4,3},{5,4},{6,5},{7,6},{8,7},{9,8},{10,9},{11,1... | collective-permute-start | bytes 6152 | tf_op jit(solution)/shard_map/ppermute | solution.py:339
